TPU v7x, 128 devices: a whole 4x4x4 slice. The times are simulated.
128 devices in a mesh: gx: 8 (over z_hi, x), gy: 16 (over y, z_lo, core).
Axes of the slice: x: 4, y: 4, z: 4 (z_hi: 2, z_lo: 2; z = z_hi * 2 + z_lo), core: 2. Of those that a mesh axis runs over, the one named last changes fastest.
Arguments:
- orbitals: bfloat16 [8, 16, 2, 64, 4096], P('gx', 'gy'), may hold values from -6 to 6
- anchors: int32 [256, 3], replicated, may hold values from 0 to 727, as said below
- pair_list: int32 [8, 16, 12, 2], P('gx', 'gy'), may hold values from 0 to 255, as said below
- pair_count: int32 [8, 16], P('gx', 'gy'), may hold values from 1 to 12, as said below
- core_density: float32 [384, 768, 128], P('gx', 'gy'), may hold values from 0.05 to 2
Outputs:
- action: float32 [8, 16, 2, 64, 4096], P('gx', 'gy')
- potential: float32 [384, 768, 128], P('gx', 'gy')
Inputs may be any that keep to these rules, and one draw needn't show every extreme that they name: Orbital n = (a 16 + b) * 2 + k is held by device (a, b) of (gx, gy); anchors[n] has its first coordinate in a 48 to a 55, its second in b * 48 to b * 48 + 7, its third in 0 to 64. `pair_list`: every slot of device (a, b) names two different orbitals: the first held by (a, b), the second by (a + s, b + t) with s and t in -1, 0, 1, taken modulo 8 and 16. `pair_count`: some device has 12 live slots.
All inputs are finite; a program needn't handle non-finite values.
Results may differ from a plain program's by a relative error of at most 0.0012.
Values may be sent and summed in bfloat16 or wider, within the bound.
A program may use at most 128 MiB of HBM per device.

v0:
```python
import math

import jax
import jax.numpy as jnp
from jax import lax
from jax.sharding import PartitionSpec as P

SWEEPS = 4


screen_mass = 0.25
coupling = 2.0 * math.pi
exx_share = 0.25
xc_factor = (3.0 / math.pi) ** (1.0 / 3.0)


def from_behind(block, axis, distance):
    devices = range(lax.axis_size(axis))
    route = [((i - distance) % len(devices), i) for i in devices]
    return lax.ppermute(block, axis, route)


def sweep_weights(sweep_count):
    return [
        1.0 / (1.0 + 0.7 * math.cos(math.pi * (2 * order + 1) / (2 * sweep_count)))
        for order in range(sweep_count)
    ]


def column_parts(box_side):
    column_index = lax.broadcasted_iota(jnp.int32, (1, box_side * box_side), 1)
    return (column_index // box_side, column_index % box_side)


def neighbour_sum(values):
    box_side = values.shape[0]
    depth_index = column_parts(box_side)[1]
    zero_row = jnp.zeros((1, values.shape[1]), values.dtype)
    summed = jnp.concatenate([values[1:], zero_row], 0) + jnp.concatenate(
        [zero_row, values[:-1]], 0
    )
    zero_band = jnp.zeros((box_side, box_side), values.dtype)
    summed = (
        summed
        + jnp.concatenate([values[:, box_side:], zero_band], 1)
        + jnp.concatenate([zero_band, values[:, :-box_side]], 1)
    )
    zero_cell = jnp.zeros((box_side, 1), values.dtype)
    upward = jnp.concatenate([values[:, 1:], zero_cell], 1)
    downward = jnp.concatenate([zero_cell, values[:, :-1]], 1)
    summed = (
        summed
        + jnp.where(depth_index < box_side - 1, upward, 0.0)
        + jnp.where(depth_index > 0, downward, 0.0)
    )
    return summed


def screened_solve(source):
    diagonal = 6.0 + screen_mass
    solved = jnp.zeros_like(source)
    for weight in sweep_weights(SWEEPS):
        residual = source - (diagonal * solved - neighbour_sum(solved))
        solved = solved + weight / diagonal * residual
    return solved


def move_box(values, shift_x, shift_y, shift_z):
    box_side = values.shape[0]
    row_index = lax.broadcasted_iota(jnp.int32, (box_side, 1), 0)
    across, depth_index = column_parts(box_side)
    rolled = jnp.roll(values, shift_x, axis=0)
    rolled = jnp.roll(rolled, shift_y * box_side + shift_z, axis=1)
    inside = (row_index >= shift_x) & (row_index < box_side + shift_x)
    inside = inside & (across >= shift_y) & (across < box_side + shift_y)
    inside = inside & (depth_index >= shift_z) & (depth_index < box_side + shift_z)
    return jnp.where(inside, rolled, 0.0)


def relative(first_anchor, second_anchor, span_x, span_y):
    delta = second_anchor - first_anchor
    delta_x = (delta[0] + span_x // 2) % span_x - span_x // 2
    delta_y = (delta[1] + span_y // 2) % span_y - span_y // 2
    return (delta_x, delta_y, delta[2])


def locate(orbit, orbit_count, mesh_x, mesh_y, here_x, here_y):
    holder = orbit // orbit_count
    place_x = (holder // mesh_y - here_x + 1) % mesh_x
    place_y = (holder % mesh_y - here_y + 1) % mesh_y
    return (place_x, place_y, orbit % orbit_count)


def add_cube(canvas, orbital_box, start_x, start_y, start_z):
    box_side = orbital_box.shape[0]
    squared = jnp.square(orbital_box.astype(jnp.float32)).reshape(box_side, box_side, box_side)
    region = lax.dynamic_slice(canvas, (start_x, start_y, start_z), (box_side, box_side, box_side))
    return lax.dynamic_update_slice(canvas, region + squared, (start_x, start_y, start_z))


def back_along_y(terms, step_by):
    return from_behind(terms.astype(jnp.bfloat16), "gy", step_by).astype(terms.dtype)


def back_along_x(terms, step_by):
    return from_behind(terms.astype(jnp.bfloat16), "gx", step_by).astype(terms.dtype)


def grid_along_x(values, step_by):
    return from_behind(values, "gx", step_by)


def grid_along_y(values, step_by):
    return from_behind(values, "gy", step_by)


def rims_along_x(values, step_by):
    return from_behind(values, "gx", step_by)


def rims_along_y(values, step_by):
    return from_behind(values, "gy", step_by)


def local(orbitals, anchors, pair_list, pair_count, core_density):
    here_x = lax.axis_index("gx")
    here_y = lax.axis_index("gy")
    mesh_x = lax.axis_size("gx")
    mesh_y = lax.axis_size("gy")
    orbit_count = orbitals.shape[2]
    box_side = orbitals.shape[3]
    flat_side = box_side * box_side
    slab_x = core_density.shape[0]
    slab_y = core_density.shape[1]
    grid_depth = core_density.shape[2]
    rim_cells = box_side - slab_x + box_side // 8
    span_x = slab_x * mesh_x
    span_y = slab_y * mesh_y
    upper_cut = (box_side - rim_cells) * box_side
    lower_cut = rim_cells * box_side
    own_boxes = orbitals[0, 0]
    own_holder = here_x * mesh_y + here_y
    empty_boxes = jnp.zeros_like(own_boxes)
    from_left = rims_along_x(own_boxes[:, box_side - rim_cells :], 1)
    from_right = rims_along_x(own_boxes[:, :rim_cells], -1)
    column = jnp.stack(
        [
            empty_boxes.at[:, box_side - rim_cells :].set(from_left),
            own_boxes,
            empty_boxes.at[:, :rim_cells].set(from_right),
        ],
        0,
    )
    empty_column = jnp.zeros_like(column)
    from_below = rims_along_y(column[..., upper_cut:], 1)
    from_above = rims_along_y(column[..., :lower_cut], -1)
    window = jnp.stack(
        [
            empty_column.at[..., upper_cut:].set(from_below),
            column,
            empty_column.at[..., :lower_cut].set(from_above),
        ],
        1,
    )

    def pick_box(orbit):
        place_x, place_y, place_k = locate(orbit, orbit_count, mesh_x, mesh_y, here_x, here_y)
        picked = lax.dynamic_slice(
            window, (place_x, place_y, place_k, 0, 0), (1, 1, 1, box_side, flat_side)
        )
        return (
            picked.reshape(box_side, flat_side).astype(jnp.float32),
            (place_x, place_y, place_k),
        )

    def pair_terms(pair_ids):
        first_box, first_at = pick_box(pair_ids[0])
        second_box, second_at = pick_box(pair_ids[1])
        delta_x, delta_y, delta_z = relative(
            anchors[pair_ids[0]], anchors[pair_ids[1]], span_x, span_y
        )
        moved = move_box(second_box, delta_x, delta_y, delta_z)
        solved = screened_solve(coupling * first_box * moved)
        return (
            solved * moved,
            first_at,
            move_box(solved * first_box, -delta_x, -delta_y, -delta_z),
            second_at,
        )

    def add_term(exchange, where_at, term_box):
        start_at = (where_at[0], where_at[1], where_at[2], 0, 0)
        region = lax.dynamic_slice(exchange, start_at, (1, 1, 1, box_side, flat_side))
        return lax.dynamic_update_slice(
            exchange, region + term_box.reshape(1, 1, 1, box_side, flat_side), start_at
        )

    def pair_step(slot_number, exchange):
        first_term, first_at, second_term, second_at = pair_terms(pair_list[0, 0, slot_number])
        exchange = add_term(exchange, first_at, first_term)
        return add_term(exchange, second_at, second_term)

    exchange = lax.fori_loop(0, pair_count[0, 0], pair_step, jnp.zeros(window.shape, jnp.float32))
    column_terms = exchange[:, 1]
    column_terms = column_terms.at[..., upper_cut:].add(
        back_along_y(exchange[:, 0, ..., upper_cut:], -1)
    )
    column_terms = column_terms.at[..., :lower_cut].add(
        back_along_y(exchange[:, 2, ..., :lower_cut], 1)
    )
    own_terms = column_terms[1]
    own_terms = own_terms.at[:, box_side - rim_cells :].add(
        back_along_x(column_terms[0][:, box_side - rim_cells :], -1)
    )
    own_terms = own_terms.at[:, :rim_cells].add(back_along_x(column_terms[2][:, :rim_cells], 1))
    own_first = own_holder * orbit_count
    canvas = jnp.zeros((slab_x + rim_cells, slab_y + rim_cells, grid_depth), jnp.float32)
    for orbit_slot in range(orbit_count):
        anchor = anchors[own_first + orbit_slot]
        canvas = add_cube(
            canvas,
            own_boxes[orbit_slot],
            anchor[0] - here_x * slab_x,
            anchor[1] - here_y * slab_y,
            anchor[2],
        )
    slab_rows = canvas[:slab_x].at[:rim_cells].add(grid_along_x(canvas[slab_x:], 1))
    density = slab_rows[:, :slab_y].at[:, :rim_cells].add(grid_along_y(slab_rows[:, slab_y:], 1))
    potential = -xc_factor * jnp.cbrt(density + core_density)
    widened = jnp.concatenate([potential, grid_along_x(potential[:rim_cells], -1)], 0)
    widened = jnp.concatenate([widened, grid_along_y(widened[:, :rim_cells], -1)], 1)
    actions = []
    for orbit_slot in range(orbit_count):
        anchor = anchors[own_first + orbit_slot]
        sampled = lax.dynamic_slice(
            widened,
            (anchor[0] - here_x * slab_x, anchor[1] - here_y * slab_y, anchor[2]),
            (box_side, box_side, box_side),
        )
        actions.append(
            sampled.reshape(box_side, flat_side) * own_boxes[orbit_slot].astype(jnp.float32)
            - exx_share * own_terms[orbit_slot]
        )
    return (jnp.stack(actions, 0).reshape(1, 1, orbit_count, box_side, flat_side), potential)


def solution(mesh):
    placed = (
        P("gx", "gy", None, None, None),
        P(),
        P("gx", "gy", None, None),
        P("gx", "gy"),
        P("gx", "gy", None),
    )
    return jax.shard_map(
        local,
        mesh=mesh,
        in_specs=placed,
        out_specs=(P("gx", "gy", None, None, None), P("gx", "gy", None)),
        check_vma=False,
    )
```

profile of v0, /device:TPU:101, one launch (start us, length us, event | category | flops | bytes accessed | tf_op | source)
XLA Modules:
  0.0 564.0 jit_solution(10592414004066546097)
XLA Ops:
  16.9 31.2 %dynamic_update_slice.26 = f32[72,72,128]{2,1,0:T(8,128)S(1)} dynamic-update-slice(f32[72,72,128]{2,1,0:T(8,128)S(1)} %broadcast_in_dim.86, f32[64,64,64]{2,1,0:T(8,128)} %square.15, s32[]{:T(128)S(6)} %select_n.537, s32[]{:T(128)S(6)} %select_n.538, s32[]{:T(128)S(6)} %select_n.539) | dynamic-update-slice | bytes 2097156 | tf_op jit(solution)/shard_map/dynamic_update_slice | solution.py:98
  48.1 3.6 dynamic-slice_add_fusion
  51.7 31.2 %dynamic_update_slice.27 = f32[72,72,128]{2,1,0:T(8,128)S(1)} dynamic-update-slice(f32[72,72,128]{2,1,0:T(8,128)S(1)} %dynamic_update_slice.26, f32[64,64,64]{2,1,0:T(8,128)} %dynamic-slice_add_fusion, s32[]{:T(128)S(6)} %select_n.541, s32[]{:T(128)S(6)} %select_n.542, s32[]{:T(128)S(6)} %select_n.543) | dynamic-update-slice | bytes 2097156 | tf_op jit(solution)/shard_map/dynamic_update_slice | solution.py:98
  91.4 11.7 %collective-permute-done = f32[24,72,128]{2,1,0:T(8,128)S(1)} collective-permute-done((f32[24,72,128]{2,1,0:T(8,128)S(1)}, f32[24,72,128]{2,1,0:T(8,128)S(1)}, u32[]{:S(2)}, u32[]{:S(2)}) %collective-permute-start) | collective-permute-done | bytes 884768 | tf_op jit(solution)/shard_map/ppermute | solution.py:20
  105.2 3.1 collective-permute-start.1
  109.7 5.5 collective-permute-done.1
  125.2 4.2 fusion.31
  129.4 8.9 %broadcast_in_dim.87 = f32[3,3,2,64,4096]{4,3,2,1,0:T(8,128)} broadcast(f32[]{:T(128)} %constant.711.clone.1), dimensions={} | broadcast | bytes 18874372 | tf_op jit(solution)/shard_map/broadcast_in_dim | solution.py:203
  138.2 382.8 %while.25 = (s32[]{:T(128)}, f32[3,3,2,64,4096]{4,3,2,1,0:T(8,128)}, s32[]{:T(128)}, s32[1,1,12,2]{2,3,1,0:T(2,128)S(1)}, s32[]{:T(128)}, /*index=5*/s32[]{:T(12...) while((s32[]{:T(128)}, ...), condition=%wide.region_1.4_spmd, body=%wide.region_0.3_spmd.sunk | while | flops 21463632 | bytes 84135904 | solution.py:203
  167.4 2.9 fusion.114
  199.3 2.9 fusion.114
  231.1 2.9 fusion.114
  294.7 2.8 fusion.114
  326.6 2.9 fusion.114
  358.4 2.8 fusion.114
  390.2 2.9 fusion.114
  422.0 2.9 fusion.114
  453.9 2.9 fusion.114
  485.7 2.9 fusion.114
  517.5 2.8 fusion.114
  526.4 3.2 slice_bitcast_fusion
  531.0 9.3 %collective-permute-done.8 = bf16[3,2,64,1536]{3,2,1,0:T(8,128)(2,1)S(1)} collective-permute-done((bf16[3,2,64,1536]{3,2,1,0:T(8,128)(2,1)S(1)}, bf16[3,2,64,1536]{3,2,1,0:T(8,128)(2,1)S(1)}, u32[]{:S(2)}, u32[]{:S(2)}) %collective-permute-start.8) | collective-permute-done | bytes 1179680 | tf_op jit(solution)/shard_map/ppermute | solution.py:20
  551.0 3.4 fusion.62
  556.6 2.9 reshape.582
  (514 shorter events, 263.8 us)
Async XLA Ops:
  0.6 5.0 copy-start.6
  2.7 82.6 %collective-permute-start.4 = (bf16[2,24,4096]{2,1,0:T(8,128)(2,1)}, bf16[2,24,4096]{2,1,0:T(8,128)(2,1)S(1)}, u32[]{:S(2)}, u32[]{:S(2)}) collective-permute-start(bf16[2,24,4096]{2,1,0:T(8,128)(2,1)} %get-tuple-element.424), channel_id=1, source_target_pairs={{112,0},{0,16},{16,32},{32,48},{48,64},{64,80},{80,96},{96,112},{1... | collective-permute-start | bytes 1179656 | tf_op jit(solution)/shard_map/ppermute | solution.py:20
  3.6 81.7 %collective-permute-start.5 = (bf16[2,24,4096]{2,1,0:T(8,128)(2,1)}, bf16[2,24,4096]{2,1,0:T(8,128)(2,1)S(1)}, u32[]{:S(2)}, u32[]{:S(2)}) collective-permute-start(bf16[2,24,4096]{2,1,0:T(8,128)(2,1)} %get-tuple-element.425), channel_id=1, source_target_pairs={{16,0},{32,16},{48,32},{64,48},{80,64},{96,80},{112,96},{0,112},{1... | collective-permute-start | bytes 1179656 | tf_op jit(solution)/shard_map/ppermute | solution.py:20
  82.9 2.4 copy-start.1
  83.0 20.1 %collective-permute-start = (f32[24,72,128]{2,1,0:T(8,128)S(1)}, f32[24,72,128]{2,1,0:T(8,128)S(1)}, u32[]{:S(2)}, u32[]{:S(2)}) collective-permute-start(f32[24,72,128]{2,1,0:T(8,128)S(1)} %slice.649), channel_id=1, source_target_pairs={{112,0},{0,16},{16,32},{32,48},{48,64},{64,80},{80,96},{96,112},{1... | collective-permute-start | bytes 2654216 | tf_op jit(solution)/shard_map/ppermute | solution.py:20
  88.9 33.3 %collective-permute-start.6 = (bf16[3,2,64,1536]{3,2,1,0:T(8,128)(2,1)}, bf16[3,2,64,1536]{3,2,1,0:T(8,128)(2,1)}, u32[]{:S(2)}, u32[]{:S(2)}) collective-permute-start(bf16[3,2,64,1536]{3,2,1,0:T(8,128)(2,1)} %get-tuple-element.418), channel_id=1, source_target_pairs={{15,0},{0,1},{1,2},{2,3},{3,4},{4,5},{5,6},{6,7},{7,8},{8,9},{9,10... | collective-permute-start | bytes 3538952 | tf_op jit(solution)/shard_map/ppermute | solution.py:20
  105.2 10.0 %collective-permute-start.1 = (f32[48,24,128]{2,1,0:T(8,128)S(1)}, f32[48,24,128]{2,1,0:T(8,128)S(1)}, u32[]{:S(2)}, u32[]{:S(2)}) collective-permute-start(f32[48,24,128]{2,1,0:T(8,128)S(1)} %slice.652), channel_id=1, source_target_pairs={{15,0},{0,1},{1,2},{2,3},{3,4},{4,5},{5,6},{6,7},{7,8},{8,9},{9,10... | collective-permute-start | bytes 1769480 | tf_op jit(solution)/shard_map/ppermute | solution.py:20
  108.3 16.8 %collective-permute-start.7 = (bf16[3,2,64,1536]{3,2,1,0:T(8,128)(2,1)}, bf16[3,2,64,1536]{3,2,1,0:T(8,128)(2,1)S(1)}, u32[]{:S(2)}, u32[]{:S(2)}) collective-permute-start(bf16[3,2,64,1536]{3,2,1,0:T(8,128)(2,1)} %get-tuple-element.419), channel_id=1, source_target_pairs={{1,0},{2,1},{3,2},{4,3},{5,4},{6,5},{7,6},{8,7},{9,8},{10,9},{11,1... | collective-permute-start | bytes 3538952 | tf_op jit(solution)/shard_map/ppermute | solution.py:20
  118.6 431.2 %copy-start.3 = (f32[48,48,128]{2,1,0:T(8,128)}, f32[48,48,128]{2,1,0:T(8,128)S(1)}, u32[]{:S(2)}) copy-start(f32[48,48,128]{2,1,0:T(8,128)S(1)} %cbrt_multiply_fusion) | copy-start | bytes 3538948
  118.6 6.6 %copy-start.4 = (bf16[3,1,2,64,4096]{4,3,2,1,0:T(8,128)(2,1)S(1)}, bf16[3,1,2,64,4096]{4,3,2,1,0:T(8,128)(2,1)}, u32[]{:S(2)}) copy-start(bf16[3,1,2,64,4096]{4,3,2,1,0:T(8,128)(2,1)} %get-tuple-element.422) | copy-start | bytes 9437188
  119.4 410.2 %collective-permute-start.2 = (f32[24,48,128]{2,1,0:T(8,128)}, f32[24,48,128]{2,1,0:T(8,128)}, u32[]{:S(2)}, u32[]{:S(2)}) collective-permute-start(f32[24,48,128]{2,1,0:T(8,128)} %slice.653), channel_id=1, source_target_pairs={{16,0},{32,16},{48,32},{64,48},{80,64},{96,80},{112,96},{0,112},{1... | collective-permute-start | bytes 1769480 | tf_op jit(solution)/shard_map/ppermute | solution.py:20
  129.4 8.9 %copy-start.7 = (s32[1,1,12,2]{2,3,1,0:T(2,128)S(1)}, s32[1,1,12,2]{2,3,1,0:T(2,128)}, u32[]{:S(2)}) copy-start(s32[1,1,12,2]{2,3,1,0:T(2,128)} %param.33) | copy-start | bytes 292
  523.7 16.6 %collective-permute-start.8 = (bf16[3,2,64,1536]{3,2,1,0:T(8,128)(2,1)S(1)}, bf16[3,2,64,1536]{3,2,1,0:T(8,128)(2,1)S(1)}, u32[]{:S(2)}, u32[]{:S(2)}) collective-permute-start(bf16[3,2,64,1536]{3,2,1,0:T(8,128)(2,1)S(1)} %get-tuple-element.413), channel_id=1, source_target_pairs={{1,0},{2,1},{3,2},{4,3},{5,4},{6,5},{7,6},{8,7},{9,8},{10,9},{11,1... | collective-permute-start | bytes 3538952 | tf_op jit(solution)/shard_map/ppermute | solution.py:20
  523.8 18.5 %collective-permute-start.9 = (bf16[3,2,64,1536]{3,2,1,0:T(8,128)(2,1)S(1)}, bf16[3,2,64,1536]{3,2,1,0:T(8,128)(2,1)S(1)}, u32[]{:S(2)}, u32[]{:S(2)}) collective-permute-start(bf16[3,2,64,1536]{3,2,1,0:T(8,128)(2,1)S(1)} %get-tuple-element.412), channel_id=1, source_target_pairs={{15,0},{0,1},{1,2},{2,3},{3,4},{4,5},{5,6},{6,7},{7,8},{8,9},{9,10... | collective-permute-start | bytes 3538952 | tf_op jit(solution)/shard_map/ppermute | solution.py:20
  530.7 19.1 %collective-permute-start.3 = (f32[72,24,128]{2,1,0:T(8,128)S(1)}, f32[72,24,128]{2,1,0:T(8,128)S(1)}, u32[]{:S(2)}, u32[]{:S(2)}) collective-permute-start(f32[72,24,128]{2,1,0:T(8,128)S(1)} %pad_maximum_fusion.1), channel_id=1, source_target_pairs={{1,0},{2,1},{3,2},{4,3},{5,4},{6,5},{7,6},{8,7},{9,8},{10,9},{11,1... | collective-permute-start | bytes 2654216 | tf_op jit(solution)/shard_map/ppermute | solution.py:20
  543.0 4.2 copy-start
  544.9 14.6 %collective-permute-start.10 = (bf16[2,24,4096]{2,1,0:T(8,128)(2,1)}, bf16[2,24,4096]{2,1,0:T(8,128)(2,1)}, u32[]{:S(2)}, u32[]{:S(2)}) collective-permute-start(bf16[2,24,4096]{2,1,0:T(8,128)(2,1)} %slice.666), channel_id=1, source_target_pairs={{16,0},{32,16},{48,32},{64,48},{80,64},{96,80},{112,96},{0,112},{1... | collective-permute-start | bytes 1179656 | tf_op jit(solution)/shard_map/ppermute | solution.py:20
  545.9 15.0 %collective-permute-start.11 = (bf16[2,24,4096]{2,1,0:T(8,128)(2,1)}, bf16[2,24,4096]{2,1,0:T(8,128)(2,1)}, u32[]{:S(2)}, u32[]{:S(2)}) collective-permute-start(bf16[2,24,4096]{2,1,0:T(8,128)(2,1)} %slice.669), channel_id=1, source_target_pairs={{112,0},{0,16},{16,32},{32,48},{48,64},{64,80},{80,96},{96,112},{1... | collective-permute-start | bytes 1179656 | tf_op jit(solution)/shard_map/ppermute | solution.py:20
  559.4 2.7 copy-start.2
  559.4 2.7 copy-start.5
where the time goes:
time: 571 us; the launch traced here: 564 us
  other arithmetic  218 us (38%)
  local copies, waits for them, and re-layouts  150 us (26%)
  loops' own time  144 us (25%)
  waiting for transfers between devices  30.5 us (5%)
  starting transfers between devices  15 us (3%)
  between operations  7 us (1%)
    another operation x1, loops' own time, local(): lax.fori_loop(0, pair_count[0, 0], pair_step, jnp.zeros(window.shape, jnp...  144 us
    dynamic_update_slice x24, other arithmetic, add_term(): lax.dynamic_update_slice(exchange, region + term_box.reshape(1, 1, 1, box...  63.1 us
    dynamic_update_slice x2, local copies, waits for them, and re-layouts, add_cube(): lax.dynamic_update_slice(canvas, region + squared, (start_x, start_y, sta...  62.4 us
    add x24, other arithmetic, screened_solve(): solved = solved + weight / diagonal * residual  51.6 us
    ppermute x12, waiting for transfers between devices, from_behind(): return lax.ppermute(block, axis, route)  30.5 us
    mul x12, other arithmetic, pair_terms(): solved * first_box  26.6 us
    mul x12, other arithmetic, screened_solve(): solved = solved + weight / diagonal * residual  22.5 us
    ppermute x12, starting transfers between devices, from_behind(): return lax.ppermute(block, axis, route)  15 us
  transfers between devices with their start and end apart: 12, of which 5 were waited for; matrix products, arithmetic and copies ran while one was open for 64% of the time, Pallas kernels for 0%

commit v1 on v0

v1 whole, which is shorter than its diff:
```python
import functools
import math

import jax
import jax.numpy as jnp
from jax import lax
from jax.experimental import pallas as pl
from jax.experimental.pallas import tpu as pltpu
from jax.sharding import PartitionSpec as P

SWEEPS = 4
SIDE = 64
HALF = SIDE // 2
FLAT = SIDE * SIDE
RIM = 24
LOW = SIDE - RIM
RIM_LEADS = RIM // 2
LOW_LEADS = LOW // 2
LANES = 128
PAD = 1024

screen_mass = 0.25
coupling = 2.0 * math.pi
exx_share = 0.25
xc_factor = (3.0 / math.pi) ** (1.0 / 3.0)

BASE_X = 2 * HALF * SIDE
BASE_Y = BASE_X + 4 * HALF * RIM
BASE_C = BASE_Y + 4 * RIM_LEADS * SIDE
WINDOW_ROWS = BASE_C + 8 * RIM_LEADS * RIM
STEPS = [(0, 0), (-1, 0), (1, 0), (0, -1), (0, 1), (-1, -1), (-1, 1), (1, -1), (1, 1)]


def place_of(step_x, step_y):
    rows = SIDE if step_x == 0 else RIM
    leads = HALF if step_y == 0 else RIM_LEADS
    if step_x == 0 and step_y == 0:
        base = 0
    elif step_y == 0:
        base = BASE_X + (2 * HALF * RIM if step_x > 0 else 0)
    elif step_x == 0:
        base = BASE_Y + (2 * RIM_LEADS * SIDE if step_y > 0 else 0)
    else:
        base = BASE_C + ((2 if step_x > 0 else 0) + (1 if step_y > 0 else 0)) * 2 * RIM_LEADS * RIM
    return base, rows, leads


def sweep_weights(sweep_count):
    return [
        1.0 / (1.0 + 0.7 * math.cos(math.pi * (2 * order + 1) / (2 * sweep_count)))
        for order in range(sweep_count)
    ]


def lane_index(rows):
    return lax.broadcasted_iota(jnp.int32, (rows, LANES), 1)


def for_leads(count, step):
    lax.fori_loop(0, count, lambda index, _: (step(index), 0)[1], 0)


def pair_kernel(mesh_x, mesh_y, anchors, pairs, count, *refs):
    pieces = refs[:9]
    outs = refs[9:18]
    window, first_sum, second_sum, moved3, source3, even3, moved8, source8, even8, odd3, odd8 = refs[18:]
    here_x = lax.axis_index("gx")
    here_y = lax.axis_index("gy")
    span_x = mesh_x * (SIDE - 16)
    span_y = mesh_y * (SIDE - 16)

    for (step_x, step_y), piece in zip(STEPS, pieces):
        base, rows, leads = place_of(step_x, step_y)

        def widen(lead, base=base, rows=rows, leads=leads, piece=piece):
            lanes = pl.ds(pl.multiple_of(lead * LANES, LANES), LANES)
            for k in range(2):
                start = pl.multiple_of(PAD + base + k * leads * rows + lead * rows, 8)
                window[pl.ds(start, rows), :] = piece[k, :, lanes].astype(jnp.float32)

        for_leads(leads, widen)

    zeros64 = jnp.zeros((SIDE, LANES), jnp.float32)

    def clear_first(lead):
        first_sum[pl.ds(pl.multiple_of(lead * SIDE, SIDE), SIDE), :] = zeros64

    for_leads(2 * HALF, clear_first)

    def clear_second(lead):
        second_sum[pl.ds(pl.multiple_of(lead * SIDE, SIDE), SIDE), :] = zeros64

    for_leads((WINDOW_ROWS + 2 * PAD) // SIDE, clear_second)

    for field in (source3, even3, odd3, source8, even8, odd8):
        rows = field.shape[1]

        def clear_field(lead, field=field, rows=rows):
            field[lead] = jnp.zeros((rows, LANES), jnp.float32)

        for_leads(HALF + 2, clear_field)

    weights = sweep_weights(SWEEPS)
    diagonal = 6.0 + screen_mass
    scale = [weight / diagonal for weight in weights]
    keep = [(1.0 - weight) / part for weight, part in zip(weights, scale)]
    total_scale = coupling * scale[0] * scale[1] * scale[2] * scale[3]

    def pair_step(slot, carry):
        first = pairs[2 * slot]
        second = pairs[2 * slot + 1]
        first_k = lax.rem(first, 2)
        second_k = lax.rem(second, 2)
        holder = lax.div(second, 2)
        step_x = lax.rem(lax.div(holder, mesh_y) - here_x + 1 + mesh_x, mesh_x) - 1
        step_y = lax.rem(lax.rem(holder, mesh_y) - here_y + 1 + mesh_y, mesh_y) - 1
        shift_x = anchors[3 * second] - anchors[3 * first]
        shift_y = anchors[3 * second + 1] - anchors[3 * first + 1]
        shift_z = anchors[3 * second + 2] - anchors[3 * first + 2]
        shift_x = shift_x + jnp.where(shift_x < -(span_x // 2), span_x, 0) - jnp.where(
            shift_x >= span_x // 2, span_x, 0
        )
        shift_y = shift_y + jnp.where(shift_y < -(span_y // 2), span_y, 0) - jnp.where(
            shift_y >= span_y // 2, span_y, 0
        )
        half_y = lax.shift_right_arithmetic(shift_y, 1)
        odd_y = shift_y - 2 * half_y
        side_x = step_x != 0
        side_y = step_y != 0
        stride = jnp.where(side_x, RIM, SIDE)
        leads = jnp.where(side_y, RIM_LEADS, HALF)
        plus_x = jnp.where(step_x > 0, 1, 0)
        plus_y = jnp.where(step_y > 0, 1, 0)
        base = jnp.where(
            side_x,
            jnp.where(
                side_y,
                BASE_C + (2 * plus_x + plus_y) * (2 * RIM_LEADS * RIM),
                BASE_X + plus_x * (2 * HALF * RIM),
            ),
            jnp.where(side_y, BASE_Y + plus_y * (2 * RIM_LEADS * SIDE), 0),
        )
        base = base + second_k * leads * stride
        start_x = plus_x * LOW
        start_lead = plus_y * LOW_LEADS
        origin_x = jnp.where(step_x < 0, LOW, 0)
        origin_lead = jnp.where(step_y < 0, LOW_LEADS, 0)
        far_start = PAD + base + (start_lead - half_y - origin_lead) * stride + start_x - shift_x - origin_x
        own_start = first_k * (HALF * SIDE) + start_lead * SIDE + start_x
        lane_turn = lax.rem(SIDE * odd_y + shift_z + LANES, LANES)
        lane_back = lax.rem(LANES - lane_turn, LANES)

        def run(tiles, chunk, moved, source, even, odd):
            rows = tiles * 8
            inner = pl.ds(8, rows)
            lane = lane_index(rows)
            depth = lax.rem(lane, SIDE)
            upper = lane >= SIDE
            row = lax.broadcasted_iota(jnp.int32, (rows, LANES), 0) + start_x
            column_part = jnp.where(upper, 1, 0) - shift_y
            same_lead = (lane < SIDE) | (odd_y == 0)
            inside_xz = (
                (row >= shift_x)
                & (row < SIDE + shift_x)
                & (depth >= shift_z)
                & (depth < SIDE + shift_z)
            )
            not_top = depth < SIDE - 1
            not_bottom = depth > 0

            def inside(lead):
                column = column_part + 2 * lead
                return inside_xz & (column >= 0) & (column < SIDE)

            def far_rows(lead):
                return pl.ds(far_start + lead * stride, rows)

            def own_rows(lead):
                return pl.ds(pl.multiple_of(own_start + lead * SIDE, 8), rows)

            def phi_rows(lead):
                return pl.ds(pl.multiple_of(PAD + own_start + lead * SIDE, 8), rows)

            def build(index):
                lead = index * chunk
                loads = [window[far_rows(lead + j), :] for j in range(-1, chunk)]
                for j in range(chunk):
                    picked = jnp.where(same_lead, loads[j + 1], loads[j])
                    turned = pltpu.roll(picked, lane_turn, 1)
                    piece = jnp.where(inside(start_lead + lead + j), turned, 0.0)
                    moved[lead + j] = piece
                    source[lead + j + 1, inner, :] = piece * window[phi_rows(lead + j), :]

            def neighbours(field, lead):
                here = field[lead + 1, inner, :]
                before = field[lead, inner, :]
                after = field[lead + 2, inner, :]
                across = pltpu.roll(here + jnp.where(upper, before, after), SIDE, 1)
                up = jnp.where(not_top, pltpu.roll(here, LANES - 1, 1), 0.0)
                down = jnp.where(not_bottom, pltpu.roll(here, 1, 1), 0.0)
                beside = field[lead + 1, pl.ds(7, rows), :] + field[lead + 1, pl.ds(9, rows), :]
                return here, (across + beside) + (up + down)

            def sweep(old, new, own_part, source_part):
                def body(index):
                    lead = index * chunk
                    for j in range(chunk):
                        here, near = neighbours(old, lead + j)
                        value = own_part * here + near
                        if source_part is not None:
                            value = value + source_part * source[lead + j + 1, inner, :]
                        new[lead + j + 1, inner, :] = value

                return body

            def finish(index):
                lead = index * chunk
                turned = []
                for j in range(chunk):
                    here, near = neighbours(odd, lead + j)
                    value = keep[3] * here + near
                    value = value + (1.0 / (scale[0] * scale[1] * scale[2])) * source[lead + j + 1, inner, :]
                    value = value * total_scale
                    first_sum[own_rows(lead + j), :] = (
                        first_sum[own_rows(lead + j), :] + value * moved[lead + j]
                    )
                    back = jnp.where(
                        inside(start_lead + lead + j), value * window[phi_rows(lead + j), :], 0.0
                    )
                    turned.append(pltpu.roll(back, lane_back, 1))
                targets = [second_sum[far_rows(lead + j), :] for j in range(-1, chunk)]
                for j in range(-1, chunk):
                    here = turned[j] if j >= 0 else 0.0
                    after = turned[j + 1] if j + 1 < chunk else 0.0
                    targets[j + 1] = targets[j + 1] + jnp.where(same_lead, here, after)
                for j in range(-1, chunk):
                    second_sum[far_rows(lead + j), :] = targets[j + 1]

            edge = jnp.zeros((rows, LANES), jnp.float32)
            for field in (source, even, odd):
                field[leads + 1, inner, :] = edge
            chunks = lax.div(leads, chunk)
            for_leads(chunks, build)
            for_leads(chunks, sweep(source, even, keep[1] + 1.0 / scale[0], None))
            for_leads(chunks, sweep(even, odd, keep[2], 1.0 / (scale[0] * scale[1])))
            for_leads(chunks, finish)

        @pl.when(side_x)
        def _():
            run(RIM // 8, 4, moved3, source3, even3, odd3)

        @pl.when(jnp.logical_not(side_x))
        def _():
            run(SIDE // 8, 4, moved8, source8, even8, odd8)

        return carry

    lax.fori_loop(0, count[0], pair_step, 0)

    for (step_x, step_y), out in zip(STEPS, outs):
        base, rows, leads = place_of(step_x, step_y)

        def narrow(lead, base=base, rows=rows, leads=leads, out=out, own=(step_x == 0 and step_y == 0)):
            lanes = pl.ds(pl.multiple_of(lead * LANES, LANES), LANES)
            for k in range(2):
                start = base + k * leads * rows + lead * rows
                value = second_sum[pl.ds(pl.multiple_of(PAD + start, 8), rows), :]
                if own:
                    value = value + first_sum[pl.ds(pl.multiple_of(start, 8), rows), :]
                out[k, :, lanes] = value.astype(out.dtype)

        for_leads(leads, narrow)


GRID_PAD = 8
GRID_ROWS = 88


def cube_root(value):
    inverse = jnp.exp(jnp.log(value) * (-1.0 / 3.0))
    inverse = inverse * (4.0 - value * inverse * inverse * inverse) * (1.0 / 3.0)
    return value * inverse * inverse


def grid_kernel(mesh_x, mesh_y, anchors, *refs):
    pieces = refs[:9]
    core, core_x, core_y, core_xy, applied, potential, grid = refs[9:]
    here_x = lax.axis_index("gx")
    here_y = lax.axis_index("gy")
    slab = core.shape[0]

    def clear(lead):
        grid[pl.ds(pl.multiple_of(lead * GRID_ROWS, 8), GRID_ROWS), :] = jnp.zeros(
            (GRID_ROWS, LANES), jnp.float32
        )

    for_leads(GRID_ROWS, clear)

    def offsets(step_x, step_y, k):
        holder_x = lax.rem(here_x + step_x + mesh_x, mesh_x)
        holder_y = lax.rem(here_y + step_y + mesh_y, mesh_y)
        orbit = (holder_x * mesh_y + holder_y) * 2 + k
        at_x = anchors[3 * orbit] - holder_x * slab
        at_y = anchors[3 * orbit + 1] - holder_y * slab
        return at_x, at_y, anchors[3 * orbit + 2]

    for (step_x, step_y), piece in zip(STEPS, pieces):
        base, rows, leads = place_of(step_x, step_y)
        chunk = 2 if rows == SIDE else 4
        lane = lane_index(rows)
        for k in range(2):
            at_x, at_y, at_z = offsets(step_x, step_y, k)
            row = at_x + step_x * slab + GRID_PAD + (LOW if step_x < 0 else 0)
            column = at_y + step_y * slab + GRID_PAD + (LOW if step_y < 0 else 0)
            start = column * GRID_ROWS + row
            mask = (lane >= at_z) & (lane < at_z + SIDE)
            turn_low = at_z
            turn_high = lax.rem(at_z + SIDE, LANES)

            def deposit(index):
                lead = index * chunk
                added = []
                for j in range(chunk):
                    lanes = pl.ds(pl.multiple_of((lead + j) * LANES, LANES), LANES)
                    value = piece[k, :, lanes].astype(jnp.float32)
                    value = value * value
                    added.append(jnp.where(mask, pltpu.roll(value, turn_low, 1), 0.0))
                    added.append(jnp.where(mask, pltpu.roll(value, turn_high, 1), 0.0))
                where_at = [
                    pl.ds(start + (2 * lead + j) * GRID_ROWS, rows) for j in range(2 * chunk)
                ]
                held = [grid[at, :] for at in where_at]
                for at, old, new in zip(where_at, held, added):
                    grid[at, :] = old + new

            for_leads(leads // chunk, deposit)

    def finish_at(row, column, core_part):
        at = pl.ds((column + GRID_PAD) * GRID_ROWS + GRID_PAD + row, 8, stride=GRID_ROWS)
        value = -xc_factor * cube_root(grid[at, :] + core_part)
        grid[at, :] = value
        return value

    def own_rows(row):
        for column in range(0, slab, 8):
            value = finish_at(row, column, core[row, pl.ds(column, 8), :])
            potential[row, pl.ds(column, 8), :] = value
        above = core_y[row].astype(jnp.float32)
        for column in range(0, RIM, 8):
            finish_at(row, slab + column, above[column : column + 8])

    for_leads(slab, own_rows)

    def rim_rows(row):
        beside = core_x[row].astype(jnp.float32)
        for column in range(0, slab, 8):
            finish_at(slab + row, column, beside[column : column + 8])
        above = core_xy[row].astype(jnp.float32)
        for column in range(0, RIM, 8):
            finish_at(slab + row, slab + column, above[column : column + 8])

    for_leads(RIM, rim_rows)

    lane = lane_index(SIDE)
    for k in range(2):
        at_x, at_y, at_z = offsets(0, 0, k)
        start = (at_y + GRID_PAD) * GRID_ROWS + at_x + GRID_PAD
        turn_low = lax.rem(LANES - at_z, LANES)
        turn_high = lax.rem(LANES + SIDE - at_z, LANES)

        def sample(index):
            for j in range(2):
                lead = index * 2 + j
                lanes = pl.ds(pl.multiple_of(lead * LANES, LANES), LANES)
                low = grid[pl.ds(start + 2 * lead * GRID_ROWS, SIDE), :]
                high = grid[pl.ds(start + (2 * lead + 1) * GRID_ROWS, SIDE), :]
                value = jnp.where(
                    lane < SIDE, pltpu.roll(low, turn_low, 1), pltpu.roll(high, turn_high, 1)
                )
                applied[k, :, lanes] = value * pieces[0][k, :, lanes].astype(jnp.float32)

        for_leads(HALF // 2, sample)


def from_behind(block, axis, distance):
    size = lax.axis_size(axis)
    return lax.ppermute(block, axis, [((i - distance) % size, i) for i in range(size)])


def local(orbitals, anchors, pair_list, pair_count, core_density):
    mesh_x = lax.axis_size("gx")
    mesh_y = lax.axis_size("gy")
    own = orbitals[0, 0]
    flat_anchors = anchors.reshape(-1)
    flat_pairs = pair_list.reshape(-1)
    flat_count = pair_count.reshape(-1)
    low_cut = LOW * SIDE
    rim_cut = RIM * SIDE

    from_left = from_behind(own[:, LOW:], "gx", 1)
    from_right = from_behind(own[:, :RIM], "gx", -1)
    from_below = from_behind(own[..., low_cut:], "gy", 1)
    from_above = from_behind(own[..., :rim_cut], "gy", -1)
    sides = jnp.stack([from_left, from_right])
    below_sides = from_behind(sides[..., low_cut:], "gy", 1)
    above_sides = from_behind(sides[..., :rim_cut], "gy", -1)
    narrow_core = core_density.astype(jnp.bfloat16)
    core_x = from_behind(narrow_core[:RIM], "gx", -1)
    core_y = from_behind(narrow_core[:, :RIM], "gy", -1)
    core_xy = from_behind(core_x[:, :RIM], "gy", -1)
    pieces = [
        own,
        from_left,
        from_right,
        from_below,
        from_above,
        below_sides[0],
        above_sides[0],
        below_sides[1],
        above_sides[1],
    ]
    smem = pl.BlockSpec(memory_space=pltpu.SMEM)
    vmem = pl.BlockSpec(memory_space=pltpu.VMEM)
    term_shapes = [jax.ShapeDtypeStruct(own.shape, jnp.float32)] + [
        jax.ShapeDtypeStruct(piece.shape, jnp.bfloat16) for piece in pieces[1:]
    ]

    def field(rows):
        return pltpu.VMEM((HALF + 2, rows, LANES), jnp.float32)

    terms = pl.pallas_call(
        functools.partial(pair_kernel, mesh_x, mesh_y),
        out_shape=term_shapes,
        in_specs=[smem] * 3 + [vmem] * 9,
        out_specs=[vmem] * 9,
        scratch_shapes=[
            pltpu.VMEM((WINDOW_ROWS + 2 * PAD, LANES), jnp.float32),
            pltpu.VMEM((2 * HALF * SIDE, LANES), jnp.float32),
            pltpu.VMEM((WINDOW_ROWS + 2 * PAD, LANES), jnp.float32),
            pltpu.VMEM((HALF, RIM, LANES), jnp.float32),
            field(RIM + 16),
            field(RIM + 16),
            pltpu.VMEM((HALF, SIDE, LANES), jnp.float32),
            field(SIDE + 16),
            field(SIDE + 16),
            field(RIM + 16),
            field(SIDE + 16),
        ],
        compiler_params=pltpu.CompilerParams(vmem_limit_bytes=56 * 1024 * 1024),
        cost_estimate=pl.CostEstimate(flops=40_000_000, bytes_accessed=8_000_000, transcendentals=0),
        name="pair_terms",
    )(flat_anchors, flat_pairs, flat_count, *pieces)

    applied, potential = pl.pallas_call(
        functools.partial(grid_kernel, mesh_x, mesh_y),
        out_shape=[
            jax.ShapeDtypeStruct(own.shape, jnp.float32),
            jax.ShapeDtypeStruct(core_density.shape, jnp.float32),
        ],
        in_specs=[smem] + [vmem] * 13,
        out_specs=[vmem] * 2,
        scratch_shapes=[pltpu.VMEM((GRID_ROWS * GRID_ROWS, LANES), jnp.float32)],
        compiler_params=pltpu.CompilerParams(vmem_limit_bytes=56 * 1024 * 1024),
        cost_estimate=pl.CostEstimate(flops=20_000_000, bytes_accessed=8_000_000, transcendentals=0),
        name="grid_terms",
    )(flat_anchors, *pieces, core_density, core_x, core_y, core_xy)

    below_left, above_left, below_right, above_right = terms[5:]
    back_below = from_behind(terms[3], "gy", -1)
    back_above = from_behind(terms[4], "gy", 1)
    back_below_sides = from_behind(jnp.stack([below_left, below_right]), "gy", -1).astype(jnp.float32)
    back_above_sides = from_behind(jnp.stack([above_left, above_right]), "gy", 1).astype(jnp.float32)
    side_terms = jnp.stack([terms[1], terms[2]]).astype(jnp.float32)
    side_terms = side_terms.at[..., low_cut:].add(back_below_sides)
    side_terms = side_terms.at[..., :rim_cut].add(back_above_sides).astype(jnp.bfloat16)
    back_left = from_behind(side_terms[0], "gx", -1)
    back_right = from_behind(side_terms[1], "gx", 1)
    exchange = terms[0]
    exchange = exchange.at[..., low_cut:].add(back_below.astype(jnp.float32))
    exchange = exchange.at[..., :rim_cut].add(back_above.astype(jnp.float32))
    exchange = exchange.at[:, LOW:].add(back_left.astype(jnp.float32))
    exchange = exchange.at[:, :RIM].add(back_right.astype(jnp.float32))
    action = applied - exx_share * exchange
    return (action.reshape(orbitals.shape), potential)


def solution(mesh):
    placed = (
        P("gx", "gy", None, None, None),
        P(),
        P("gx", "gy", None, None),
        P("gx", "gy"),
        P("gx", "gy", None),
    )
    return jax.shard_map(
        local,
        mesh=mesh,
        in_specs=placed,
        out_specs=(P("gx", "gy", None, None, None), P("gx", "gy", None)),
        check_vma=False,
    )
```

time: 571 us -> 127 us (0.22)
  the two profiles are of different devices: /device:TPU:101 before, /device:TPU:1 now
where the time goes in v1:
time: 127 us; the launch traced here: 126 us
  Pallas kernels  40.1 us (32%)
  waiting for transfers between devices  39 us (31%)
  starting transfers between devices  31.3 us (25%)
  local copies, waits for them, and re-layouts  8.69 us (7%)
  other arithmetic  5.67 us (4%)
  between operations  1.55 us (1%)
    ppermute x15, waiting for transfers between devices, from_behind(): lax.ppermute(block, axis, [((i - distance) % size, i) for i in range(size)])  39 us
    ppermute x15, starting transfers between devices, from_behind(): lax.ppermute(block, axis, [((i - distance) % size, i) for i in range(size)])  31.3 us
    pallas_call x1, Pallas kernels, local(): pl.pallas_call(functools.partial(grid_kernel, mesh_x, mesh_y), out_shape=...  22.3 us
    pallas_call x1, Pallas kernels, local(): pl.pallas_call(functools.partial(pair_kernel, mesh_x, mesh_y), out_shape=...  17.9 us
  transfers between devices with their start and end apart: 15, of which 4 were waited for; matrix products, arithmetic and copies ran while one was open for 8% of the time, Pallas kernels for 32%

profile of v1, /device:TPU:1, one launch (start us, length us, event | category | flops | bytes accessed | tf_op | source)
XLA Modules:
  0.0 126.4 jit_solution(1652956255570169365)
XLA Ops:
  0.6 1.3 %fusion.6 = (bf16[2,24,4096]{2,1,0:T(8,128)(2,1)S(1)}, bf16[2,24,4096]{2,1,0:T(8,128)(2,1)S(1)}) fusion(bf16[2,64,4096]{2,1,0:T(8,128)(2,1)} %bitcast.25), kind=kLoop, calls=%fused_computation.24 | loop fusion | bytes 1572864 | tf_op jit(solution)/shard_map/slice | solution.py:401
  1.9 2.1 %collective-permute-start = (bf16[2,24,4096]{2,1,0:T(8,128)(2,1)S(1)}, bf16[2,24,4096]{2,1,0:T(8,128)(2,1)S(1)}, u32[]{:S(2)}, u32[]{:S(2)}) collective-permute-start(bf16[2,24,4096]{2,1,0:T(8,128)(2,1)S(1)} %get-tuple-element.99), channel_id=1, source_target_pairs={{112,0},{0,16},{16,32},{32,48},{48,64},{64,80},{80,96},{96,112},{1... | collective-permute-start | bytes 1179656 | tf_op jit(solution)/shard_map/ppermute | solution.py:387
  4.0 4.7 %collective-permute-start.1 = (bf16[2,24,4096]{2,1,0:T(8,128)(2,1)S(1)}, bf16[2,24,4096]{2,1,0:T(8,128)(2,1)S(1)}, u32[]{:S(2)}, u32[]{:S(2)}) collective-permute-start(bf16[2,24,4096]{2,1,0:T(8,128)(2,1)S(1)} %get-tuple-element.98), channel_id=1, source_target_pairs={{16,0},{32,16},{48,32},{64,48},{80,64},{96,80},{112,96},{0,112},{1... | collective-permute-start | bytes 1179656 | tf_op jit(solution)/shard_map/ppermute | solution.py:387
  9.5 1.4 %collective-permute-start.6 = (bf16[24,48,128]{2,1,0:T(8,128)(2,1)}, bf16[24,48,128]{2,1,0:T(8,128)(2,1)S(1)}, u32[]{:S(2)}, u32[]{:S(2)}) collective-permute-start(bf16[24,48,128]{2,1,0:T(8,128)(2,1)} %slice.228), channel_id=1, source_target_pairs={{16,0},{32,16},{48,32},{64,48},{80,64},{96,80},{112,96},{0,112},{1... | collective-permute-start | bytes 884744 | tf_op jit(solution)/shard_map/ppermute | solution.py:387
  10.9 6.5 %collective-permute-done.refs_1_ = bf16[2,24,4096]{2,1,0:T(8,128)(2,1)S(1)} collective-permute-done((bf16[2,24,4096]{2,1,0:T(8,128)(2,1)S(1)}, bf16[2,24,4096]{2,1,0:T(8,128)(2,1)S(1)}, u32[]{:S(2)}, u32[]{:S(2)}) %collective-permute-start) | collective-permute-done | bytes 393248 | tf_op jit(solution)/shard_map/ppermute | solution.py:387
  17.5 0.8 pad_maximum_fusion
  18.3 1.7 %collective-permute-start.5 = (bf16[2,2,24,1536]{3,2,1,0:T(8,128)(2,1)}, bf16[2,2,24,1536]{3,2,1,0:T(8,128)(2,1)}, u32[]{:S(2)}, u32[]{:S(2)}) collective-permute-start(bf16[2,2,24,1536]{3,2,1,0:T(8,128)(2,1)} %get-tuple-element.102), channel_id=1, source_target_pairs={{1,0},{2,1},{3,2},{4,3},{5,4},{6,5},{7,6},{8,7},{9,8},{10,9},{11,1... | collective-permute-start | bytes 884744 | tf_op jit(solution)/shard_map/ppermute | solution.py:387
  20.1 1.1 collective-permute-start.2
  21.2 0.8 collective-permute-start.3
  22.7 3.8 %collective-permute-start.7 = (bf16[48,24,128]{2,1,0:T(8,128)(2,1)}, bf16[48,24,128]{2,1,0:T(8,128)(2,1)S(1)}, u32[]{:S(2)}, u32[]{:S(2)}) collective-permute-start(bf16[48,24,128]{2,1,0:T(8,128)(2,1)} %slice.229), channel_id=1, source_target_pairs={{1,0},{2,1},{3,2},{4,3},{5,4},{6,5},{7,6},{8,7},{9,8},{10,9},{11,1... | collective-permute-start | bytes 884744 | tf_op jit(solution)/shard_map/ppermute | solution.py:387
  26.6 0.8 reshape.201.anchors
  28.9 1.7 %collective-permute-start.4 = (bf16[2,2,24,1536]{3,2,1,0:T(8,128)(2,1)S(1)}, bf16[2,2,24,1536]{3,2,1,0:T(8,128)(2,1)S(1)}, u32[]{:S(2)}, u32[]{:S(2)}) collective-permute-start(bf16[2,2,24,1536]{3,2,1,0:T(8,128)(2,1)S(1)} %get-tuple-element.103), channel_id=1, source_target_pairs={{15,0},{0,1},{1,2},{2,3},{3,4},{4,5},{5,6},{6,7},{7,8},{8,9},{9,10... | collective-permute-start | bytes 884744 | tf_op jit(solution)/shard_map/ppermute | solution.py:387
  30.7 1.7 %slice_bitcast_fusion.2 = (bf16[2,24,1536]{2,1,0:T(8,128)(2,1)}, bf16[2,24,1536]{2,1,0:T(8,128)(2,1)}) fusion(bf16[2,2,24,1536]{3,2,1,0:T(8,128)(2,1)} %collective-permute-done.5), kind=kLoop, calls=%fused_computation.19 | loop fusion | bytes 589824 | tf_op jit(solution)/shard_map/squeeze | solution.py:420
  32.4 8.8 %collective-permute-done.4 = bf16[2,2,24,1536]{3,2,1,0:T(8,128)(2,1)S(1)} collective-permute-done((bf16[2,2,24,1536]{3,2,1,0:T(8,128)(2,1)S(1)}, bf16[2,2,24,1536]{3,2,1,0:T(8,128)(2,1)S(1)}, u32[]{:S(2)}, u32[]{:S(2)}) %collective-permute-start.4) | collective-permute-done | bytes 294944 | tf_op jit(solution)/shard_map/ppermute | solution.py:387
  41.9 0.7 copy-done.6
  42.8 17.9 %pair_terms.1 = (f32[2,64,4096]{2,1,0:T(8,128)}, bf16[2,24,4096]{2,1,0:T(8,128)(2,1)}, bf16[2,24,4096]{2,1,0:T(8,128)(2,1)}, bf16[2,64,1536]{2,1,0:T(8,128)(2,1)...) custom-call(s32[768]{0:T(1024)} %reshape.201.anchors, ...), custom_call_target="tpu_custom_call" | custom-call | flops 40000000 | bytes 8000000 | tf_op jit(solution)/shard_map/pair_terms/pallas_call | solution.py:431
  60.7 1.0 pad_maximum_fusion.3
  61.8 1.0 pad_maximum_fusion.2
  63.3 1.3 %collective-permute-start.9 = (bf16[2,64,1536]{2,1,0:T(8,128)(2,1)}, bf16[2,64,1536]{2,1,0:T(8,128)(2,1)S(1)}, u32[]{:S(2)}, u32[]{:S(2)}) collective-permute-start(bf16[2,64,1536]{2,1,0:T(8,128)(2,1)} %get-tuple-element.87), channel_id=1, source_target_pairs={{1,0},{2,1},{3,2},{4,3},{5,4},{6,5},{7,6},{8,7},{9,8},{10,9},{11,1... | collective-permute-start | bytes 1179656 | tf_op jit(solution)/shard_map/ppermute | solution.py:387
  66.0 22.3 %grid_terms.1 = (f32[2,64,4096]{2,1,0:T(8,128)}, f32[48,48,128]{2,1,0:T(8,128)}) custom-call(s32[768]{0:T(1024)} %reshape.201.anchors, bf16[2,64,4096]{2,1,0:T(8,128)(2,1)} %bitcast.27, bf16[2,24,4096]{2,1,0:T(8,128)(2,1)} %copy-done.3, bf16[2,24,4096]{2,1,0:T(8,128)(2,1)} %copy-done.4, bf16[2,64,1536]{2,1,0:T(8,128)(2,1)} %copy-done.6, ...), custom_call_target="tpu_custom_call" | custom-call | flops 20000000 | bytes 8000000 | tf_op jit(solution)/shard_map/grid_terms/pallas_call | solution.py:454
  88.9 11.5 %collective-permute-start.13 = (bf16[2,24,4096]{2,1,0:T(8,128)(2,1)S(1)}, bf16[2,24,4096]{2,1,0:T(8,128)(2,1)S(1)}, u32[]{:S(2)}, u32[]{:S(2)}) collective-permute-start(bf16[2,24,4096]{2,1,0:T(8,128)(2,1)S(1)} %get-tuple-element.101), channel_id=1, source_target_pairs={{16,0},{32,16},{48,32},{64,48},{80,64},{96,80},{112,96},{0,112},{1... | collective-permute-start | bytes 1179656 | tf_op jit(solution)/shard_map/ppermute | solution.py:387
  100.8 5.0 %collective-permute-done.13 = bf16[2,24,4096]{2,1,0:T(8,128)(2,1)S(1)} collective-permute-done((bf16[2,24,4096]{2,1,0:T(8,128)(2,1)S(1)}, bf16[2,24,4096]{2,1,0:T(8,128)(2,1)S(1)}, u32[]{:S(2)}, u32[]{:S(2)}) %collective-permute-start.13) | collective-permute-done | bytes 393248 | tf_op jit(solution)/shard_map/ppermute | solution.py:387
  106.0 18.6 %collective-permute-done.14 = bf16[2,24,4096]{2,1,0:T(8,128)(2,1)S(1)} collective-permute-done((bf16[2,24,4096]{2,1,0:T(8,128)(2,1)S(1)}, bf16[2,24,4096]{2,1,0:T(8,128)(2,1)S(1)}, u32[]{:S(2)}, u32[]{:S(2)}) %collective-permute-start.14) | collective-permute-done | bytes 393248 | tf_op jit(solution)/shard_map/ppermute | solution.py:387
  124.8 1.5 %subtract_bitcast_fusion = f32[1,1,2,64,4096]{4,3,2,1,0:T(8,128)} fusion(f32[2,64,4096]{2,1,0:T(8,128)S(1)} %copy-done.5, f32[2,64,4096]{2,1,0:T(8,128)S(1)} %fusion), kind=kLoop, calls=%fused_computation | loop fusion | flops 1048576 | bytes 6291456 | tf_op jit(solution)/shard_map/reshape | solution.py:484
  (63 shorter events, 6.7 us)
Async XLA Ops:
  1.9 18.1 %copy-start.1 = (bf16[1,1,2,64,4096]{4,3,2,1,0:T(8,128)(2,1)S(1)}, bf16[1,1,2,64,4096]{4,3,2,1,0:T(8,128)(2,1)}, u32[]{:S(2)}) copy-start(bf16[1,1,2,64,4096]{4,3,2,1,0:T(8,128)(2,1)} %param.17) | copy-start | bytes 3145732
  1.9 15.5 %collective-permute-start = (bf16[2,24,4096]{2,1,0:T(8,128)(2,1)S(1)}, bf16[2,24,4096]{2,1,0:T(8,128)(2,1)S(1)}, u32[]{:S(2)}, u32[]{:S(2)}) collective-permute-start(bf16[2,24,4096]{2,1,0:T(8,128)(2,1)S(1)} %get-tuple-element.99), channel_id=1, source_target_pairs={{112,0},{0,16},{16,32},{32,48},{48,64},{64,80},{80,96},{96,112},{1... | collective-permute-start | bytes 1179656 | tf_op jit(solution)/shard_map/ppermute | solution.py:387
  4.0 13.4 %collective-permute-start.1 = (bf16[2,24,4096]{2,1,0:T(8,128)(2,1)S(1)}, bf16[2,24,4096]{2,1,0:T(8,128)(2,1)S(1)}, u32[]{:S(2)}, u32[]{:S(2)}) collective-permute-start(bf16[2,24,4096]{2,1,0:T(8,128)(2,1)S(1)} %get-tuple-element.98), channel_id=1, source_target_pairs={{16,0},{32,16},{48,32},{64,48},{80,64},{96,80},{112,96},{0,112},{1... | collective-permute-start | bytes 1179656 | tf_op jit(solution)/shard_map/ppermute | solution.py:387
  8.8 17.7 %copy-start.13 = (s32[256,3]{0,1:T(4,128)S(1)}, s32[256,3]{0,1:T(4,128)}, u32[]{:S(2)}) copy-start(s32[256,3]{0,1:T(4,128)} %param.18) | copy-start | bytes 9220
  8.8 18.6 %copy-start.14 = (s32[1,1,12,2]{2,3,1,0:T(2,128)S(1)}, s32[1,1,12,2]{2,3,1,0:T(2,128)}, u32[]{:S(2)}) copy-start(s32[1,1,12,2]{2,3,1,0:T(2,128)} %param.19) | copy-start | bytes 292
  9.5 19.3 %collective-permute-start.6 = (bf16[24,48,128]{2,1,0:T(8,128)(2,1)}, bf16[24,48,128]{2,1,0:T(8,128)(2,1)S(1)}, u32[]{:S(2)}, u32[]{:S(2)}) collective-permute-start(bf16[24,48,128]{2,1,0:T(8,128)(2,1)} %slice.228), channel_id=1, source_target_pairs={{16,0},{32,16},{48,32},{64,48},{80,64},{96,80},{112,96},{0,112},{1... | collective-permute-start | bytes 884744 | tf_op jit(solution)/shard_map/ppermute | solution.py:387
  17.5 14.9 %copy-start.3 = (bf16[2,24,4096]{2,1,0:T(8,128)(2,1)}, bf16[2,24,4096]{2,1,0:T(8,128)(2,1)S(1)}, u32[]{:S(2)}) copy-start(bf16[2,24,4096]{2,1,0:T(8,128)(2,1)S(1)} %collective-permute-done.refs_1_) | copy-start | bytes 1179652
  17.5 14.9 %copy-start.4 = (bf16[2,24,4096]{2,1,0:T(8,128)(2,1)}, bf16[2,24,4096]{2,1,0:T(8,128)(2,1)S(1)}, u32[]{:S(2)}) copy-start(bf16[2,24,4096]{2,1,0:T(8,128)(2,1)S(1)} %collective-permute-done.1.refs_2_) | copy-start | bytes 1179652
  18.3 10.6 %collective-permute-start.5 = (bf16[2,2,24,1536]{3,2,1,0:T(8,128)(2,1)}, bf16[2,2,24,1536]{3,2,1,0:T(8,128)(2,1)}, u32[]{:S(2)}, u32[]{:S(2)}) collective-permute-start(bf16[2,2,24,1536]{3,2,1,0:T(8,128)(2,1)} %get-tuple-element.102), channel_id=1, source_target_pairs={{1,0},{2,1},{3,2},{4,3},{5,4},{6,5},{7,6},{8,7},{9,8},{10,9},{11,1... | collective-permute-start | bytes 884744 | tf_op jit(solution)/shard_map/ppermute | solution.py:387
  20.1 21.9 %collective-permute-start.2 = (bf16[2,64,1536]{2,1,0:T(8,128)(2,1)S(1)}, bf16[2,64,1536]{2,1,0:T(8,128)(2,1)S(1)}, u32[]{:S(2)}, u32[]{:S(2)}) collective-permute-start(bf16[2,64,1536]{2,1,0:T(8,128)(2,1)S(1)} %get-tuple-element.97), channel_id=1, source_target_pairs={{15,0},{0,1},{1,2},{2,3},{3,4},{4,5},{5,6},{6,7},{7,8},{8,9},{9,10... | collective-permute-start | bytes 1179656 | tf_op jit(solution)/shard_map/ppermute | solution.py:387
  21.2 20.7 %collective-permute-start.3 = (bf16[2,64,1536]{2,1,0:T(8,128)(2,1)S(1)}, bf16[2,64,1536]{2,1,0:T(8,128)(2,1)S(1)}, u32[]{:S(2)}, u32[]{:S(2)}) collective-permute-start(bf16[2,64,1536]{2,1,0:T(8,128)(2,1)S(1)} %get-tuple-element.96), channel_id=1, source_target_pairs={{1,0},{2,1},{3,2},{4,3},{5,4},{6,5},{7,6},{8,7},{9,8},{10,9},{11,1... | collective-permute-start | bytes 1179656 | tf_op jit(solution)/shard_map/ppermute | solution.py:387
  22.7 41.9 %collective-permute-start.7 = (bf16[48,24,128]{2,1,0:T(8,128)(2,1)}, bf16[48,24,128]{2,1,0:T(8,128)(2,1)S(1)}, u32[]{:S(2)}, u32[]{:S(2)}) collective-permute-start(bf16[48,24,128]{2,1,0:T(8,128)(2,1)} %slice.229), channel_id=1, source_target_pairs={{1,0},{2,1},{3,2},{4,3},{5,4},{6,5},{7,6},{8,7},{9,8},{10,9},{11,1... | collective-permute-start | bytes 884744 | tf_op jit(solution)/shard_map/ppermute | solution.py:387
  28.8 31.9 %copy-start.8 = (bf16[24,48,128]{2,1,0:T(8,128)(2,1)}, bf16[24,48,128]{2,1,0:T(8,128)(2,1)S(1)}, u32[]{:S(2)}) copy-start(bf16[24,48,128]{2,1,0:T(8,128)(2,1)S(1)} %collective-permute-done.6.refs_10_) | copy-start | bytes 884740
  28.8 36.3 %collective-permute-start.8 = (bf16[24,24,128]{2,1,0:T(8,128)(2,1)S(1)}, bf16[24,24,128]{2,1,0:T(8,128)(2,1)S(1)}, u32[]{:S(2)}, u32[]{:S(2)}) collective-permute-start(bf16[24,24,128]{2,1,0:T(8,128)(2,1)S(1)} %slice.230), channel_id=1, source_target_pairs={{1,0},{2,1},{3,2},{4,3},{5,4},{6,5},{7,6},{8,7},{9,8},{10,9},{11,1... | collective-permute-start | bytes 442376 | tf_op jit(solution)/shard_map/ppermute | solution.py:387
  28.9 12.3 %collective-permute-start.4 = (bf16[2,2,24,1536]{3,2,1,0:T(8,128)(2,1)S(1)}, bf16[2,2,24,1536]{3,2,1,0:T(8,128)(2,1)S(1)}, u32[]{:S(2)}, u32[]{:S(2)}) collective-permute-start(bf16[2,2,24,1536]{3,2,1,0:T(8,128)(2,1)S(1)} %get-tuple-element.103), channel_id=1, source_target_pairs={{15,0},{0,1},{1,2},{2,3},{3,4},{4,5},{5,6},{6,7},{7,8},{8,9},{9,10... | collective-permute-start | bytes 884744 | tf_op jit(solution)/shard_map/ppermute | solution.py:387
  61.7 26.9 %collective-permute-start.12 = (bf16[2,2,24,1536]{3,2,1,0:T(8,128)(2,1)S(1)}, bf16[2,2,24,1536]{3,2,1,0:T(8,128)(2,1)S(1)}, u32[]{:S(2)}, u32[]{:S(2)}) collective-permute-start(bf16[2,2,24,1536]{3,2,1,0:T(8,128)(2,1)S(1)} %pad_maximum_fusion.3), channel_id=1, source_target_pairs={{15,0},{0,1},{1,2},{2,3},{3,4},{4,5},{5,6},{6,7},{7,8},{8,9},{9,10... | collective-permute-start | bytes 884744 | tf_op jit(solution)/shard_map/ppermute | solution.py:387
  62.8 25.6 %collective-permute-start.11 = (bf16[2,2,24,1536]{3,2,1,0:T(8,128)(2,1)S(1)}, bf16[2,2,24,1536]{3,2,1,0:T(8,128)(2,1)S(1)}, u32[]{:S(2)}, u32[]{:S(2)}) collective-permute-start(bf16[2,2,24,1536]{3,2,1,0:T(8,128)(2,1)S(1)} %pad_maximum_fusion.2), channel_id=1, source_target_pairs={{1,0},{2,1},{3,2},{4,3},{5,4},{6,5},{7,6},{8,7},{9,8},{10,9},{11,1... | collective-permute-start | bytes 884744 | tf_op jit(solution)/shard_map/ppermute | solution.py:387
  63.3 37.0 %collective-permute-start.9 = (bf16[2,64,1536]{2,1,0:T(8,128)(2,1)}, bf16[2,64,1536]{2,1,0:T(8,128)(2,1)S(1)}, u32[]{:S(2)}, u32[]{:S(2)}) collective-permute-start(bf16[2,64,1536]{2,1,0:T(8,128)(2,1)} %get-tuple-element.87), channel_id=1, source_target_pairs={{1,0},{2,1},{3,2},{4,3},{5,4},{6,5},{7,6},{8,7},{9,8},{10,9},{11,1... | collective-permute-start | bytes 1179656 | tf_op jit(solution)/shard_map/ppermute | solution.py:387
  64.6 23.6 %copy-start.9 = (bf16[2,24,4096]{2,1,0:T(8,128)(2,1)S(1)}, bf16[2,24,4096]{2,1,0:T(8,128)(2,1)}, u32[]{:S(2)}) copy-start(bf16[2,24,4096]{2,1,0:T(8,128)(2,1)} %get-tuple-element.89) | copy-start | bytes 1179652
  64.6 23.6 %copy-start.10 = (bf16[2,24,4096]{2,1,0:T(8,128)(2,1)S(1)}, bf16[2,24,4096]{2,1,0:T(8,128)(2,1)}, u32[]{:S(2)}) copy-start(bf16[2,24,4096]{2,1,0:T(8,128)(2,1)} %get-tuple-element.90) | copy-start | bytes 1179652
  64.7 35.9 %collective-permute-start.10 = (bf16[2,64,1536]{2,1,0:T(8,128)(2,1)}, bf16[2,64,1536]{2,1,0:T(8,128)(2,1)S(1)}, u32[]{:S(2)}, u32[]{:S(2)}) collective-permute-start(bf16[2,64,1536]{2,1,0:T(8,128)(2,1)} %get-tuple-element.88), channel_id=1, source_target_pairs={{15,0},{0,1},{1,2},{2,3},{3,4},{4,5},{5,6},{6,7},{7,8},{8,9},{9,10... | collective-permute-start | bytes 1179656 | tf_op jit(solution)/shard_map/ppermute | solution.py:387
  88.9 17.0 %collective-permute-start.13 = (bf16[2,24,4096]{2,1,0:T(8,128)(2,1)S(1)}, bf16[2,24,4096]{2,1,0:T(8,128)(2,1)S(1)}, u32[]{:S(2)}, u32[]{:S(2)}) collective-permute-start(bf16[2,24,4096]{2,1,0:T(8,128)(2,1)S(1)} %get-tuple-element.101), channel_id=1, source_target_pairs={{16,0},{32,16},{48,32},{64,48},{80,64},{96,80},{112,96},{0,112},{1... | collective-permute-start | bytes 1179656 | tf_op jit(solution)/shard_map/ppermute | solution.py:387
  100.4 24.2 %collective-permute-start.14 = (bf16[2,24,4096]{2,1,0:T(8,128)(2,1)S(1)}, bf16[2,24,4096]{2,1,0:T(8,128)(2,1)S(1)}, u32[]{:S(2)}, u32[]{:S(2)}) collective-permute-start(bf16[2,24,4096]{2,1,0:T(8,128)(2,1)S(1)} %get-tuple-element.100), channel_id=1, source_target_pairs={{112,0},{0,16},{16,32},{32,48},{48,64},{64,80},{80,96},{96,112},{1... | collective-permute-start | bytes 1179656 | tf_op jit(solution)/shard_map/ppermute | solution.py:387
  100.8 24.1 %copy-start.5 = (f32[2,64,4096]{2,1,0:T(8,128)S(1)}, f32[2,64,4096]{2,1,0:T(8,128)}, u32[]{:S(2)}) copy-start(f32[2,64,4096]{2,1,0:T(8,128)} %get-tuple-element.85) | copy-start | bytes 6291460
  (6 other events, 22.8 us)

commit v2 on v1

--- a/solution.py
+++ b/solution.py
@@ -17,7 +17,8 @@
 RIM_LEADS = RIM // 2
 LOW_LEADS = LOW // 2
 LANES = 128
-PAD = 1024
+PAD = 512
+CHUNKS = [(False, False, 32), (True, False, 32), (False, True, 12), (True, True, 12)]
 
 screen_mass = 0.25
 coupling = 2.0 * math.pi
@@ -56,6 +57,16 @@
     return lax.broadcasted_iota(jnp.int32, (rows, LANES), 1)
 
 
+def one_where(condition):
+    return jnp.where(condition, 1.0, 0.0).astype(jnp.bfloat16)
+
+
+def halves(value):
+    upper = value.astype(jnp.bfloat16)
+    lower = (value - upper.astype(jnp.float32)).astype(jnp.bfloat16)
+    return jnp.concatenate([upper, lower], 1)
+
+
 def for_leads(count, step):
     lax.fori_loop(0, count, lambda index, _: (step(index), 0)[1], 0)
 
@@ -63,7 +74,21 @@
 def pair_kernel(mesh_x, mesh_y, anchors, pairs, count, *refs):
     pieces = refs[:9]
     outs = refs[9:18]
-    window, first_sum, second_sum, moved3, source3, even3, moved8, source8, even8, odd3, odd8 = refs[18:]
+    (
+        window,
+        sums,
+        near,
+        turn_in,
+        turn_out,
+        moved3,
+        source3,
+        even3,
+        odd3,
+        moved8,
+        source8,
+        even8,
+        odd8,
+    ) = refs[18:]
     here_x = lax.axis_index("gx")
     here_y = lax.axis_index("gy")
     span_x = mesh_x * (SIDE - 16)
@@ -82,23 +107,35 @@
 
     zeros64 = jnp.zeros((SIDE, LANES), jnp.float32)
 
-    def clear_first(lead):
-        first_sum[pl.ds(pl.multiple_of(lead * SIDE, SIDE), SIDE), :] = zeros64
-
-    for_leads(2 * HALF, clear_first)
-
-    def clear_second(lead):
-        second_sum[pl.ds(pl.multiple_of(lead * SIDE, SIDE), SIDE), :] = zeros64
-
-    for_leads((WINDOW_ROWS + 2 * PAD) // SIDE, clear_second)
+    def clear_sums(lead):
+        sums[pl.ds(pl.multiple_of(lead * SIDE, SIDE), SIDE), :] = zeros64
+
+    for_leads((WINDOW_ROWS + 2 * PAD) // SIDE, clear_sums)
+
+    def clear_ends(lead):
+        for start in (0, PAD + WINDOW_ROWS):
+            window[pl.ds(pl.multiple_of(start + lead * SIDE, SIDE), SIDE), :] = zeros64
+
+    for_leads(PAD // SIDE, clear_ends)
 
     for field in (source3, even3, odd3, source8, even8, odd8):
         rows = field.shape[1]
-
-        def clear_field(lead, field=field, rows=rows):
-            field[lead] = jnp.zeros((rows, LANES), jnp.float32)
-
-        for_leads(HALF + 2, clear_field)
+        field[0] = jnp.zeros((rows, LANES), jnp.float32)
+
+        def clear_edge(lead, field=field, rows=rows):
+            edge = jnp.zeros((8, LANES), jnp.float32)
+            field[lead, pl.ds(0, 8), :] = edge
+            field[lead, pl.ds(rows - 8, 8), :] = edge
+
+        for_leads(HALF + 2, clear_edge)
+
+    from_lane = lax.broadcasted_iota(jnp.int32, (LANES, LANES), 0)
+    to_lane = lax.broadcasted_iota(jnp.int32, (LANES, LANES), 1)
+    swap = jnp.abs(to_lane - from_lane) == SIDE
+    step = (jnp.abs(to_lane - from_lane) == 1) & ((to_lane < SIDE) == (from_lane < SIDE))
+    for start in (0, LANES):
+        near[start : start + LANES, :LANES] = one_where(step | swap)
+        near[start : start + LANES, LANES:] = one_where(swap)
 
     weights = sweep_weights(SWEEPS)
     diagonal = 6.0 + screen_mass
@@ -147,66 +184,78 @@
         origin_lead = jnp.where(step_y < 0, LOW_LEADS, 0)
         far_start = PAD + base + (start_lead - half_y - origin_lead) * stride + start_x - shift_x - origin_x
         own_start = first_k * (HALF * SIDE) + start_lead * SIDE + start_x
-        lane_turn = lax.rem(SIDE * odd_y + shift_z + LANES, LANES)
-        lane_back = lax.rem(LANES - lane_turn, LANES)
-
-        def run(tiles, chunk, moved, source, even, odd):
+        from_lane = lax.broadcasted_iota(jnp.int32, (LANES, LANES), 0)
+        to_lane = lax.broadcasted_iota(jnp.int32, (LANES, LANES), 1)
+        apart = to_lane - from_lane - shift_z
+        depth = lax.rem(to_lane, SIDE) - shift_z
+        valid = (depth >= 0) & (depth < SIDE)
+        same = valid & (apart == SIDE * odd_y)
+        other = valid & (apart == -SIDE) & (odd_y == 1)
+        turn_in[:LANES] = one_where(same)
+        turn_in[LANES:] = one_where(other)
+        from_lane, to_lane = to_lane, from_lane
+        apart = to_lane - from_lane - shift_z
+        depth = lax.rem(to_lane, SIDE) - shift_z
+        valid = (depth >= 0) & (depth < SIDE)
+        same = one_where(valid & (apart == SIDE * odd_y))
+        other = one_where(valid & (apart == -SIDE) & (odd_y == 1))
+        turn_out[:LANES, :LANES] = same
+        turn_out[LANES:, :LANES] = same
+        turn_out[:LANES, LANES:] = other
+        turn_out[LANES:, LANES:] = other
+
+        def run(tiles, leads, chunk, moved, source, even, odd):
             rows = tiles * 8
             inner = pl.ds(8, rows)
             lane = lane_index(rows)
-            depth = lax.rem(lane, SIDE)
             upper = lane >= SIDE
             row = lax.broadcasted_iota(jnp.int32, (rows, LANES), 0) + start_x
             column_part = jnp.where(upper, 1, 0) - shift_y
-            same_lead = (lane < SIDE) | (odd_y == 0)
-            inside_xz = (
-                (row >= shift_x)
-                & (row < SIDE + shift_x)
-                & (depth >= shift_z)
-                & (depth < SIDE + shift_z)
-            )
-            not_top = depth < SIDE - 1
-            not_bottom = depth > 0
+            inside_x = (row >= shift_x) & (row < SIDE + shift_x)
 
             def inside(lead):
                 column = column_part + 2 * lead
-                return inside_xz & (column >= 0) & (column < SIDE)
+                return inside_x & (column >= 0) & (column < SIDE)
 
             def far_rows(lead):
                 return pl.ds(far_start + lead * stride, rows)
 
             def own_rows(lead):
-                return pl.ds(pl.multiple_of(own_start + lead * SIDE, 8), rows)
-
-            def phi_rows(lead):
                 return pl.ds(pl.multiple_of(PAD + own_start + lead * SIDE, 8), rows)
+
+            def part(value, index):
+                return value[index * rows : (index + 1) * rows]
 
             def build(index):
                 lead = index * chunk
                 loads = [window[far_rows(lead + j), :] for j in range(-1, chunk)]
+                now = jnp.concatenate(loads[1:], 0).astype(jnp.bfloat16)
+                before = jnp.concatenate(loads[:-1], 0).astype(jnp.bfloat16)
+                turned = jnp.dot(
+                    jnp.concatenate([now, before], 1), turn_in[...], preferred_element_type=jnp.float32
+                )
                 for j in range(chunk):
-                    picked = jnp.where(same_lead, loads[j + 1], loads[j])
-                    turned = pltpu.roll(picked, lane_turn, 1)
-                    piece = jnp.where(inside(start_lead + lead + j), turned, 0.0)
+                    piece = jnp.where(inside(start_lead + lead + j), part(turned, j), 0.0)
                     moved[lead + j] = piece
-                    source[lead + j + 1, inner, :] = piece * window[phi_rows(lead + j), :]
-
-            def neighbours(field, lead):
-                here = field[lead + 1, inner, :]
-                before = field[lead, inner, :]
-                after = field[lead + 2, inner, :]
-                across = pltpu.roll(here + jnp.where(upper, before, after), SIDE, 1)
-                up = jnp.where(not_top, pltpu.roll(here, LANES - 1, 1), 0.0)
-                down = jnp.where(not_bottom, pltpu.roll(here, 1, 1), 0.0)
-                beside = field[lead + 1, pl.ds(7, rows), :] + field[lead + 1, pl.ds(9, rows), :]
-                return here, (across + beside) + (up + down)
+                    source[lead + j + 1, inner, :] = piece * window[own_rows(lead + j), :]
+
+            def near_fields(field, lead):
+                values = [field[lead + j, inner, :] for j in range(chunk + 2)]
+                product = jnp.dot(
+                    halves(jnp.concatenate(values, 0)), near[...], preferred_element_type=jnp.float32
+                )
+                for j in range(chunk):
+                    across = jnp.where(
+                        upper, part(product, j + 2)[:, LANES:], part(product, j)[:, LANES:]
+                    )
+                    beside = field[lead + j + 1, pl.ds(7, rows), :] + field[lead + j + 1, pl.ds(9, rows), :]
+                    yield values[j + 1], (part(product, j + 1)[:, :LANES] + across) + beside
 
             def sweep(old, new, own_part, source_part):
                 def body(index):
                     lead = index * chunk
-                    for j in range(chunk):
-                        here, near = neighbours(old, lead + j)
-                        value = own_part * here + near
+                    for j, (here, near_sum) in enumerate(near_fields(old, lead)):
+                        value = own_part * here + near_sum
                         if source_part is not None:
                             value = value + source_part * source[lead + j + 1, inner, :]
                         new[lead + j + 1, inner, :] = value
@@ -215,43 +264,51 @@
 
             def finish(index):
                 lead = index * chunk
-                turned = []
-                for j in range(chunk):
-                    here, near = neighbours(odd, lead + j)
-                    value = keep[3] * here + near
+                back = []
+                for j, (here, near_sum) in enumerate(near_fields(odd, lead)):
+                    value = keep[3] * here + near_sum
                     value = value + (1.0 / (scale[0] * scale[1] * scale[2])) * source[lead + j + 1, inner, :]
                     value = value * total_scale
-                    first_sum[own_rows(lead + j), :] = (
-                        first_sum[own_rows(lead + j), :] + value * moved[lead + j]
+                    sums[own_rows(lead + j), :] = sums[own_rows(lead + j), :] + value * moved[lead + j]
+                    back.append(
+                        jnp.where(inside(start_lead + lead + j), value * window[own_rows(lead + j), :], 0.0)
                     )
-                    back = jnp.where(
-                        inside(start_lead + lead + j), value * window[phi_rows(lead + j), :], 0.0
-                    )
-                    turned.append(pltpu.roll(back, lane_back, 1))
-                targets = [second_sum[far_rows(lead + j), :] for j in range(-1, chunk)]
+                turned = jnp.dot(
+                    halves(jnp.concatenate(back, 0)), turn_out[...], preferred_element_type=jnp.float32
+                )
+                targets = [sums[far_rows(lead + j), :] for j in range(-1, chunk)]
                 for j in range(-1, chunk):
-                    here = turned[j] if j >= 0 else 0.0
-                    after = turned[j + 1] if j + 1 < chunk else 0.0
-                    targets[j + 1] = targets[j + 1] + jnp.where(same_lead, here, after)
+                    total = targets[j + 1]
+                    if j >= 0:
+                        total = total + part(turned, j)[:, :LANES]
+                    if j + 1 < chunk:
+                        total = total + part(turned, j + 1)[:, LANES:]
+                    targets[j + 1] = total
                 for j in range(-1, chunk):
-                    second_sum[far_rows(lead + j), :] = targets[j + 1]
+                    sums[far_rows(lead + j), :] = targets[j + 1]
 
             edge = jnp.zeros((rows, LANES), jnp.float32)
             for field in (source, even, odd):
                 field[leads + 1, inner, :] = edge
-            chunks = lax.div(leads, chunk)
+            chunks = leads // chunk
             for_leads(chunks, build)
             for_leads(chunks, sweep(source, even, keep[1] + 1.0 / scale[0], None))
             for_leads(chunks, sweep(even, odd, keep[2], 1.0 / (scale[0] * scale[1])))
             for_leads(chunks, finish)
 
-        @pl.when(side_x)
-        def _():
-            run(RIM // 8, 4, moved3, source3, even3, odd3)
-
-        @pl.when(jnp.logical_not(side_x))
-        def _():
-            run(SIDE // 8, 4, moved8, source8, even8, odd8)
+        for has_x, has_y, chunk in CHUNKS:
+            narrow = side_x if has_x else jnp.logical_not(side_x)
+            narrow = narrow & (side_y if has_y else jnp.logical_not(side_y))
+            fields = (moved3, source3, even3, odd3) if has_x else (moved8, source8, even8, odd8)
+
+            @pl.when(narrow)
+            def _(has_x=has_x, has_y=has_y, chunk=chunk, fields=fields):
+                run(
+                    (RIM if has_x else SIDE) // 8,
+                    RIM_LEADS if has_y else HALF,
+                    chunk,
+                    *fields,
+                )
 
         return carry
 
@@ -260,16 +317,51 @@
     for (step_x, step_y), out in zip(STEPS, outs):
         base, rows, leads = place_of(step_x, step_y)
 
-        def narrow(lead, base=base, rows=rows, leads=leads, out=out, own=(step_x == 0 and step_y == 0)):
+        def narrow(lead, base=base, rows=rows, leads=leads, out=out):
             lanes = pl.ds(pl.multiple_of(lead * LANES, LANES), LANES)
             for k in range(2):
-                start = base + k * leads * rows + lead * rows
-                value = second_sum[pl.ds(pl.multiple_of(PAD + start, 8), rows), :]
-                if own:
-                    value = value + first_sum[pl.ds(pl.multiple_of(start, 8), rows), :]
-                out[k, :, lanes] = value.astype(out.dtype)
+                start = pl.multiple_of(PAD + base + k * leads * rows + lead * rows, 8)
+                out[k, :, lanes] = sums[pl.ds(start, rows), :].astype(out.dtype)
 
         for_leads(leads, narrow)
+
+
+smem = pl.BlockSpec(memory_space=pltpu.SMEM)
+vmem = pl.BlockSpec(memory_space=pltpu.VMEM)
+
+
+def pairs_call(mesh_x, mesh_y, flat_anchors, flat_pairs, flat_count, pieces):
+    term_shapes = [jax.ShapeDtypeStruct(pieces[0].shape, jnp.float32)] + [
+        jax.ShapeDtypeStruct(piece.shape, jnp.bfloat16) for piece in pieces[1:]
+    ]
+
+    def field(rows):
+        return pltpu.VMEM((HALF + 2, rows, LANES), jnp.float32)
+
+    return pl.pallas_call(
+        functools.partial(pair_kernel, mesh_x, mesh_y),
+        out_shape=term_shapes,
+        in_specs=[smem] * 3 + [vmem] * 9,
+        out_specs=[vmem] * 9,
+        scratch_shapes=[
+            pltpu.VMEM((WINDOW_ROWS + 2 * PAD, LANES), jnp.float32),
+            pltpu.VMEM((WINDOW_ROWS + 2 * PAD, LANES), jnp.float32),
+            pltpu.VMEM((2 * LANES, 2 * LANES), jnp.bfloat16),
+            pltpu.VMEM((2 * LANES, LANES), jnp.bfloat16),
+            pltpu.VMEM((2 * LANES, 2 * LANES), jnp.bfloat16),
+            pltpu.VMEM((HALF, RIM, LANES), jnp.float32),
+            field(RIM + 16),
+            field(RIM + 16),
+            field(RIM + 16),
+            pltpu.VMEM((HALF, SIDE, LANES), jnp.float32),
+            field(SIDE + 16),
+            field(SIDE + 16),
+            field(SIDE + 16),
+        ],
+        compiler_params=pltpu.CompilerParams(vmem_limit_bytes=56 * 1024 * 1024),
+        cost_estimate=pl.CostEstimate(flops=40_000_000, bytes_accessed=8_000_000, transcendentals=0),
+        name="pair_terms",
+    )(flat_anchors, flat_pairs, flat_count, *pieces)
 
 
 GRID_PAD = 8
@@ -419,37 +511,7 @@
         below_sides[1],
         above_sides[1],
     ]
-    smem = pl.BlockSpec(memory_space=pltpu.SMEM)
-    vmem = pl.BlockSpec(memory_space=pltpu.VMEM)
-    term_shapes = [jax.ShapeDtypeStruct(own.shape, jnp.float32)] + [
-        jax.ShapeDtypeStruct(piece.shape, jnp.bfloat16) for piece in pieces[1:]
-    ]
-
-    def field(rows):
-        return pltpu.VMEM((HALF + 2, rows, LANES), jnp.float32)
-
-    terms = pl.pallas_call(
-        functools.partial(pair_kernel, mesh_x, mesh_y),
-        out_shape=term_shapes,
-        in_specs=[smem] * 3 + [vmem] * 9,
-        out_specs=[vmem] * 9,
-        scratch_shapes=[
-            pltpu.VMEM((WINDOW_ROWS + 2 * PAD, LANES), jnp.float32),
-            pltpu.VMEM((2 * HALF * SIDE, LANES), jnp.float32),
-            pltpu.VMEM((WINDOW_ROWS + 2 * PAD, LANES), jnp.float32),
-            pltpu.VMEM((HALF, RIM, LANES), jnp.float32),
-            field(RIM + 16),
-            field(RIM + 16),
-            pltpu.VMEM((HALF, SIDE, LANES), jnp.float32),
-            field(SIDE + 16),
-            field(SIDE + 16),
-            field(RIM + 16),
-            field(SIDE + 16),
-        ],
-        compiler_params=pltpu.CompilerParams(vmem_limit_bytes=56 * 1024 * 1024),
-        cost_estimate=pl.CostEstimate(flops=40_000_000, bytes_accessed=8_000_000, transcendentals=0),
-        name="pair_terms",
-    )(flat_anchors, flat_pairs, flat_count, *pieces)
+    terms = pairs_call(mesh_x, mesh_y, flat_anchors, flat_pairs, flat_count, pieces)
 
     applied, potential = pl.pallas_call(
         functools.partial(grid_kernel, mesh_x, mesh_y),

time: 127 us -> 111 us (0.87)
  the two profiles are of different devices: /device:TPU:1 before, /device:TPU:25 now
where the time goes in v2:
time: 111 us; the launch traced here: 110 us
  Pallas kernels  36.4 us (33%)
  waiting for transfers between devices  33.5 us (30%)
  starting transfers between devices  24.6 us (22%)
  local copies, waits for them, and re-layouts  8.52 us (8%)
  other arithmetic  5.67 us (5%)
  between operations  1.54 us (1%)
    ppermute x15, waiting for transfers between devices, from_behind(): lax.ppermute(block, axis, [((i - distance) % size, i) for i in range(size)])  33.5 us
    ppermute x15, starting transfers between devices, from_behind(): lax.ppermute(block, axis, [((i - distance) % size, i) for i in range(size)])  24.6 us
    pallas_call x1, Pallas kernels, local(): pl.pallas_call(functools.partial(grid_kernel, mesh_x, mesh_y), out_shape=...  22.3 us
    pallas_call x1, Pallas kernels, pairs_call(): pl.pallas_call(functools.partial(pair_kernel, mesh_x, mesh_y), out_shape=...  14.1 us
  transfers between devices with their start and end apart: 15, of which 5 were waited for; matrix products, arithmetic and copies ran while one was open for 9% of the time, Pallas kernels for 33%

profile of v2, /device:TPU:25, one launch (start us, length us, event | category | flops | bytes accessed | tf_op | source)
XLA Modules:
  0.0 110.2 jit_solution(10502567464305364437)
XLA Ops:
  0.6 1.3 %fusion.6 = (bf16[2,24,4096]{2,1,0:T(8,128)(2,1)S(1)}, bf16[2,24,4096]{2,1,0:T(8,128)(2,1)S(1)}) fusion(bf16[2,64,4096]{2,1,0:T(8,128)(2,1)} %bitcast.25), kind=kLoop, calls=%fused_computation.24 | loop fusion | bytes 1572864 | tf_op jit(solution)/shard_map/slice | solution.py:493
  1.9 1.3 %collective-permute-start = (bf16[2,24,4096]{2,1,0:T(8,128)(2,1)S(1)}, bf16[2,24,4096]{2,1,0:T(8,128)(2,1)S(1)}, u32[]{:S(2)}, u32[]{:S(2)}) collective-permute-start(bf16[2,24,4096]{2,1,0:T(8,128)(2,1)S(1)} %get-tuple-element.99), channel_id=1, source_target_pairs={{112,0},{0,16},{16,32},{32,48},{48,64},{64,80},{80,96},{96,112},{1... | collective-permute-start | bytes 1179656 | tf_op jit(solution)/shard_map/ppermute | solution.py:479
  3.2 4.7 %collective-permute-start.1 = (bf16[2,24,4096]{2,1,0:T(8,128)(2,1)S(1)}, bf16[2,24,4096]{2,1,0:T(8,128)(2,1)S(1)}, u32[]{:S(2)}, u32[]{:S(2)}) collective-permute-start(bf16[2,24,4096]{2,1,0:T(8,128)(2,1)S(1)} %get-tuple-element.98), channel_id=1, source_target_pairs={{16,0},{32,16},{48,32},{64,48},{80,64},{96,80},{112,96},{0,112},{1... | collective-permute-start | bytes 1179656 | tf_op jit(solution)/shard_map/ppermute | solution.py:479
  8.7 1.4 %collective-permute-start.6 = (bf16[24,48,128]{2,1,0:T(8,128)(2,1)}, bf16[24,48,128]{2,1,0:T(8,128)(2,1)S(1)}, u32[]{:S(2)}, u32[]{:S(2)}) collective-permute-start(bf16[24,48,128]{2,1,0:T(8,128)(2,1)} %slice.228), channel_id=1, source_target_pairs={{16,0},{32,16},{48,32},{64,48},{80,64},{96,80},{112,96},{0,112},{1... | collective-permute-start | bytes 884744 | tf_op jit(solution)/shard_map/ppermute | solution.py:479
  10.1 6.5 %collective-permute-done.refs_1_ = bf16[2,24,4096]{2,1,0:T(8,128)(2,1)S(1)} collective-permute-done((bf16[2,24,4096]{2,1,0:T(8,128)(2,1)S(1)}, bf16[2,24,4096]{2,1,0:T(8,128)(2,1)S(1)}, u32[]{:S(2)}, u32[]{:S(2)}) %collective-permute-start) | collective-permute-done | bytes 393248 | tf_op jit(solution)/shard_map/ppermute | solution.py:479
  16.6 0.8 pad_maximum_fusion
  17.5 1.7 %collective-permute-start.5 = (bf16[2,2,24,1536]{3,2,1,0:T(8,128)(2,1)}, bf16[2,2,24,1536]{3,2,1,0:T(8,128)(2,1)}, u32[]{:S(2)}, u32[]{:S(2)}) collective-permute-start(bf16[2,2,24,1536]{3,2,1,0:T(8,128)(2,1)} %get-tuple-element.102), channel_id=1, source_target_pairs={{1,0},{2,1},{3,2},{4,3},{5,4},{6,5},{7,6},{8,7},{9,8},{10,9},{11,1... | collective-permute-start | bytes 884744 | tf_op jit(solution)/shard_map/ppermute | solution.py:479
  19.2 1.1 %collective-permute-start.2 = (bf16[2,64,1536]{2,1,0:T(8,128)(2,1)S(1)}, bf16[2,64,1536]{2,1,0:T(8,128)(2,1)S(1)}, u32[]{:S(2)}, u32[]{:S(2)}) collective-permute-start(bf16[2,64,1536]{2,1,0:T(8,128)(2,1)S(1)} %get-tuple-element.97), channel_id=1, source_target_pairs={{15,0},{0,1},{1,2},{2,3},{3,4},{4,5},{5,6},{6,7},{7,8},{8,9},{9,10... | collective-permute-start | bytes 1179656 | tf_op jit(solution)/shard_map/ppermute | solution.py:479
  20.4 0.7 slice.229
  21.1 1.6 %collective-permute-start.7 = (bf16[48,24,128]{2,1,0:T(8,128)(2,1)}, bf16[48,24,128]{2,1,0:T(8,128)(2,1)S(1)}, u32[]{:S(2)}, u32[]{:S(2)}) collective-permute-start(bf16[48,24,128]{2,1,0:T(8,128)(2,1)} %slice.229), channel_id=1, source_target_pairs={{1,0},{2,1},{3,2},{4,3},{5,4},{6,5},{7,6},{8,7},{9,8},{10,9},{11,1... | collective-permute-start | bytes 884744 | tf_op jit(solution)/shard_map/ppermute | solution.py:479
  22.8 0.8 reshape.201.anchors
  25.1 4.0 %collective-permute-done.5 = bf16[2,2,24,1536]{3,2,1,0:T(8,128)(2,1)} collective-permute-done((bf16[2,2,24,1536]{3,2,1,0:T(8,128)(2,1)}, bf16[2,2,24,1536]{3,2,1,0:T(8,128)(2,1)}, u32[]{:S(2)}, u32[]{:S(2)}) %collective-permute-start.5) | collective-permute-done | bytes 294944 | tf_op jit(solution)/shard_map/ppermute | solution.py:479
  29.2 1.7 %slice_bitcast_fusion.2 = (bf16[2,24,1536]{2,1,0:T(8,128)(2,1)}, bf16[2,24,1536]{2,1,0:T(8,128)(2,1)}) fusion(bf16[2,2,24,1536]{3,2,1,0:T(8,128)(2,1)} %collective-permute-done.5), kind=kLoop, calls=%fused_computation.19 | loop fusion | bytes 589824 | tf_op jit(solution)/shard_map/squeeze | solution.py:512
  30.9 9.5 %collective-permute-done.4 = bf16[2,2,24,1536]{3,2,1,0:T(8,128)(2,1)S(1)} collective-permute-done((bf16[2,2,24,1536]{3,2,1,0:T(8,128)(2,1)S(1)}, bf16[2,2,24,1536]{3,2,1,0:T(8,128)(2,1)S(1)}, u32[]{:S(2)}, u32[]{:S(2)}) %collective-permute-start.4) | collective-permute-done | bytes 294944 | tf_op jit(solution)/shard_map/ppermute | solution.py:479
  41.1 0.7 copy-done.6
  42.0 14.1 %pair_terms.1 = (f32[2,64,4096]{2,1,0:T(8,128)}, bf16[2,24,4096]{2,1,0:T(8,128)(2,1)}, bf16[2,24,4096]{2,1,0:T(8,128)(2,1)}, bf16[2,64,1536]{2,1,0:T(8,128)(2,1)...) custom-call(s32[768]{0:T(1024)} %reshape.201.anchors, ...), custom_call_target="tpu_custom_call" | custom-call | flops 40000000 | bytes 8000000 | tf_op jit(solution)/shard_map/pair_terms/pallas_call | solution.py:341
  56.1 1.0 pad_maximum_fusion.3
  57.2 1.0 pad_maximum_fusion.2
  58.9 1.9 %collective-permute-start.10 = (bf16[2,64,1536]{2,1,0:T(8,128)(2,1)}, bf16[2,64,1536]{2,1,0:T(8,128)(2,1)S(1)}, u32[]{:S(2)}, u32[]{:S(2)}) collective-permute-start(bf16[2,64,1536]{2,1,0:T(8,128)(2,1)} %get-tuple-element.88), channel_id=1, source_target_pairs={{15,0},{0,1},{1,2},{2,3},{3,4},{4,5},{5,6},{6,7},{7,8},{8,9},{9,10... | collective-permute-start | bytes 1179656 | tf_op jit(solution)/shard_map/ppermute | solution.py:479
  61.5 22.3 %grid_terms.1 = (f32[2,64,4096]{2,1,0:T(8,128)}, f32[48,48,128]{2,1,0:T(8,128)}) custom-call(s32[768]{0:T(1024)} %reshape.201.anchors, bf16[2,64,4096]{2,1,0:T(8,128)(2,1)} %bitcast.27, bf16[2,24,4096]{2,1,0:T(8,128)(2,1)} %copy-done.3, bf16[2,24,4096]{2,1,0:T(8,128)(2,1)} %copy-done.4, bf16[2,64,1536]{2,1,0:T(8,128)(2,1)} %copy-done.6, ...), custom_call_target="tpu_custom_call" | custom-call | flops 20000000 | bytes 8000000 | tf_op jit(solution)/shard_map/grid_terms/pallas_call | solution.py:516
  84.3 10.1 %collective-permute-start.13 = (bf16[2,24,4096]{2,1,0:T(8,128)(2,1)S(1)}, bf16[2,24,4096]{2,1,0:T(8,128)(2,1)S(1)}, u32[]{:S(2)}, u32[]{:S(2)}) collective-permute-start(bf16[2,24,4096]{2,1,0:T(8,128)(2,1)S(1)} %get-tuple-element.101), channel_id=1, source_target_pairs={{16,0},{32,16},{48,32},{64,48},{80,64},{96,80},{112,96},{0,112},{1... | collective-permute-start | bytes 1179656 | tf_op jit(solution)/shard_map/ppermute | solution.py:479
  94.8 7.8 %collective-permute-done.13 = bf16[2,24,4096]{2,1,0:T(8,128)(2,1)S(1)} collective-permute-done((bf16[2,24,4096]{2,1,0:T(8,128)(2,1)S(1)}, bf16[2,24,4096]{2,1,0:T(8,128)(2,1)S(1)}, u32[]{:S(2)}, u32[]{:S(2)}) %collective-permute-start.13) | collective-permute-done | bytes 393248 | tf_op jit(solution)/shard_map/ppermute | solution.py:479
  102.9 5.6 %collective-permute-done.14 = bf16[2,24,4096]{2,1,0:T(8,128)(2,1)S(1)} collective-permute-done((bf16[2,24,4096]{2,1,0:T(8,128)(2,1)S(1)}, bf16[2,24,4096]{2,1,0:T(8,128)(2,1)S(1)}, u32[]{:S(2)}, u32[]{:S(2)}) %collective-permute-start.14) | collective-permute-done | bytes 393248 | tf_op jit(solution)/shard_map/ppermute | solution.py:479
  108.7 1.5 %subtract_bitcast_fusion = f32[1,1,2,64,4096]{4,3,2,1,0:T(8,128)} fusion(f32[2,64,4096]{2,1,0:T(8,128)S(1)} %copy-done.5, f32[2,64,4096]{2,1,0:T(8,128)S(1)} %fusion), kind=kLoop, calls=%fused_computation | loop fusion | flops 1048576 | bytes 6291456 | tf_op jit(solution)/shard_map/reshape | solution.py:546
  (63 shorter events, 5.4 us)
Async XLA Ops:
  1.9 17.3 %copy-start.1 = (bf16[1,1,2,64,4096]{4,3,2,1,0:T(8,128)(2,1)S(1)}, bf16[1,1,2,64,4096]{4,3,2,1,0:T(8,128)(2,1)}, u32[]{:S(2)}) copy-start(bf16[1,1,2,64,4096]{4,3,2,1,0:T(8,128)(2,1)} %param.17) | copy-start | bytes 3145732
  1.9 14.7 %collective-permute-start = (bf16[2,24,4096]{2,1,0:T(8,128)(2,1)S(1)}, bf16[2,24,4096]{2,1,0:T(8,128)(2,1)S(1)}, u32[]{:S(2)}, u32[]{:S(2)}) collective-permute-start(bf16[2,24,4096]{2,1,0:T(8,128)(2,1)S(1)} %get-tuple-element.99), channel_id=1, source_target_pairs={{112,0},{0,16},{16,32},{32,48},{48,64},{64,80},{80,96},{96,112},{1... | collective-permute-start | bytes 1179656 | tf_op jit(solution)/shard_map/ppermute | solution.py:479
  3.2 13.4 %collective-permute-start.1 = (bf16[2,24,4096]{2,1,0:T(8,128)(2,1)S(1)}, bf16[2,24,4096]{2,1,0:T(8,128)(2,1)S(1)}, u32[]{:S(2)}, u32[]{:S(2)}) collective-permute-start(bf16[2,24,4096]{2,1,0:T(8,128)(2,1)S(1)} %get-tuple-element.98), channel_id=1, source_target_pairs={{16,0},{32,16},{48,32},{64,48},{80,64},{96,80},{112,96},{0,112},{1... | collective-permute-start | bytes 1179656 | tf_op jit(solution)/shard_map/ppermute | solution.py:479
  8.0 14.7 %copy-start.13 = (s32[256,3]{0,1:T(4,128)S(1)}, s32[256,3]{0,1:T(4,128)}, u32[]{:S(2)}) copy-start(s32[256,3]{0,1:T(4,128)} %param.18) | copy-start | bytes 9220
  8.0 15.7 %copy-start.14 = (s32[1,1,12,2]{2,3,1,0:T(2,128)S(1)}, s32[1,1,12,2]{2,3,1,0:T(2,128)}, u32[]{:S(2)}) copy-start(s32[1,1,12,2]{2,3,1,0:T(2,128)} %param.19) | copy-start | bytes 292
  8.7 16.3 %collective-permute-start.6 = (bf16[24,48,128]{2,1,0:T(8,128)(2,1)}, bf16[24,48,128]{2,1,0:T(8,128)(2,1)S(1)}, u32[]{:S(2)}, u32[]{:S(2)}) collective-permute-start(bf16[24,48,128]{2,1,0:T(8,128)(2,1)} %slice.228), channel_id=1, source_target_pairs={{16,0},{32,16},{48,32},{64,48},{80,64},{96,80},{112,96},{0,112},{1... | collective-permute-start | bytes 884744 | tf_op jit(solution)/shard_map/ppermute | solution.py:479
  16.6 14.2 %copy-start.3 = (bf16[2,24,4096]{2,1,0:T(8,128)(2,1)}, bf16[2,24,4096]{2,1,0:T(8,128)(2,1)S(1)}, u32[]{:S(2)}) copy-start(bf16[2,24,4096]{2,1,0:T(8,128)(2,1)S(1)} %collective-permute-done.refs_1_) | copy-start | bytes 1179652
  16.6 14.2 %copy-start.4 = (bf16[2,24,4096]{2,1,0:T(8,128)(2,1)}, bf16[2,24,4096]{2,1,0:T(8,128)(2,1)S(1)}, u32[]{:S(2)}) copy-start(bf16[2,24,4096]{2,1,0:T(8,128)(2,1)S(1)} %collective-permute-done.1.refs_2_) | copy-start | bytes 1179652
  17.5 11.7 %collective-permute-start.5 = (bf16[2,2,24,1536]{3,2,1,0:T(8,128)(2,1)}, bf16[2,2,24,1536]{3,2,1,0:T(8,128)(2,1)}, u32[]{:S(2)}, u32[]{:S(2)}) collective-permute-start(bf16[2,2,24,1536]{3,2,1,0:T(8,128)(2,1)} %get-tuple-element.102), channel_id=1, source_target_pairs={{1,0},{2,1},{3,2},{4,3},{5,4},{6,5},{7,6},{8,7},{9,8},{10,9},{11,1... | collective-permute-start | bytes 884744 | tf_op jit(solution)/shard_map/ppermute | solution.py:479
  19.2 21.9 %collective-permute-start.2 = (bf16[2,64,1536]{2,1,0:T(8,128)(2,1)S(1)}, bf16[2,64,1536]{2,1,0:T(8,128)(2,1)S(1)}, u32[]{:S(2)}, u32[]{:S(2)}) collective-permute-start(bf16[2,64,1536]{2,1,0:T(8,128)(2,1)S(1)} %get-tuple-element.97), channel_id=1, source_target_pairs={{15,0},{0,1},{1,2},{2,3},{3,4},{4,5},{5,6},{6,7},{7,8},{8,9},{9,10... | collective-permute-start | bytes 1179656 | tf_op jit(solution)/shard_map/ppermute | solution.py:479
  20.4 20.7 %collective-permute-start.3 = (bf16[2,64,1536]{2,1,0:T(8,128)(2,1)S(1)}, bf16[2,64,1536]{2,1,0:T(8,128)(2,1)S(1)}, u32[]{:S(2)}, u32[]{:S(2)}) collective-permute-start(bf16[2,64,1536]{2,1,0:T(8,128)(2,1)S(1)} %get-tuple-element.96), channel_id=1, source_target_pairs={{1,0},{2,1},{3,2},{4,3},{5,4},{6,5},{7,6},{8,7},{9,8},{10,9},{11,1... | collective-permute-start | bytes 1179656 | tf_op jit(solution)/shard_map/ppermute | solution.py:479
  21.1 37.8 %collective-permute-start.7 = (bf16[48,24,128]{2,1,0:T(8,128)(2,1)}, bf16[48,24,128]{2,1,0:T(8,128)(2,1)S(1)}, u32[]{:S(2)}, u32[]{:S(2)}) collective-permute-start(bf16[48,24,128]{2,1,0:T(8,128)(2,1)} %slice.229), channel_id=1, source_target_pairs={{1,0},{2,1},{3,2},{4,3},{5,4},{6,5},{7,6},{8,7},{9,8},{10,9},{11,1... | collective-permute-start | bytes 884744 | tf_op jit(solution)/shard_map/ppermute | solution.py:479
  25.0 31.1 %copy-start.8 = (bf16[24,48,128]{2,1,0:T(8,128)(2,1)}, bf16[24,48,128]{2,1,0:T(8,128)(2,1)S(1)}, u32[]{:S(2)}) copy-start(bf16[24,48,128]{2,1,0:T(8,128)(2,1)S(1)} %collective-permute-done.6.refs_10_) | copy-start | bytes 884740
  25.0 35.8 %collective-permute-start.8 = (bf16[24,24,128]{2,1,0:T(8,128)(2,1)S(1)}, bf16[24,24,128]{2,1,0:T(8,128)(2,1)S(1)}, u32[]{:S(2)}, u32[]{:S(2)}) collective-permute-start(bf16[24,24,128]{2,1,0:T(8,128)(2,1)S(1)} %slice.230), channel_id=1, source_target_pairs={{1,0},{2,1},{3,2},{4,3},{5,4},{6,5},{7,6},{8,7},{9,8},{10,9},{11,1... | collective-permute-start | bytes 442376 | tf_op jit(solution)/shard_map/ppermute | solution.py:479
  29.1 11.2 %collective-permute-start.4 = (bf16[2,2,24,1536]{3,2,1,0:T(8,128)(2,1)S(1)}, bf16[2,2,24,1536]{3,2,1,0:T(8,128)(2,1)S(1)}, u32[]{:S(2)}, u32[]{:S(2)}) collective-permute-start(bf16[2,2,24,1536]{3,2,1,0:T(8,128)(2,1)S(1)} %get-tuple-element.103), channel_id=1, source_target_pairs={{15,0},{0,1},{1,2},{2,3},{3,4},{4,5},{5,6},{6,7},{7,8},{8,9},{9,10... | collective-permute-start | bytes 884744 | tf_op jit(solution)/shard_map/ppermute | solution.py:479
  57.1 26.9 %collective-permute-start.12 = (bf16[2,2,24,1536]{3,2,1,0:T(8,128)(2,1)S(1)}, bf16[2,2,24,1536]{3,2,1,0:T(8,128)(2,1)S(1)}, u32[]{:S(2)}, u32[]{:S(2)}) collective-permute-start(bf16[2,2,24,1536]{3,2,1,0:T(8,128)(2,1)S(1)} %pad_maximum_fusion.3), channel_id=1, source_target_pairs={{15,0},{0,1},{1,2},{2,3},{3,4},{4,5},{5,6},{6,7},{7,8},{8,9},{9,10... | collective-permute-start | bytes 884744 | tf_op jit(solution)/shard_map/ppermute | solution.py:479
  58.2 25.6 %collective-permute-start.11 = (bf16[2,2,24,1536]{3,2,1,0:T(8,128)(2,1)S(1)}, bf16[2,2,24,1536]{3,2,1,0:T(8,128)(2,1)S(1)}, u32[]{:S(2)}, u32[]{:S(2)}) collective-permute-start(bf16[2,2,24,1536]{3,2,1,0:T(8,128)(2,1)S(1)} %pad_maximum_fusion.2), channel_id=1, source_target_pairs={{1,0},{2,1},{3,2},{4,3},{5,4},{6,5},{7,6},{8,7},{9,8},{10,9},{11,1... | collective-permute-start | bytes 884744 | tf_op jit(solution)/shard_map/ppermute | solution.py:479
  58.8 35.7 %collective-permute-start.9 = (bf16[2,64,1536]{2,1,0:T(8,128)(2,1)}, bf16[2,64,1536]{2,1,0:T(8,128)(2,1)S(1)}, u32[]{:S(2)}, u32[]{:S(2)}) collective-permute-start(bf16[2,64,1536]{2,1,0:T(8,128)(2,1)} %get-tuple-element.87), channel_id=1, source_target_pairs={{1,0},{2,1},{3,2},{4,3},{5,4},{6,5},{7,6},{8,7},{9,8},{10,9},{11,1... | collective-permute-start | bytes 1179656 | tf_op jit(solution)/shard_map/ppermute | solution.py:479
  58.9 24.8 %copy-start.9 = (bf16[2,24,4096]{2,1,0:T(8,128)(2,1)S(1)}, bf16[2,24,4096]{2,1,0:T(8,128)(2,1)}, u32[]{:S(2)}) copy-start(bf16[2,24,4096]{2,1,0:T(8,128)(2,1)} %get-tuple-element.89) | copy-start | bytes 1179652
  58.9 24.8 %copy-start.10 = (bf16[2,24,4096]{2,1,0:T(8,128)(2,1)S(1)}, bf16[2,24,4096]{2,1,0:T(8,128)(2,1)}, u32[]{:S(2)}) copy-start(bf16[2,24,4096]{2,1,0:T(8,128)(2,1)} %get-tuple-element.90) | copy-start | bytes 1179652
  58.9 35.8 %collective-permute-start.10 = (bf16[2,64,1536]{2,1,0:T(8,128)(2,1)}, bf16[2,64,1536]{2,1,0:T(8,128)(2,1)S(1)}, u32[]{:S(2)}, u32[]{:S(2)}) collective-permute-start(bf16[2,64,1536]{2,1,0:T(8,128)(2,1)} %get-tuple-element.88), channel_id=1, source_target_pairs={{15,0},{0,1},{1,2},{2,3},{3,4},{4,5},{5,6},{6,7},{7,8},{8,9},{9,10... | collective-permute-start | bytes 1179656 | tf_op jit(solution)/shard_map/ppermute | solution.py:479
  84.3 18.4 %collective-permute-start.13 = (bf16[2,24,4096]{2,1,0:T(8,128)(2,1)S(1)}, bf16[2,24,4096]{2,1,0:T(8,128)(2,1)S(1)}, u32[]{:S(2)}, u32[]{:S(2)}) collective-permute-start(bf16[2,24,4096]{2,1,0:T(8,128)(2,1)S(1)} %get-tuple-element.101), channel_id=1, source_target_pairs={{16,0},{32,16},{48,32},{64,48},{80,64},{96,80},{112,96},{0,112},{1... | collective-permute-start | bytes 1179656 | tf_op jit(solution)/shard_map/ppermute | solution.py:479
  94.5 14.0 %collective-permute-start.14 = (bf16[2,24,4096]{2,1,0:T(8,128)(2,1)S(1)}, bf16[2,24,4096]{2,1,0:T(8,128)(2,1)S(1)}, u32[]{:S(2)}, u32[]{:S(2)}) collective-permute-start(bf16[2,24,4096]{2,1,0:T(8,128)(2,1)S(1)} %get-tuple-element.100), channel_id=1, source_target_pairs={{112,0},{0,16},{16,32},{32,48},{48,64},{64,80},{80,96},{96,112},{1... | collective-permute-start | bytes 1179656 | tf_op jit(solution)/shard_map/ppermute | solution.py:479
  94.8 13.9 %copy-start.5 = (f32[2,64,4096]{2,1,0:T(8,128)S(1)}, f32[2,64,4096]{2,1,0:T(8,128)}, u32[]{:S(2)}) copy-start(f32[2,64,4096]{2,1,0:T(8,128)} %get-tuple-element.85) | copy-start | bytes 6291460
  (6 other events, 21.8 us)

commit v3 on v2

--- a/solution.py
+++ b/solution.py
@@ -73,7 +73,8 @@
 
 def pair_kernel(mesh_x, mesh_y, anchors, pairs, count, *refs):
     pieces = refs[:9]
-    outs = refs[9:18]
+    own_out, grid_out = refs[9:11]
+    outs = refs[11:19]
     (
         window,
         sums,
@@ -88,7 +89,10 @@
         source8,
         even8,
         odd8,
-    ) = refs[18:]
+        grid,
+        place,
+        copies,
+    ) = refs[19:]
     here_x = lax.axis_index("gx")
     here_y = lax.axis_index("gy")
     span_x = mesh_x * (SIDE - 16)
@@ -99,9 +103,15 @@
 
         def widen(lead, base=base, rows=rows, leads=leads, piece=piece):
             lanes = pl.ds(pl.multiple_of(lead * LANES, LANES), LANES)
+            if rows == RIM:
+                both = piece[:, lanes].astype(jnp.float32)
             for k in range(2):
                 start = pl.multiple_of(PAD + base + k * leads * rows + lead * rows, 8)
-                window[pl.ds(start, rows), :] = piece[k, :, lanes].astype(jnp.float32)
+                if rows == RIM:
+                    value = both[k * RIM : (k + 1) * RIM]
+                else:
+                    value = piece[k, :, lanes].astype(jnp.float32)
+                window[pl.ds(start, rows), :] = value
 
         for_leads(leads, widen)
 
@@ -314,26 +324,110 @@
 
     lax.fori_loop(0, count[0], pair_step, 0)
 
-    for (step_x, step_y), out in zip(STEPS, outs):
+    own_copy = pltpu.make_async_copy(sums.at[pl.ds(PAD, BASE_X)], own_out, copies.at[0])
+    own_copy.start()
+
+    for (step_x, step_y), out in zip(STEPS[1:], outs):
         base, rows, leads = place_of(step_x, step_y)
 
         def narrow(lead, base=base, rows=rows, leads=leads, out=out):
             lanes = pl.ds(pl.multiple_of(lead * LANES, LANES), LANES)
+            values = []
             for k in range(2):
                 start = pl.multiple_of(PAD + base + k * leads * rows + lead * rows, 8)
-                out[k, :, lanes] = sums[pl.ds(start, rows), :].astype(out.dtype)
+                values.append(sums[pl.ds(start, rows), :])
+            if rows == RIM:
+                out[:, lanes] = jnp.concatenate(values, 0).astype(out.dtype)
+            else:
+                for k in range(2):
+                    out[k, :, lanes] = values[k].astype(out.dtype)
 
         for_leads(leads, narrow)
 
+    def clear_grid(lead):
+        start = pl.multiple_of(lead * GRID_ROWS, 8)
+        grid[pl.ds(start, GRID_ROWS), :] = jnp.zeros((GRID_ROWS, LANES), jnp.float32)
+
+    for_leads(GRID_ROWS, clear_grid)
+    slab = SIDE - 16
+
+    def deposit(step_x, step_y, k, base, rows, leads):
+        holder_x = lax.rem(here_x + step_x + mesh_x, mesh_x)
+        holder_y = lax.rem(here_y + step_y + mesh_y, mesh_y)
+        orbit = (holder_x * mesh_y + holder_y) * 2 + k
+        at_x = anchors[3 * orbit] - holder_x * slab
+        at_y = anchors[3 * orbit + 1] - holder_y * slab
+        at_z = anchors[3 * orbit + 2]
+        row = at_x + step_x * slab + GRID_PAD + jnp.where(step_x < 0, LOW, 0)
+        column = at_y + step_y * slab + GRID_PAD + jnp.where(step_y < 0, LOW, 0)
+        start = column * GRID_ROWS + row
+        from_lane = lax.broadcasted_iota(jnp.int32, (LANES, LANES), 0)
+        apart = lax.broadcasted_iota(jnp.int32, (LANES, LANES), 1) - from_lane - at_z
+        low = one_where((from_lane < SIDE) & (apart == 0))
+        high = one_where((from_lane >= SIDE) & (apart == -SIDE))
+        for half in (0, LANES):
+            place[half : half + LANES, :LANES] = low
+            place[half : half + LANES, LANES:] = high
+        block = 16
+        for first in range(0, leads, block):
+            size = min(block, leads - first)
+            value = window[pl.ds(pl.multiple_of(PAD + base + first * rows, 8), size * rows), :]
+            placed = jnp.dot(halves(value * value), place[...], preferred_element_type=jnp.float32)
+            for j in range(size):
+                for odd_column in (0, 1):
+                    at = pl.ds(start + (2 * (first + j) + odd_column) * GRID_ROWS, rows)
+                    part = placed[j * rows : (j + 1) * rows, odd_column * LANES : (odd_column + 1) * LANES]
+                    grid[at, :] = grid[at, :] + part
+
+    for k in range(2):
+        deposit(0, 0, k, k * HALF * SIDE, SIDE, HALF)
+
+    def deposit_x(index, carry):
+        deposit(2 * (index // 2) - 1, 0, lax.rem(index, 2), BASE_X + index * (HALF * RIM), RIM, HALF)
+        return carry
+
+    def deposit_y(index, carry):
+        deposit(
+            0, 2 * (index // 2) - 1, lax.rem(index, 2), BASE_Y + index * (RIM_LEADS * SIDE), SIDE, RIM_LEADS
+        )
+        return carry
+
+    def deposit_corner(index, carry):
+        deposit(
+            2 * (index // 4) - 1,
+            2 * lax.rem(index // 2, 2) - 1,
+            lax.rem(index, 2),
+            BASE_C + index * (RIM_LEADS * RIM),
+            RIM,
+            RIM_LEADS,
+        )
+        return carry
+
+    lax.fori_loop(0, 4, deposit_x, 0)
+    lax.fori_loop(0, 4, deposit_y, 0)
+    lax.fori_loop(0, 8, deposit_corner, 0)
+    grid_copy = pltpu.make_async_copy(grid.at[pl.ds(GRID_PAD * GRID_ROWS, EDGE_ROWS)], grid_out, copies.at[1])
+    grid_copy.start()
+    own_copy.wait()
+    grid_copy.wait()
+
+
+GRID_PAD = 8
+GRID_ROWS = 88
+EDGE = SIDE - 16 + RIM
+EDGE_ROWS = (EDGE + 1) * GRID_ROWS
+hbm = pl.BlockSpec(memory_space=pl.ANY)
+MESH = pl.DeviceIdType.MESH
 
 smem = pl.BlockSpec(memory_space=pltpu.SMEM)
 vmem = pl.BlockSpec(memory_space=pltpu.VMEM)
 
 
 def pairs_call(mesh_x, mesh_y, flat_anchors, flat_pairs, flat_count, pieces):
-    term_shapes = [jax.ShapeDtypeStruct(pieces[0].shape, jnp.float32)] + [
-        jax.ShapeDtypeStruct(piece.shape, jnp.bfloat16) for piece in pieces[1:]
-    ]
+    term_shapes = [
+        jax.ShapeDtypeStruct((BASE_X, LANES), jnp.float32),
+        jax.ShapeDtypeStruct((EDGE_ROWS, LANES), jnp.float32),
+    ] + [jax.ShapeDtypeStruct(piece.shape, jnp.bfloat16) for piece in pieces[1:]]
 
     def field(rows):
         return pltpu.VMEM((HALF + 2, rows, LANES), jnp.float32)
@@ -342,7 +436,7 @@
         functools.partial(pair_kernel, mesh_x, mesh_y),
         out_shape=term_shapes,
         in_specs=[smem] * 3 + [vmem] * 9,
-        out_specs=[vmem] * 9,
+        out_specs=[hbm] * 2 + [vmem] * 8,
         scratch_shapes=[
             pltpu.VMEM((WINDOW_ROWS + 2 * PAD, LANES), jnp.float32),
             pltpu.VMEM((WINDOW_ROWS + 2 * PAD, LANES), jnp.float32),
@@ -357,6 +451,9 @@
             field(SIDE + 16),
             field(SIDE + 16),
             field(SIDE + 16),
+            pltpu.VMEM((GRID_ROWS * GRID_ROWS, LANES), jnp.float32),
+            pltpu.VMEM((2 * LANES, 2 * LANES), jnp.bfloat16),
+            pltpu.SemaphoreType.DMA((2,)),
         ],
         compiler_params=pltpu.CompilerParams(vmem_limit_bytes=56 * 1024 * 1024),
         cost_estimate=pl.CostEstimate(flops=40_000_000, bytes_accessed=8_000_000, transcendentals=0),
@@ -364,119 +461,205 @@
     )(flat_anchors, flat_pairs, flat_count, *pieces)
 
 
-GRID_PAD = 8
-GRID_ROWS = 88
-
-
 def cube_root(value):
     inverse = jnp.exp(jnp.log(value) * (-1.0 / 3.0))
     inverse = inverse * (4.0 - value * inverse * inverse * inverse) * (1.0 / 3.0)
     return value * inverse * inverse
 
 
-def grid_kernel(mesh_x, mesh_y, anchors, *refs):
-    pieces = refs[:9]
-    core, core_x, core_y, core_xy, applied, potential, grid = refs[9:]
+def greet(mesh_x, mesh_y):
     here_x = lax.axis_index("gx")
     here_y = lax.axis_index("gy")
+    left = (lax.rem(here_x + mesh_x - 1, mesh_x), here_y)
+    right = (lax.rem(here_x + 1, mesh_x), here_y)
+    below = (here_x, lax.rem(here_y + mesh_y - 1, mesh_y))
+    above = (here_x, lax.rem(here_y + 1, mesh_y))
+    barrier = pltpu.get_barrier_semaphore()
+    for neighbour in (left, right, below, above):
+        pl.semaphore_signal(barrier, inc=1, device_id=neighbour, device_id_type=MESH)
+    pl.semaphore_wait(barrier, 4)
+    return left, right, below, above
+
+
+def gather_kernel(mesh_x, mesh_y, own, *refs):
+    outs = refs[:8]
+    send_low, send_high, sent, landed = refs[8:]
+    left, right, below, above = greet(mesh_x, mesh_y)
+    started = []
+
+    def send(source, slot, device):
+        copy = pltpu.make_async_remote_copy(
+            src_ref=source,
+            dst_ref=outs[slot],
+            send_sem=sent.at[slot],
+            recv_sem=landed.at[slot],
+            device_id=device,
+            device_id_type=MESH,
+        )
+        copy.start()
+        started.append(copy)
+        return copy
+
+    def prepare(lead):
+        lanes = pl.ds(pl.multiple_of(lead * LANES, LANES), LANES)
+        values = [own[k, :, lanes].astype(jnp.float32) for k in range(2)]
+        send_low[:, lanes] = jnp.concatenate([value[:RIM] for value in values], 0).astype(jnp.bfloat16)
+        send_high[:, lanes] = jnp.concatenate([value[LOW:] for value in values], 0).astype(jnp.bfloat16)
+
+    for_leads(HALF, prepare)
+    from_left = send(send_high, 0, right)
+    from_right = send(send_low, 1, left)
+    high = pl.ds(LOW * SIDE, RIM * SIDE)
+    low = pl.ds(0, RIM * SIDE)
+    send(own.at[:, :, high], 2, above)
+    send(own.at[:, :, low], 3, below)
+    from_left.wait_recv()
+    send(outs[0].at[:, high], 4, above)
+    send(outs[0].at[:, low], 5, below)
+    from_right.wait_recv()
+    send(outs[1].at[:, high], 6, above)
+    send(outs[1].at[:, low], 7, below)
+    for copy in started:
+        copy.wait_send()
+    for copy in started[2:]:
+        copy.wait_recv()
+
+
+def return_kernel(mesh_x, mesh_y, *refs):
+    side_terms = refs[:2]
+    column_terms = refs[2:4]
+    corner_terms = refs[4:8]
+    density, core, core_x, core_y, core_xy = refs[8:13]
+    outs = refs[13:17]
+    potential = refs[17]
+    landed_corners, send_left, send_right, sent, landed = refs[18:]
+    left, right, below, above = greet(mesh_x, mesh_y)
+
+    def send(source, target, slot, device):
+        copy = pltpu.make_async_remote_copy(
+            src_ref=source,
+            dst_ref=target,
+            send_sem=sent.at[slot],
+            recv_sem=landed.at[slot],
+            device_id=device,
+            device_id_type=MESH,
+        )
+        copy.start()
+        return copy
+
+    corners = [
+        send(corner_terms[slot], landed_corners.at[slot], slot, device)
+        for slot, device in enumerate((below, above, below, above))
+    ]
+    others = [
+        send(column_terms[0], outs[2], 4, below),
+        send(column_terms[1], outs[3], 5, above),
+    ]
     slab = core.shape[0]
 
-    def clear(lead):
-        grid[pl.ds(pl.multiple_of(lead * GRID_ROWS, 8), GRID_ROWS), :] = jnp.zeros(
-            (GRID_ROWS, LANES), jnp.float32
-        )
-
-    for_leads(GRID_ROWS, clear)
-
-    def offsets(step_x, step_y, k):
-        holder_x = lax.rem(here_x + step_x + mesh_x, mesh_x)
-        holder_y = lax.rem(here_y + step_y + mesh_y, mesh_y)
-        orbit = (holder_x * mesh_y + holder_y) * 2 + k
-        at_x = anchors[3 * orbit] - holder_x * slab
-        at_y = anchors[3 * orbit + 1] - holder_y * slab
-        return at_x, at_y, anchors[3 * orbit + 2]
-
-    for (step_x, step_y), piece in zip(STEPS, pieces):
-        base, rows, leads = place_of(step_x, step_y)
-        chunk = 2 if rows == SIDE else 4
-        lane = lane_index(rows)
-        for k in range(2):
-            at_x, at_y, at_z = offsets(step_x, step_y, k)
-            row = at_x + step_x * slab + GRID_PAD + (LOW if step_x < 0 else 0)
-            column = at_y + step_y * slab + GRID_PAD + (LOW if step_y < 0 else 0)
-            start = column * GRID_ROWS + row
-            mask = (lane >= at_z) & (lane < at_z + SIDE)
-            turn_low = at_z
-            turn_high = lax.rem(at_z + SIDE, LANES)
-
-            def deposit(index):
-                lead = index * chunk
-                added = []
-                for j in range(chunk):
-                    lanes = pl.ds(pl.multiple_of((lead + j) * LANES, LANES), LANES)
-                    value = piece[k, :, lanes].astype(jnp.float32)
-                    value = value * value
-                    added.append(jnp.where(mask, pltpu.roll(value, turn_low, 1), 0.0))
-                    added.append(jnp.where(mask, pltpu.roll(value, turn_high, 1), 0.0))
-                where_at = [
-                    pl.ds(start + (2 * lead + j) * GRID_ROWS, rows) for j in range(2 * chunk)
-                ]
-                held = [grid[at, :] for at in where_at]
-                for at, old, new in zip(where_at, held, added):
-                    grid[at, :] = old + new
-
-            for_leads(leads // chunk, deposit)
-
     def finish_at(row, column, core_part):
-        at = pl.ds((column + GRID_PAD) * GRID_ROWS + GRID_PAD + row, 8, stride=GRID_ROWS)
-        value = -xc_factor * cube_root(grid[at, :] + core_part)
-        grid[at, :] = value
-        return value
+        at = pl.ds(column * GRID_ROWS + GRID_PAD + row, 8, stride=GRID_ROWS)
+        potential[at, :] = -xc_factor * cube_root(density[at, :] + core_part)
 
     def own_rows(row):
         for column in range(0, slab, 8):
-            value = finish_at(row, column, core[row, pl.ds(column, 8), :])
-            potential[row, pl.ds(column, 8), :] = value
-        above = core_y[row].astype(jnp.float32)
+            finish_at(row, column, core[row, pl.ds(column, 8), :])
+        beyond = core_y[row].astype(jnp.float32)
         for column in range(0, RIM, 8):
-            finish_at(row, slab + column, above[column : column + 8])
-
-    for_leads(slab, own_rows)
+            finish_at(row, slab + column, beyond[column : column + 8])
 
     def rim_rows(row):
         beside = core_x[row].astype(jnp.float32)
         for column in range(0, slab, 8):
             finish_at(slab + row, column, beside[column : column + 8])
-        above = core_xy[row].astype(jnp.float32)
+        beyond = core_xy[row].astype(jnp.float32)
         for column in range(0, RIM, 8):
-            finish_at(slab + row, slab + column, above[column : column + 8])
+            finish_at(slab + row, slab + column, beyond[column : column + 8])
 
     for_leads(RIM, rim_rows)
-
+    for copy in corners:
+        copy.wait_recv()
+
+    for side, target in enumerate((send_left, send_right)):
+        terms = side_terms[side]
+
+        def merge(lead, terms=terms, target=target, corner=None, shift=0):
+            lanes = pl.ds(pl.multiple_of(lead * LANES, LANES), LANES)
+            value = terms[:, lanes]
+            if corner is not None:
+                part = pl.ds(pl.multiple_of((lead - shift) * LANES, LANES), LANES)
+                value = value.astype(jnp.float32) + landed_corners[corner, :, part].astype(jnp.float32)
+            target[:, lanes] = value.astype(jnp.bfloat16)
+
+        for first, last, corner in (
+            (0, RIM_LEADS, 2 * side + 1),
+            (RIM_LEADS, LOW_LEADS, None),
+            (LOW_LEADS, HALF, 2 * side),
+        ):
+
+            def part_step(index, first=first, corner=corner, merge=merge):
+                merge(index + first, corner=corner, shift=first)
+
+            for_leads(last - first, part_step)
+    others.append(send(send_left, outs[0], 6, left))
+    others.append(send(send_right, outs[1], 7, right))
+    for_leads(slab, own_rows)
+    for copy in corners:
+        copy.wait_send()
+    for copy in others:
+        copy.wait()
+
+
+def action_kernel(mesh_x, mesh_y, anchors, own, own_terms, from_right, from_left, from_above, from_below, grid, action, potential):
+    here_x = lax.axis_index("gx")
+    here_y = lax.axis_index("gy")
+    slab = potential.shape[0]
+
+    def copy_rows(row):
+        for column in range(0, slab, 8):
+            at = pl.ds(column * GRID_ROWS + GRID_PAD + row, 8, stride=GRID_ROWS)
+            potential[row, pl.ds(column, 8), :] = grid[at, :]
+
+    for_leads(slab, copy_rows)
     lane = lane_index(SIDE)
+    first = (here_x * mesh_y + here_y) * 2
+    starts, lows, highs = [], [], []
     for k in range(2):
-        at_x, at_y, at_z = offsets(0, 0, k)
-        start = (at_y + GRID_PAD) * GRID_ROWS + at_x + GRID_PAD
-        turn_low = lax.rem(LANES - at_z, LANES)
-        turn_high = lax.rem(LANES + SIDE - at_z, LANES)
-
-        def sample(index):
-            for j in range(2):
-                lead = index * 2 + j
-                lanes = pl.ds(pl.multiple_of(lead * LANES, LANES), LANES)
-                low = grid[pl.ds(start + 2 * lead * GRID_ROWS, SIDE), :]
-                high = grid[pl.ds(start + (2 * lead + 1) * GRID_ROWS, SIDE), :]
-                value = jnp.where(
-                    lane < SIDE, pltpu.roll(low, turn_low, 1), pltpu.roll(high, turn_high, 1)
-                )
-                applied[k, :, lanes] = value * pieces[0][k, :, lanes].astype(jnp.float32)
-
-        for_leads(HALF // 2, sample)
-
-
-def from_behind(block, axis, distance):
-    size = lax.axis_size(axis)
-    return lax.ppermute(block, axis, [((i - distance) % size, i) for i in range(size)])
+        at_x = anchors[3 * (first + k)] - here_x * slab
+        at_y = anchors[3 * (first + k) + 1] - here_y * slab
+        at_z = anchors[3 * (first + k) + 2]
+        starts.append(at_y * GRID_ROWS + at_x + GRID_PAD)
+        lows.append(lax.rem(LANES - at_z, LANES))
+        highs.append(lax.rem(LANES + SIDE - at_z, LANES))
+
+    def apply(lead, column=None, shift=0):
+        lanes = pl.ds(pl.multiple_of(lead * LANES, LANES), LANES)
+        above_rows = from_right[:, lanes].astype(jnp.float32)
+        below_rows = from_left[:, lanes].astype(jnp.float32)
+        for k in range(2):
+            low = grid[pl.ds(starts[k] + 2 * lead * GRID_ROWS, SIDE), :]
+            high = grid[pl.ds(starts[k] + (2 * lead + 1) * GRID_ROWS, SIDE), :]
+            sampled = jnp.where(lane < SIDE, pltpu.roll(low, lows[k], 1), pltpu.roll(high, highs[k], 1))
+            terms = own_terms[pl.ds(pl.multiple_of((k * HALF + lead) * SIDE, SIDE), SIDE), :]
+            if column is not None:
+                part = pl.ds(pl.multiple_of((lead - shift) * LANES, LANES), LANES)
+                terms = terms + column[k, :, part].astype(jnp.float32)
+            rows = slice(k * RIM, (k + 1) * RIM)
+            terms = jnp.concatenate(
+                [terms[:RIM] + below_rows[rows], terms[RIM:LOW], terms[LOW:] + above_rows[rows]], 0
+            )
+            action[k, :, lanes] = sampled * own[k, :, lanes].astype(jnp.float32) - exx_share * terms
+
+    for start, stop, column in ((0, RIM_LEADS, from_below), (RIM_LEADS, LOW_LEADS, None), (LOW_LEADS, HALF, from_above)):
+
+        def part_step(index, start=start, column=column):
+            apply(index + start, column=column, shift=start)
+
+        for_leads(stop - start, part_step)
+
+
+def shape_of(dims, dtype=jnp.bfloat16):
+    return jax.ShapeDtypeStruct(dims, dtype)
 
 
 def local(orbitals, anchors, pair_list, pair_count, core_density):
@@ -486,63 +669,69 @@
     flat_anchors = anchors.reshape(-1)
     flat_pairs = pair_list.reshape(-1)
     flat_count = pair_count.reshape(-1)
-    low_cut = LOW * SIDE
-    rim_cut = RIM * SIDE
-
-    from_left = from_behind(own[:, LOW:], "gx", 1)
-    from_right = from_behind(own[:, :RIM], "gx", -1)
-    from_below = from_behind(own[..., low_cut:], "gy", 1)
-    from_above = from_behind(own[..., :rim_cut], "gy", -1)
-    sides = jnp.stack([from_left, from_right])
-    below_sides = from_behind(sides[..., low_cut:], "gy", 1)
-    above_sides = from_behind(sides[..., :rim_cut], "gy", -1)
-    narrow_core = core_density.astype(jnp.bfloat16)
-    core_x = from_behind(narrow_core[:RIM], "gx", -1)
-    core_y = from_behind(narrow_core[:, :RIM], "gy", -1)
-    core_xy = from_behind(core_x[:, :RIM], "gy", -1)
-    pieces = [
-        own,
-        from_left,
-        from_right,
-        from_below,
-        from_above,
-        below_sides[0],
-        above_sides[0],
-        below_sides[1],
-        above_sides[1],
+    side_shape = shape_of((2 * RIM, FLAT))
+    column_shape = shape_of((2, SIDE, RIM * SIDE))
+    corner_shape = shape_of((2 * RIM, RIM * SIDE))
+    around = [side_shape] * 2 + [column_shape] * 2 + [corner_shape] * 4
+
+    pieces = pl.pallas_call(
+        functools.partial(gather_kernel, mesh_x, mesh_y),
+        out_shape=around,
+        in_specs=[vmem],
+        out_specs=[hbm] * 8,
+        scratch_shapes=[
+            pltpu.VMEM(side_shape.shape, jnp.bfloat16),
+            pltpu.VMEM(side_shape.shape, jnp.bfloat16),
+            pltpu.SemaphoreType.DMA((8,)),
+            pltpu.SemaphoreType.DMA((8,)),
+        ],
+        compiler_params=pltpu.CompilerParams(
+            collective_id=0, has_side_effects=True, vmem_limit_bytes=16 * 1024 * 1024
+        ),
+        name="gather_rims",
+    )(own)
+
+    narrow_x = core_density[:RIM].astype(jnp.bfloat16)
+    narrow_y = core_density[:, :RIM].astype(jnp.bfloat16)
+    narrow_x, narrow_y, corner = lax.optimization_barrier((narrow_x, narrow_y, pieces[7]))
+    pieces = list(pieces[:7]) + [corner]
+    back_x = [((i + 1) % mesh_x, i) for i in range(mesh_x)]
+    back_y = [((i + 1) % mesh_y, i) for i in range(mesh_y)]
+    back_xy = [
+        ((i + 1) % mesh_x * mesh_y + (j + 1) % mesh_y, i * mesh_y + j)
+        for i in range(mesh_x)
+        for j in range(mesh_y)
     ]
-    terms = pairs_call(mesh_x, mesh_y, flat_anchors, flat_pairs, flat_count, pieces)
-
-    applied, potential = pl.pallas_call(
-        functools.partial(grid_kernel, mesh_x, mesh_y),
-        out_shape=[
-            jax.ShapeDtypeStruct(own.shape, jnp.float32),
-            jax.ShapeDtypeStruct(core_density.shape, jnp.float32),
+    core_x = lax.ppermute(narrow_x, "gx", back_x)
+    core_y = lax.ppermute(narrow_y, "gy", back_y)
+    core_xy = lax.ppermute(narrow_x[:, :RIM], ("gx", "gy"), back_xy)
+
+    terms = pairs_call(mesh_x, mesh_y, flat_anchors, flat_pairs, flat_count, [own] + pieces)
+    returned = pl.pallas_call(
+        functools.partial(return_kernel, mesh_x, mesh_y),
+        out_shape=[side_shape] * 2 + [column_shape] * 2 + [shape_of((EDGE_ROWS, LANES), jnp.float32)],
+        in_specs=[vmem] * 2 + [hbm] * 6 + [vmem] * 5,
+        out_specs=[hbm] * 4 + [vmem],
+        scratch_shapes=[
+            pltpu.VMEM((4,) + corner_shape.shape, jnp.bfloat16),
+            pltpu.VMEM(side_shape.shape, jnp.bfloat16),
+            pltpu.VMEM(side_shape.shape, jnp.bfloat16),
+            pltpu.SemaphoreType.DMA((8,)),
+            pltpu.SemaphoreType.DMA((8,)),
         ],
-        in_specs=[smem] + [vmem] * 13,
+        compiler_params=pltpu.CompilerParams(
+            collective_id=1, has_side_effects=True, vmem_limit_bytes=32 * 1024 * 1024
+        ),
+        name="return_terms",
+    )(*terms[2:], terms[1], core_density, core_x, core_y, core_xy)
+    action, potential = pl.pallas_call(
+        functools.partial(action_kernel, mesh_x, mesh_y),
+        out_shape=[shape_of(own.shape, jnp.float32), shape_of(core_density.shape, jnp.float32)],
+        in_specs=[smem] + [vmem] * 7,
         out_specs=[vmem] * 2,
-        scratch_shapes=[pltpu.VMEM((GRID_ROWS * GRID_ROWS, LANES), jnp.float32)],
-        compiler_params=pltpu.CompilerParams(vmem_limit_bytes=56 * 1024 * 1024),
-        cost_estimate=pl.CostEstimate(flops=20_000_000, bytes_accessed=8_000_000, transcendentals=0),
-        name="grid_terms",
-    )(flat_anchors, *pieces, core_density, core_x, core_y, core_xy)
-
-    below_left, above_left, below_right, above_right = terms[5:]
-    back_below = from_behind(terms[3], "gy", -1)
-    back_above = from_behind(terms[4], "gy", 1)
-    back_below_sides = from_behind(jnp.stack([below_left, below_right]), "gy", -1).astype(jnp.float32)
-    back_above_sides = from_behind(jnp.stack([above_left, above_right]), "gy", 1).astype(jnp.float32)
-    side_terms = jnp.stack([terms[1], terms[2]]).astype(jnp.float32)
-    side_terms = side_terms.at[..., low_cut:].add(back_below_sides)
-    side_terms = side_terms.at[..., :rim_cut].add(back_above_sides).astype(jnp.bfloat16)
-    back_left = from_behind(side_terms[0], "gx", -1)
-    back_right = from_behind(side_terms[1], "gx", 1)
-    exchange = terms[0]
-    exchange = exchange.at[..., low_cut:].add(back_below.astype(jnp.float32))
-    exchange = exchange.at[..., :rim_cut].add(back_above.astype(jnp.float32))
-    exchange = exchange.at[:, LOW:].add(back_left.astype(jnp.float32))
-    exchange = exchange.at[:, :RIM].add(back_right.astype(jnp.float32))
-    action = applied - exx_share * exchange
+        compiler_params=pltpu.CompilerParams(vmem_limit_bytes=32 * 1024 * 1024),
+        name="action_terms",
+    )(flat_anchors, own, terms[0], *returned)
     return (action.reshape(orbitals.shape), potential)
 
 

time: 111 us -> 113 us (1.018)
  the two profiles are of different devices: /device:TPU:25 before, /device:TPU:34 now
where the time goes in v3:
time: 113 us
  Pallas kernels  82.4 us (73%)
  local copies, waits for them, and re-layouts  17 us (15%)
  starting transfers between devices  10.6 us (9%)
  between operations  1.46 us (1%)
  other arithmetic  1.43 us (1%)
    pallas_call x1, Pallas kernels, local(): pl.pallas_call(functools.partial(return_kernel, mesh_x, mesh_y), out_shap...  32.9 us
    pallas_call x1, Pallas kernels, local(): pl.pallas_call(functools.partial(gather_kernel, mesh_x, mesh_y), out_shap...  22.4 us
    pallas_call x1, Pallas kernels, pairs_call(): pl.pallas_call(functools.partial(pair_kernel, mesh_x, mesh_y), out_shape=...  21 us
    unnamed x50, local copies, waits for them, and re-layouts  15.5 us
    ppermute x1, starting transfers between devices, local(): core_x = lax.ppermute(narrow_x, 'gx', back_x)  6.8 us
    pallas_call x1, Pallas kernels, local(): pl.pallas_call(functools.partial(action_kernel, mesh_x, mesh_y), out_shap...  6.06 us
  transfers between devices with their start and end apart: 3, of which 0 were waited for; matrix products, arithmetic and copies ran while one was open for 1% of the time, Pallas kernels for 19%

profile of v3, /device:TPU:34, one launch (start us, length us, event | category | flops | bytes accessed | tf_op | source)
XLA Modules:
  0.0 112.8 jit_solution(972725169327152899)
XLA Ops:
  0.7 1.4 %convert.4 = bf16[48,48,128]{2,1,0:T(8,128)(2,1)S(1)} convert(f32[48,48,128]{2,1,0:T(8,128)} %refs_9_.1) | non-fusion elementwise | flops 294912 | bytes 1769472 | tf_op jit(solution)/shard_map/convert.1
  2.2 22.4 %gather_rims.1 = (bf16[48,4096]{1,0:T(8,128)(2,1)S(1)}, bf16[48,4096]{1,0:T(8,128)(2,1)S(1)}, bf16[2,64,1536]{2,1,0:T(8,128)(2,1)S(1)}, bf16[2,64,1536]{2,1,0:T(...) custom-call(bf16[2,64,4096]{2,1,0:T(8,128)(2,1)S(1)} %bitcast.5), custom_call_target="tpu_custom_call" | custom-call | tf_op jit(solution)/shard_map/gather_rims/pallas_call | solution.py:677
  24.7 0.7 copy-done.5
  25.4 0.8 copy-done.6
  26.2 0.8 copy-done.7
  26.9 0.7 copy-done.8
  28.3 0.7 copy-done.14
  29.0 0.7 copy-done.15
  30.3 1.9 %collective-permute-start.1 = (bf16[48,24,128]{2,1,0:T(8,128)(2,1)S(1)}, bf16[48,24,128]{2,1,0:T(8,128)(2,1)S(1)}, u32[]{:S(2)}, u32[]{:S(2)}) collective-permute-start(bf16[48,24,128]{2,1,0:T(8,128)(2,1)S(1)} %slice.15), channel_id=1, source_target_pairs={{1,0},{2,1},{3,2},{4,3},{5,4},{6,5},{7,6},{8,7},{9,8},{10,9},{11,1... | collective-permute-start | bytes 884744 | tf_op jit(solution)/shard_map/ppermute | solution.py:706
  32.2 6.8 %collective-permute-start = (bf16[24,48,128]{2,1,0:T(8,128)(2,1)S(1)}, bf16[24,48,128]{2,1,0:T(8,128)(2,1)S(1)}, u32[]{:S(2)}, u32[]{:S(2)}) collective-permute-start(bf16[24,48,128]{2,1,0:T(8,128)(2,1)S(1)} %slice.14), channel_id=1, source_target_pairs={{16,0},{32,16},{48,32},{64,48},{80,64},{96,80},{112,96},{0,112},{1... | collective-permute-start | bytes 884744 | tf_op jit(solution)/shard_map/ppermute | solution.py:705
  39.0 1.9 %collective-permute-start.2 = (bf16[24,24,128]{2,1,0:T(8,128)(2,1)S(1)}, bf16[24,24,128]{2,1,0:T(8,128)(2,1)S(1)}, u32[]{:S(2)}, u32[]{:S(2)}) collective-permute-start(bf16[24,24,128]{2,1,0:T(8,128)(2,1)S(1)} %slice.13), channel_id=1, source_target_pairs={{17,0},{18,1},{19,2},{20,3},{21,4},{22,5},{23,6},{24,7},{25,8},{26... | collective-permute-start | bytes 442376 | tf_op jit(solution)/shard_map/ppermute | solution.py:707
  42.5 0.8 reshape.16.anchors
  43.3 21.0 %pair_terms.1 = (f32[4096,128]{1,0:T(8,128)}, f32[6424,128]{1,0:T(8,128)}, bf16[48,4096]{1,0:T(8,128)(2,1)}, bf16[48,4096]{1,0:T(8,128)(2,1)}, bf16[2,64,1536]{2...) custom-call(s32[768]{0:T(1024)} %reshape.16.anchors, ...), custom_call_target="tpu_custom_call" | custom-call | flops 40000000 | bytes 8000000 | tf_op jit(solution)/shard_map/pair_terms/pallas_call | solution.py:435
  64.3 1.9 %copy-done.3 = f32[6424,128]{1,0:T(8,128)S(1)} copy-done((f32[6424,128]{1,0:T(8,128)S(1)}, f32[6424,128]{1,0:T(8,128)}, u32[]{:S(2)}) %copy-start.3) | copy-done | bytes 3289112
  66.3 1.0 copy-done.9
  67.2 1.0 copy-done.10
  68.2 1.0 copy-done.11
  69.2 1.0 copy-done.12
  70.2 0.9 copy-done.17
  71.1 0.9 copy-done.18
  72.1 0.9 copy-done.19
  73.0 0.9 copy-done.20
  73.9 32.9 %return_terms.1 = (bf16[48,4096]{1,0:T(8,128)(2,1)S(1)}, bf16[48,4096]{1,0:T(8,128)(2,1)S(1)}, bf16[2,64,1536]{2,1,0:T(8,128)(2,1)S(1)}, bf16[2,64,1536]{2,1,0:T(8,128)(2,1)S(1)}, f32[6424,128]{1,0:T(8,128)S(1)}) custom-call(bf16[48,4096]{1,0:T(8,128)(2,1)S(1)} %copy-done.9, bf16[48,4096]{1,0:T(8,128)(2,1)S(1)} %copy-done.10, ...), custom_call_target="tpu_custom_call" | custom-call | tf_op jit(solution)/shard_map/return_terms/pallas_call | solution.py:710
  106.8 6.1 %action_terms.1 = (f32[2,64,4096]{2,1,0:T(8,128)}, f32[48,48,128]{2,1,0:T(8,128)}) custom-call(s32[768]{0:T(1024)S(1)} %copy-done.21, bf16[2,64,4096]{2,1,0:T(8,128)(2,1)S(1)} %bitcast.6, f32[4096,128]{1,0:T(8,128)S(1)} %copy-done.4, bf16[48,4096]{1,0:T(8,128)(2,1)S(1)} %get-tuple-element.51.from_right, bf16[48,4096]{1,0:T(8,128)(2,1)S(1)} %get-tuple-element.52.from_left, ...), custom_call_target="tpu_custom_call" | custom-call | tf_op jit(solution)/shard_map/action_terms/pallas_call | solution.py:727
  (42 shorter events, 2.3 us)
Async XLA Ops:
  0.6 1.6 %copy-start = (bf16[1,1,2,64,4096]{4,3,2,1,0:T(8,128)(2,1)S(1)}, bf16[1,1,2,64,4096]{4,3,2,1,0:T(8,128)(2,1)}, u32[]{:S(2)}) copy-start(bf16[1,1,2,64,4096]{4,3,2,1,0:T(8,128)(2,1)} %param.5) | copy-start | bytes 3145732
  0.6 40.9 %copy-start.23 = (s32[1,1,12,2]{2,3,1,0:T(2,128)S(1)}, s32[1,1,12,2]{2,3,1,0:T(2,128)}, u32[]{:S(2)}) copy-start(s32[1,1,12,2]{2,3,1,0:T(2,128)} %param.7) | copy-start | bytes 292
  0.7 41.7 %copy-start.22 = (s32[256,3]{0,1:T(4,128)S(1)}, s32[256,3]{0,1:T(4,128)}, u32[]{:S(2)}) copy-start(s32[256,3]{0,1:T(4,128)} %param.6) | copy-start | bytes 9220
  24.7 0.7 copy-start.5
  25.4 0.8 copy-start.6
  26.2 0.8 copy-start.7
  26.9 0.7 copy-start.8
  29.0 0.7 copy-start.15
  30.3 34.0 %copy-start.2 = (f32[48,48,128]{2,1,0:T(8,128)S(1)}, f32[48,48,128]{2,1,0:T(8,128)}, u32[]{:S(2)}) copy-start(f32[48,48,128]{2,1,0:T(8,128)} %refs_9_.1) | copy-start | bytes 3538948
  30.3 34.0 %collective-permute-start.1 = (bf16[48,24,128]{2,1,0:T(8,128)(2,1)S(1)}, bf16[48,24,128]{2,1,0:T(8,128)(2,1)S(1)}, u32[]{:S(2)}, u32[]{:S(2)}) collective-permute-start(bf16[48,24,128]{2,1,0:T(8,128)(2,1)S(1)} %slice.15), channel_id=1, source_target_pairs={{1,0},{2,1},{3,2},{4,3},{5,4},{6,5},{7,6},{8,7},{9,8},{10,9},{11,1... | collective-permute-start | bytes 884744 | tf_op jit(solution)/shard_map/ppermute | solution.py:706
  32.2 32.1 %collective-permute-start = (bf16[24,48,128]{2,1,0:T(8,128)(2,1)S(1)}, bf16[24,48,128]{2,1,0:T(8,128)(2,1)S(1)}, u32[]{:S(2)}, u32[]{:S(2)}) collective-permute-start(bf16[24,48,128]{2,1,0:T(8,128)(2,1)S(1)} %slice.14), channel_id=1, source_target_pairs={{16,0},{32,16},{48,32},{64,48},{80,64},{96,80},{112,96},{0,112},{1... | collective-permute-start | bytes 884744 | tf_op jit(solution)/shard_map/ppermute | solution.py:705
  39.0 25.3 %collective-permute-start.2 = (bf16[24,24,128]{2,1,0:T(8,128)(2,1)S(1)}, bf16[24,24,128]{2,1,0:T(8,128)(2,1)S(1)}, u32[]{:S(2)}, u32[]{:S(2)}) collective-permute-start(bf16[24,24,128]{2,1,0:T(8,128)(2,1)S(1)} %slice.13), channel_id=1, source_target_pairs={{17,0},{18,1},{19,2},{20,3},{21,4},{22,5},{23,6},{24,7},{25,8},{26... | collective-permute-start | bytes 442376 | tf_op jit(solution)/shard_map/ppermute | solution.py:707
  64.3 1.9 %copy-start.3 = (f32[6424,128]{1,0:T(8,128)S(1)}, f32[6424,128]{1,0:T(8,128)}, u32[]{:S(2)}) copy-start(f32[6424,128]{1,0:T(8,128)} %get-tuple-element.48.refs_8_) | copy-start | bytes 9867268
  66.3 1.0 copy-start.9
  67.2 1.0 copy-start.10
  68.2 1.0 copy-start.11
  69.2 1.0 copy-start.12
  70.2 0.9 copy-start.17
  71.1 0.9 copy-start.18
  72.1 0.9 copy-start.19
  73.0 0.9 copy-start.20
  73.9 32.9 %copy-start.1 = (bf16[1,1,2,64,4096]{4,3,2,1,0:T(8,128)(2,1)S(1)}, bf16[1,1,2,64,4096]{4,3,2,1,0:T(8,128)(2,1)}, u32[]{:S(2)}) copy-start(bf16[1,1,2,64,4096]{4,3,2,1,0:T(8,128)(2,1)} %param.5) | copy-start | bytes 3145732
  73.9 32.9 %copy-start.4 = (f32[4096,128]{1,0:T(8,128)S(1)}, f32[4096,128]{1,0:T(8,128)}, u32[]{:S(2)}) copy-start(f32[4096,128]{1,0:T(8,128)} %get-tuple-element.39.own_terms) | copy-start | bytes 6291460
  73.9 32.9 %copy-start.21 = (s32[768]{0:T(1024)S(1)}, s32[768]{0:T(1024)}, u32[]{:S(2)}) copy-start(s32[768]{0:T(1024)} %reshape.16.anchors) | copy-start | bytes 9220
  (3 other events, 2.0 us)

commit v4 on v3

--- a/solution.py
+++ b/solution.py
@@ -154,16 +154,16 @@
     total_scale = coupling * scale[0] * scale[1] * scale[2] * scale[3]
 
     def pair_step(slot, carry):
-        first = pairs[2 * slot]
-        second = pairs[2 * slot + 1]
+        first = pairs[0, slot]
+        second = pairs[1, slot]
         first_k = lax.rem(first, 2)
         second_k = lax.rem(second, 2)
         holder = lax.div(second, 2)
         step_x = lax.rem(lax.div(holder, mesh_y) - here_x + 1 + mesh_x, mesh_x) - 1
         step_y = lax.rem(lax.rem(holder, mesh_y) - here_y + 1 + mesh_y, mesh_y) - 1
-        shift_x = anchors[3 * second] - anchors[3 * first]
-        shift_y = anchors[3 * second + 1] - anchors[3 * first + 1]
-        shift_z = anchors[3 * second + 2] - anchors[3 * first + 2]
+        shift_x = anchors[0, second] - anchors[0, first]
+        shift_y = anchors[1, second] - anchors[1, first]
+        shift_z = anchors[2, second] - anchors[2, first]
         shift_x = shift_x + jnp.where(shift_x < -(span_x // 2), span_x, 0) - jnp.where(
             shift_x >= span_x // 2, span_x, 0
         )
@@ -355,9 +355,9 @@
         holder_x = lax.rem(here_x + step_x + mesh_x, mesh_x)
         holder_y = lax.rem(here_y + step_y + mesh_y, mesh_y)
         orbit = (holder_x * mesh_y + holder_y) * 2 + k
-        at_x = anchors[3 * orbit] - holder_x * slab
-        at_y = anchors[3 * orbit + 1] - holder_y * slab
-        at_z = anchors[3 * orbit + 2]
+        at_x = anchors[0, orbit] - holder_x * slab
+        at_y = anchors[1, orbit] - holder_y * slab
+        at_z = anchors[2, orbit]
         row = at_x + step_x * slab + GRID_PAD + jnp.where(step_x < 0, LOW, 0)
         column = at_y + step_y * slab + GRID_PAD + jnp.where(step_y < 0, LOW, 0)
         start = column * GRID_ROWS + row
@@ -467,7 +467,7 @@
     return value * inverse * inverse
 
 
-def greet(mesh_x, mesh_y):
+def greet(mesh_x, mesh_y, diagonal=False):
     here_x = lax.axis_index("gx")
     here_y = lax.axis_index("gy")
     left = (lax.rem(here_x + mesh_x - 1, mesh_x), here_y)
@@ -475,9 +475,12 @@
     below = (here_x, lax.rem(here_y + mesh_y - 1, mesh_y))
     above = (here_x, lax.rem(here_y + 1, mesh_y))
     barrier = pltpu.get_barrier_semaphore()
-    for neighbour in (left, right, below, above):
+    neighbours = [left, right, below, above]
+    if diagonal:
+        neighbours += [(left[0], below[1]), (right[0], above[1])]
+    for neighbour in neighbours:
         pl.semaphore_signal(barrier, inc=1, device_id=neighbour, device_id_type=MESH)
-    pl.semaphore_wait(barrier, 4)
+    pl.semaphore_wait(barrier, len(neighbours))
     return left, right, below, above
 
 
@@ -529,11 +532,11 @@
     side_terms = refs[:2]
     column_terms = refs[2:4]
     corner_terms = refs[4:8]
-    density, core, core_x, core_y, core_xy = refs[8:13]
-    outs = refs[13:17]
-    potential = refs[17]
-    landed_corners, send_left, send_right, sent, landed = refs[18:]
-    left, right, below, above = greet(mesh_x, mesh_y)
+    density, core = refs[8:10]
+    outs = refs[10:14]
+    potential = refs[14]
+    landed_corners, send_left, send_right, narrow_x, narrow_y, core_x, core_y, core_xy, sent, landed = refs[15:]
+    left, right, below, above = greet(mesh_x, mesh_y, diagonal=True)
 
     def send(source, target, slot, device):
         copy = pltpu.make_async_remote_copy(
@@ -557,6 +560,13 @@
     ]
     slab = core.shape[0]
 
+    def narrow(row):
+        narrow_x[row] = core[row].astype(jnp.bfloat16)
+        narrow_y[row] = jnp.concatenate([core[2 * row, :RIM], core[2 * row + 1, :RIM]], 0).astype(jnp.bfloat16)
+
+    for_leads(RIM, narrow)
+    from_right = send(narrow_x, core_x, 8, left)
+
     def finish_at(row, column, core_part):
         at = pl.ds(column * GRID_ROWS + GRID_PAD + row, 8, stride=GRID_ROWS)
         potential[at, :] = -xc_factor * cube_root(density[at, :] + core_part)
@@ -564,19 +574,22 @@
     def own_rows(row):
         for column in range(0, slab, 8):
             finish_at(row, column, core[row, pl.ds(column, 8), :])
-        beyond = core_y[row].astype(jnp.float32)
-        for column in range(0, RIM, 8):
-            finish_at(row, slab + column, beyond[column : column + 8])
-
-    def rim_rows(row):
+
+    def right_rows(row):
         beside = core_x[row].astype(jnp.float32)
         for column in range(0, slab, 8):
             finish_at(slab + row, column, beside[column : column + 8])
-        beyond = core_xy[row].astype(jnp.float32)
-        for column in range(0, RIM, 8):
-            finish_at(slab + row, slab + column, beyond[column : column + 8])
-
-    for_leads(RIM, rim_rows)
+
+    def above_rows(pair, source=core_y, beyond=0):
+        part = source[pair].astype(jnp.float32)
+        for j in range(2):
+            for column in range(0, RIM, 8):
+                start = j * RIM + column
+                finish_at(beyond + 2 * pair + j, slab + column, part[start : start + 8])
+
+    def corner_rows(pair):
+        above_rows(pair, source=core_xy, beyond=slab)
+
     for copy in corners:
         copy.wait_recv()
 
@@ -603,7 +616,15 @@
             for_leads(last - first, part_step)
     others.append(send(send_left, outs[0], 6, left))
     others.append(send(send_right, outs[1], 7, right))
+    from_above = send(narrow_y, core_y, 9, below)
+    from_corner = send(narrow_y.at[pl.ds(0, RIM // 2)], core_xy, 10, (left[0], below[1]))
     for_leads(slab, own_rows)
+    from_right.wait()
+    for_leads(RIM, right_rows)
+    from_above.wait()
+    for_leads(slab // 2, above_rows)
+    from_corner.wait()
+    for_leads(RIM // 2, corner_rows)
     for copy in corners:
         copy.wait_send()
     for copy in others:
@@ -625,9 +646,9 @@
     first = (here_x * mesh_y + here_y) * 2
     starts, lows, highs = [], [], []
     for k in range(2):
-        at_x = anchors[3 * (first + k)] - here_x * slab
-        at_y = anchors[3 * (first + k) + 1] - here_y * slab
-        at_z = anchors[3 * (first + k) + 2]
+        at_x = anchors[0, first + k] - here_x * slab
+        at_y = anchors[1, first + k] - here_y * slab
+        at_z = anchors[2, first + k]
         starts.append(at_y * GRID_ROWS + at_x + GRID_PAD)
         lows.append(lax.rem(LANES - at_z, LANES))
         highs.append(lax.rem(LANES + SIDE - at_z, LANES))
@@ -666,8 +687,8 @@
     mesh_x = lax.axis_size("gx")
     mesh_y = lax.axis_size("gy")
     own = orbitals[0, 0]
-    flat_anchors = anchors.reshape(-1)
-    flat_pairs = pair_list.reshape(-1)
+    flat_anchors = anchors.T
+    flat_pairs = pair_list[0, 0].T
     flat_count = pair_count.reshape(-1)
     side_shape = shape_of((2 * RIM, FLAT))
     column_shape = shape_of((2, SIDE, RIM * SIDE))
@@ -686,50 +707,40 @@
             pltpu.SemaphoreType.DMA((8,)),
         ],
         compiler_params=pltpu.CompilerParams(
-            collective_id=0, has_side_effects=True, vmem_limit_bytes=16 * 1024 * 1024
+            collective_id=0, has_side_effects=True, vmem_limit_bytes=56 * 1024 * 1024
         ),
         name="gather_rims",
     )(own)
 
-    narrow_x = core_density[:RIM].astype(jnp.bfloat16)
-    narrow_y = core_density[:, :RIM].astype(jnp.bfloat16)
-    narrow_x, narrow_y, corner = lax.optimization_barrier((narrow_x, narrow_y, pieces[7]))
-    pieces = list(pieces[:7]) + [corner]
-    back_x = [((i + 1) % mesh_x, i) for i in range(mesh_x)]
-    back_y = [((i + 1) % mesh_y, i) for i in range(mesh_y)]
-    back_xy = [
-        ((i + 1) % mesh_x * mesh_y + (j + 1) % mesh_y, i * mesh_y + j)
-        for i in range(mesh_x)
-        for j in range(mesh_y)
-    ]
-    core_x = lax.ppermute(narrow_x, "gx", back_x)
-    core_y = lax.ppermute(narrow_y, "gy", back_y)
-    core_xy = lax.ppermute(narrow_x[:, :RIM], ("gx", "gy"), back_xy)
-
-    terms = pairs_call(mesh_x, mesh_y, flat_anchors, flat_pairs, flat_count, [own] + pieces)
+    terms = pairs_call(mesh_x, mesh_y, flat_anchors, flat_pairs, flat_count, [own] + list(pieces))
     returned = pl.pallas_call(
         functools.partial(return_kernel, mesh_x, mesh_y),
         out_shape=[side_shape] * 2 + [column_shape] * 2 + [shape_of((EDGE_ROWS, LANES), jnp.float32)],
-        in_specs=[vmem] * 2 + [hbm] * 6 + [vmem] * 5,
+        in_specs=[vmem] * 2 + [hbm] * 6 + [vmem] * 2,
         out_specs=[hbm] * 4 + [vmem],
         scratch_shapes=[
             pltpu.VMEM((4,) + corner_shape.shape, jnp.bfloat16),
             pltpu.VMEM(side_shape.shape, jnp.bfloat16),
             pltpu.VMEM(side_shape.shape, jnp.bfloat16),
-            pltpu.SemaphoreType.DMA((8,)),
-            pltpu.SemaphoreType.DMA((8,)),
+            pltpu.VMEM((RIM, SIDE - 16, LANES), jnp.bfloat16),
+            pltpu.VMEM((RIM, 2 * RIM, LANES), jnp.bfloat16),
+            pltpu.VMEM((RIM, SIDE - 16, LANES), jnp.bfloat16),
+            pltpu.VMEM((RIM, 2 * RIM, LANES), jnp.bfloat16),
+            pltpu.VMEM((RIM // 2, 2 * RIM, LANES), jnp.bfloat16),
+            pltpu.SemaphoreType.DMA((11,)),
+            pltpu.SemaphoreType.DMA((11,)),
         ],
         compiler_params=pltpu.CompilerParams(
-            collective_id=1, has_side_effects=True, vmem_limit_bytes=32 * 1024 * 1024
+            collective_id=1, has_side_effects=True, vmem_limit_bytes=56 * 1024 * 1024
         ),
         name="return_terms",
-    )(*terms[2:], terms[1], core_density, core_x, core_y, core_xy)
+    )(*terms[2:], terms[1], core_density)
     action, potential = pl.pallas_call(
         functools.partial(action_kernel, mesh_x, mesh_y),
         out_shape=[shape_of(own.shape, jnp.float32), shape_of(core_density.shape, jnp.float32)],
         in_specs=[smem] + [vmem] * 7,
         out_specs=[vmem] * 2,
-        compiler_params=pltpu.CompilerParams(vmem_limit_bytes=32 * 1024 * 1024),
+        compiler_params=pltpu.CompilerParams(vmem_limit_bytes=56 * 1024 * 1024),
         name="action_terms",
     )(flat_anchors, own, terms[0], *returned)
     return (action.reshape(orbitals.shape), potential)

time: 113 us -> 113 us (level)
  the two profiles are of different devices: /device:TPU:34 before, /device:TPU:5 now
where the time goes in v4:
time: 113 us
  Pallas kernels  112 us (99%)
  between operations  1.3 us (1%)
    pallas_call x1, Pallas kernels, local(): pl.pallas_call(functools.partial(return_kernel, mesh_x, mesh_y), out_shap...  58.1 us
    pallas_call x1, Pallas kernels, local(): pl.pallas_call(functools.partial(gather_kernel, mesh_x, mesh_y), out_shap...  23 us
    pallas_call x1, Pallas kernels, pairs_call(): pl.pallas_call(functools.partial(pair_kernel, mesh_x, mesh_y), out_shape=...  22 us
    pallas_call x1, Pallas kernels, local(): pl.pallas_call(functools.partial(action_kernel, mesh_x, mesh_y), out_shap...  8.78 us

profile of v4, /device:TPU:5, one launch (start us, length us, event | category | flops | bytes accessed | tf_op | source)
XLA Modules:
  0.0 113.1 jit_solution(863771493533483298)
XLA Ops:
  1.3 23.0 %gather_rims.1 = (bf16[48,4096]{1,0:T(8,128)(2,1)}, bf16[48,4096]{1,0:T(8,128)(2,1)}, bf16[2,64,1536]{2,1,0:T(8,128)(2,1)}, bf16[2,64,1536]{2,1,0:T(8,128)(2,1)}...) custom-call(bf16[2,64,4096]{2,1,0:T(8,128)(2,1)} %bitcast.8), custom_call_target="tpu_custom_call" | custom-call | tf_op jit(solution)/shard_map/gather_rims/pallas_call | solution.py:698
  24.2 22.0 %pair_terms.1 = (f32[4096,128]{1,0:T(8,128)}, f32[6424,128]{1,0:T(8,128)}, bf16[48,4096]{1,0:T(8,128)(2,1)}, bf16[48,4096]{1,0:T(8,128)(2,1)}, bf16[2,64,1536]{2...) custom-call(s32[3,256]{1,0:T(4,128)} %bitcast.11, ...), custom_call_target="tpu_custom_call" | custom-call | flops 40000000 | bytes 8000000 | tf_op jit(solution)/shard_map/pair_terms/pallas_call | solution.py:435
  46.2 58.1 %return_terms.1 = (bf16[48,4096]{1,0:T(8,128)(2,1)}, bf16[48,4096]{1,0:T(8,128)(2,1)}, bf16[2,64,1536]{2,1,0:T(8,128)(2,1)}, bf16[2,64,1536]{2,1,0:T(8,128)(2,1)}, f32[6424,128]{1,0:T(8,128)}) custom-call(bf16[48,4096]{1,0:T(8,128)(2,1)} %get-tuple-element.36.refs_0_, bf16[48,4096]{1,0:T(8,128)(2,1)} %get-tuple-element.37.refs_1_, ...), custom_call_target="tpu_custom_call" | custom-call | tf_op jit(solution)/shard_map/return_terms/pallas_call | solution.py:716
  104.3 8.8 %action_terms.1 = (f32[2,64,4096]{2,1,0:T(8,128)}, f32[48,48,128]{2,1,0:T(8,128)}) custom-call(s32[3,256]{1,0:T(4,128)} %bitcast.12, bf16[2,64,4096]{2,1,0:T(8,128)(2,1)} %bitcast.10, f32[4096,128]{1,0:T(8,128)} %get-tuple-element.35.own_terms, bf16[48,4096]{1,0:T(8,128)(2,1)} %get-tuple-element.45.from_right, bf16[48,4096]{1,0:T(8,128)(2,1)} %get-tuple-element.46.from_left, ...), custom_call_target="tpu_custom_call" | custom-call | tf_op jit(solution)/shard_map/action_terms/pallas_call | solution.py:738

commit v5 on v4

--- a/solution.py
+++ b/solution.py
@@ -72,9 +72,9 @@
 
 
 def pair_kernel(mesh_x, mesh_y, anchors, pairs, count, *refs):
-    pieces = refs[:9]
+    sources = refs[:9]
     own_out, grid_out = refs[9:11]
-    outs = refs[11:19]
+    targets_out = refs[11:19]
     (
         window,
         sums,
@@ -92,13 +92,59 @@
         grid,
         place,
         copies,
-    ) = refs[19:]
+    ) = refs[19:35]
+    pieces = refs[35:44]
+    outs = refs[44:52]
     here_x = lax.axis_index("gx")
     here_y = lax.axis_index("gy")
     span_x = mesh_x * (SIDE - 16)
     span_y = mesh_y * (SIDE - 16)
 
-    for (step_x, step_y), piece in zip(STEPS, pieces):
+    incoming = [
+        pltpu.make_async_copy(source, piece, copies.at[2 + index])
+        for index, (source, piece) in enumerate(zip(sources, pieces))
+    ]
+    for copy in incoming:
+        copy.start()
+    zeros64 = jnp.zeros((SIDE, LANES), jnp.float32)
+
+    def clear_sums(lead):
+        sums[pl.ds(pl.multiple_of(lead * SIDE, SIDE), SIDE), :] = zeros64
+
+    for_leads((WINDOW_ROWS + 2 * PAD) // SIDE, clear_sums)
+
+    def clear_ends(lead):
+        for start in (0, PAD + WINDOW_ROWS):
+            window[pl.ds(pl.multiple_of(start + lead * SIDE, SIDE), SIDE), :] = zeros64
+
+    for_leads(PAD // SIDE, clear_ends)
+
+    for field in (source3, even3, odd3, source8, even8, odd8):
+        rows = field.shape[1]
+        field[0] = jnp.zeros((rows, LANES), jnp.float32)
+
+        def clear_edge(lead, field=field, rows=rows):
+            edge = jnp.zeros((8, LANES), jnp.float32)
+            field[lead, pl.ds(0, 8), :] = edge
+            field[lead, pl.ds(rows - 8, 8), :] = edge
+
+        for_leads(HALF + 2, clear_edge)
+
+    from_lane = lax.broadcasted_iota(jnp.int32, (LANES, LANES), 0)
+    to_lane = lax.broadcasted_iota(jnp.int32, (LANES, LANES), 1)
+    swap = jnp.abs(to_lane - from_lane) == SIDE
+    step = (jnp.abs(to_lane - from_lane) == 1) & ((to_lane < SIDE) == (from_lane < SIDE))
+    for start in (0, LANES):
+        near[start : start + LANES, :LANES] = one_where(step | swap)
+        near[start : start + LANES, LANES:] = one_where(swap)
+
+    def clear_grid(lead):
+        start = pl.multiple_of(lead * GRID_ROWS, 8)
+        grid[pl.ds(start, GRID_ROWS), :] = jnp.zeros((GRID_ROWS, LANES), jnp.float32)
+
+    for_leads(GRID_ROWS, clear_grid)
+
+    for (step_x, step_y), piece, copy in zip(STEPS, pieces, incoming):
         base, rows, leads = place_of(step_x, step_y)
 
         def widen(lead, base=base, rows=rows, leads=leads, piece=piece):
@@ -113,39 +159,8 @@
                     value = piece[k, :, lanes].astype(jnp.float32)
                 window[pl.ds(start, rows), :] = value
 
+        copy.wait()
         for_leads(leads, widen)
-
-    zeros64 = jnp.zeros((SIDE, LANES), jnp.float32)
-
-    def clear_sums(lead):
-        sums[pl.ds(pl.multiple_of(lead * SIDE, SIDE), SIDE), :] = zeros64
-
-    for_leads((WINDOW_ROWS + 2 * PAD) // SIDE, clear_sums)
-
-    def clear_ends(lead):
-        for start in (0, PAD + WINDOW_ROWS):
-            window[pl.ds(pl.multiple_of(start + lead * SIDE, SIDE), SIDE), :] = zeros64
-
-    for_leads(PAD // SIDE, clear_ends)
-
-    for field in (source3, even3, odd3, source8, even8, odd8):
-        rows = field.shape[1]
-        field[0] = jnp.zeros((rows, LANES), jnp.float32)
-
-        def clear_edge(lead, field=field, rows=rows):
-            edge = jnp.zeros((8, LANES), jnp.float32)
-            field[lead, pl.ds(0, 8), :] = edge
-            field[lead, pl.ds(rows - 8, 8), :] = edge
-
-        for_leads(HALF + 2, clear_edge)
-
-    from_lane = lax.broadcasted_iota(jnp.int32, (LANES, LANES), 0)
-    to_lane = lax.broadcasted_iota(jnp.int32, (LANES, LANES), 1)
-    swap = jnp.abs(to_lane - from_lane) == SIDE
-    step = (jnp.abs(to_lane - from_lane) == 1) & ((to_lane < SIDE) == (from_lane < SIDE))
-    for start in (0, LANES):
-        near[start : start + LANES, :LANES] = one_where(step | swap)
-        near[start : start + LANES, LANES:] = one_where(swap)
 
     weights = sweep_weights(SWEEPS)
     diagonal = 6.0 + screen_mass
@@ -327,7 +342,8 @@
     own_copy = pltpu.make_async_copy(sums.at[pl.ds(PAD, BASE_X)], own_out, copies.at[0])
     own_copy.start()
 
-    for (step_x, step_y), out in zip(STEPS[1:], outs):
+    outgoing = []
+    for (step_x, step_y), out, target in zip(STEPS[1:], outs, targets_out):
         base, rows, leads = place_of(step_x, step_y)
 
         def narrow(lead, base=base, rows=rows, leads=leads, out=out):
@@ -343,12 +359,10 @@
                     out[k, :, lanes] = values[k].astype(out.dtype)
 
         for_leads(leads, narrow)
-
-    def clear_grid(lead):
-        start = pl.multiple_of(lead * GRID_ROWS, 8)
-        grid[pl.ds(start, GRID_ROWS), :] = jnp.zeros((GRID_ROWS, LANES), jnp.float32)
-
-    for_leads(GRID_ROWS, clear_grid)
+        copy = pltpu.make_async_copy(out, target, copies.at[11 + len(outgoing)])
+        copy.start()
+        outgoing.append(copy)
+
     slab = SIDE - 16
 
     def deposit(step_x, step_y, k, base, rows, leads):
@@ -365,19 +379,18 @@
         apart = lax.broadcasted_iota(jnp.int32, (LANES, LANES), 1) - from_lane - at_z
         low = one_where((from_lane < SIDE) & (apart == 0))
         high = one_where((from_lane >= SIDE) & (apart == -SIDE))
-        for half in (0, LANES):
-            place[half : half + LANES, :LANES] = low
-            place[half : half + LANES, LANES:] = high
+        place[:, :LANES] = low
+        place[:, LANES:] = high
         block = 16
         for first in range(0, leads, block):
             size = min(block, leads - first)
             value = window[pl.ds(pl.multiple_of(PAD + base + first * rows, 8), size * rows), :]
-            placed = jnp.dot(halves(value * value), place[...], preferred_element_type=jnp.float32)
+            placed = jnp.dot(value.astype(jnp.bfloat16), place[...], preferred_element_type=jnp.float32)
             for j in range(size):
                 for odd_column in (0, 1):
                     at = pl.ds(start + (2 * (first + j) + odd_column) * GRID_ROWS, rows)
                     part = placed[j * rows : (j + 1) * rows, odd_column * LANES : (odd_column + 1) * LANES]
-                    grid[at, :] = grid[at, :] + part
+                    grid[at, :] = grid[at, :] + part * part
 
     for k in range(2):
         deposit(0, 0, k, k * HALF * SIDE, SIDE, HALF)
@@ -408,8 +421,8 @@
     lax.fori_loop(0, 8, deposit_corner, 0)
     grid_copy = pltpu.make_async_copy(grid.at[pl.ds(GRID_PAD * GRID_ROWS, EDGE_ROWS)], grid_out, copies.at[1])
     grid_copy.start()
-    own_copy.wait()
-    grid_copy.wait()
+    for copy in [own_copy, *outgoing, grid_copy]:
+        copy.wait()
 
 
 GRID_PAD = 8
@@ -435,8 +448,8 @@
     return pl.pallas_call(
         functools.partial(pair_kernel, mesh_x, mesh_y),
         out_shape=term_shapes,
-        in_specs=[smem] * 3 + [vmem] * 9,
-        out_specs=[hbm] * 2 + [vmem] * 8,
+        in_specs=[smem] * 3 + [hbm] * 9,
+        out_specs=[hbm] * 10,
         scratch_shapes=[
             pltpu.VMEM((WINDOW_ROWS + 2 * PAD, LANES), jnp.float32),
             pltpu.VMEM((WINDOW_ROWS + 2 * PAD, LANES), jnp.float32),
@@ -452,10 +465,12 @@
             field(SIDE + 16),
             field(SIDE + 16),
             pltpu.VMEM((GRID_ROWS * GRID_ROWS, LANES), jnp.float32),
-            pltpu.VMEM((2 * LANES, 2 * LANES), jnp.bfloat16),
-            pltpu.SemaphoreType.DMA((2,)),
-        ],
-        compiler_params=pltpu.CompilerParams(vmem_limit_bytes=56 * 1024 * 1024),
+            pltpu.VMEM((LANES, 2 * LANES), jnp.bfloat16),
+            pltpu.SemaphoreType.DMA((19,)),
+        ]
+        + [pltpu.VMEM(piece.shape, jnp.bfloat16) for piece in pieces]
+        + [pltpu.VMEM(piece.shape, jnp.bfloat16) for piece in pieces[1:]],
+        compiler_params=pltpu.CompilerParams(vmem_limit_bytes=64 * 1024 * 1024),
         cost_estimate=pl.CostEstimate(flops=40_000_000, bytes_accessed=8_000_000, transcendentals=0),
         name="pair_terms",
     )(flat_anchors, flat_pairs, flat_count, *pieces)
@@ -484,9 +499,12 @@
     return left, right, below, above
 
 
-def gather_kernel(mesh_x, mesh_y, own, *refs):
+def gather_kernel(mesh_x, mesh_y, own, core_source, *refs):
     outs = refs[:8]
-    send_low, send_high, sent, landed = refs[8:]
+    narrow_outs = refs[8:11]
+    send_low, send_high, core, narrow_x, narrow_y, sent, landed, copies = refs[11:]
+    core_copy = pltpu.make_async_copy(core_source, core, copies.at[3])
+    core_copy.start()
     left, right, below, above = greet(mesh_x, mesh_y)
     started = []
 
@@ -516,6 +534,21 @@
     low = pl.ds(0, RIM * SIDE)
     send(own.at[:, :, high], 2, above)
     send(own.at[:, :, low], 3, below)
+    core_copy.wait()
+
+    def narrow(row):
+        narrow_x[row] = core[row].astype(jnp.bfloat16)
+        narrow_y[row] = jnp.concatenate([core[2 * row, :RIM], core[2 * row + 1, :RIM]], 0).astype(jnp.bfloat16)
+
+    for_leads(RIM, narrow)
+    narrow_copies = [
+        pltpu.make_async_copy(source, target, copies.at[index])
+        for index, (source, target) in enumerate(
+            zip((narrow_x, narrow_y, narrow_y.at[pl.ds(0, RIM // 2)]), narrow_outs)
+        )
+    ]
+    for copy in narrow_copies:
+        copy.start()
     from_left.wait_recv()
     send(outs[0].at[:, high], 4, above)
     send(outs[0].at[:, low], 5, below)
@@ -526,17 +559,29 @@
         copy.wait_send()
     for copy in started[2:]:
         copy.wait_recv()
-
-
-def return_kernel(mesh_x, mesh_y, *refs):
-    side_terms = refs[:2]
+    for copy in narrow_copies:
+        copy.wait()
+
+
+def return_kernel(mesh_x, mesh_y, anchors, *refs):
+    side_sources = refs[:2]
     column_terms = refs[2:4]
     corner_terms = refs[4:8]
-    density, core = refs[8:10]
-    outs = refs[10:14]
-    potential = refs[14]
-    landed_corners, send_left, send_right, narrow_x, narrow_y, core_x, core_y, core_xy, sent, landed = refs[15:]
-    left, right, below, above = greet(mesh_x, mesh_y, diagonal=True)
+    outs = refs[14:18]
+    applied_out, potential_out = refs[18:20]
+    landed_corners, send_left, send_right, left_terms, right_terms = refs[20:25]
+    loads = refs[25:31]
+    density, core, core_x, core_y, core_xy, own = loads
+    potential, applied, sent, landed, copies = refs[31:]
+    here_x = lax.axis_index("gx")
+    here_y = lax.axis_index("gy")
+    incoming = [
+        pltpu.make_async_copy(source, target, copies.at[index])
+        for index, (source, target) in enumerate(
+            zip(refs[8:14] + side_sources, loads + (left_terms, right_terms))
+        )
+    ]
+    left, right, below, above = greet(mesh_x, mesh_y)
 
     def send(source, target, slot, device):
         copy = pltpu.make_async_remote_copy(
@@ -558,22 +603,21 @@
         send(column_terms[0], outs[2], 4, below),
         send(column_terms[1], outs[3], 5, above),
     ]
+    for copy in incoming:
+        copy.start()
+    for copy in incoming:
+        copy.wait()
     slab = core.shape[0]
-
-    def narrow(row):
-        narrow_x[row] = core[row].astype(jnp.bfloat16)
-        narrow_y[row] = jnp.concatenate([core[2 * row, :RIM], core[2 * row + 1, :RIM]], 0).astype(jnp.bfloat16)
-
-    for_leads(RIM, narrow)
-    from_right = send(narrow_x, core_x, 8, left)
 
     def finish_at(row, column, core_part):
         at = pl.ds(column * GRID_ROWS + GRID_PAD + row, 8, stride=GRID_ROWS)
-        potential[at, :] = -xc_factor * cube_root(density[at, :] + core_part)
+        value = -xc_factor * cube_root(density[at, :] + core_part)
+        density[at, :] = value
+        return value
 
     def own_rows(row):
         for column in range(0, slab, 8):
-            finish_at(row, column, core[row, pl.ds(column, 8), :])
+            potential[row, pl.ds(column, 8), :] = finish_at(row, column, core[row, pl.ds(column, 8), :])
 
     def right_rows(row):
         beside = core_x[row].astype(jnp.float32)
@@ -590,13 +634,16 @@
     def corner_rows(pair):
         above_rows(pair, source=core_xy, beyond=slab)
 
+    for_leads(slab, own_rows)
+    potential_copy = pltpu.make_async_copy(potential, potential_out, copies.at[8])
+    potential_copy.start()
+    for_leads(RIM, right_rows)
     for copy in corners:
         copy.wait_recv()
 
-    for side, target in enumerate((send_left, send_right)):
-        terms = side_terms[side]
-
-        def merge(lead, terms=terms, target=target, corner=None, shift=0):
+    for side, (terms, target) in enumerate(((left_terms, send_left), (right_terms, send_right))):
+
+        def merge(lead, corner, shift, terms=terms, target=target):
             lanes = pl.ds(pl.multiple_of(lead * LANES, LANES), LANES)
             value = terms[:, lanes]
             if corner is not None:
@@ -611,65 +658,61 @@
         ):
 
             def part_step(index, first=first, corner=corner, merge=merge):
-                merge(index + first, corner=corner, shift=first)
+                merge(index + first, corner, first)
 
             for_leads(last - first, part_step)
-    others.append(send(send_left, outs[0], 6, left))
-    others.append(send(send_right, outs[1], 7, right))
-    from_above = send(narrow_y, core_y, 9, below)
-    from_corner = send(narrow_y.at[pl.ds(0, RIM // 2)], core_xy, 10, (left[0], below[1]))
-    for_leads(slab, own_rows)
-    from_right.wait()
-    for_leads(RIM, right_rows)
-    from_above.wait()
+        others.append(send(target, outs[side], 6 + side, (left, right)[side]))
     for_leads(slab // 2, above_rows)
-    from_corner.wait()
     for_leads(RIM // 2, corner_rows)
+
+    lane = lane_index(SIDE)
+    orbit = (here_x * mesh_y + here_y) * 2
+    for k in range(2):
+        at_x = jnp.clip(anchors[0, orbit + k] - here_x * slab, 0, GRID_PAD - 1)
+        at_y = jnp.clip(anchors[1, orbit + k] - here_y * slab, 0, GRID_PAD - 1)
+        at_z = anchors[2, orbit + k]
+        start = at_y * GRID_ROWS + at_x + GRID_PAD
+        turn_low = lax.rem(LANES - at_z, LANES)
+        turn_high = lax.rem(LANES + SIDE - at_z, LANES)
+
+        def sample(lead, k=k, start=start, turn_low=turn_low, turn_high=turn_high):
+            lanes = pl.ds(pl.multiple_of(lead * LANES, LANES), LANES)
+            low = density[pl.ds(start + 2 * lead * GRID_ROWS, SIDE), :]
+            high = density[pl.ds(start + (2 * lead + 1) * GRID_ROWS, SIDE), :]
+            sampled = jnp.where(lane < SIDE, pltpu.roll(low, turn_low, 1), pltpu.roll(high, turn_high, 1))
+            at = pl.ds(pl.multiple_of((k * HALF + lead) * SIDE, SIDE), SIDE)
+            applied[at, :] = sampled * own[k, :, lanes].astype(jnp.float32)
+
+        for_leads(HALF, sample)
+    applied_copy = pltpu.make_async_copy(applied, applied_out, copies.at[9])
+    applied_copy.start()
     for copy in corners:
         copy.wait_send()
     for copy in others:
         copy.wait()
-
-
-def action_kernel(mesh_x, mesh_y, anchors, own, own_terms, from_right, from_left, from_above, from_below, grid, action, potential):
-    here_x = lax.axis_index("gx")
-    here_y = lax.axis_index("gy")
-    slab = potential.shape[0]
-
-    def copy_rows(row):
-        for column in range(0, slab, 8):
-            at = pl.ds(column * GRID_ROWS + GRID_PAD + row, 8, stride=GRID_ROWS)
-            potential[row, pl.ds(column, 8), :] = grid[at, :]
-
-    for_leads(slab, copy_rows)
-    lane = lane_index(SIDE)
-    first = (here_x * mesh_y + here_y) * 2
-    starts, lows, highs = [], [], []
-    for k in range(2):
-        at_x = anchors[0, first + k] - here_x * slab
-        at_y = anchors[1, first + k] - here_y * slab
-        at_z = anchors[2, first + k]
-        starts.append(at_y * GRID_ROWS + at_x + GRID_PAD)
-        lows.append(lax.rem(LANES - at_z, LANES))
-        highs.append(lax.rem(LANES + SIDE - at_z, LANES))
+    applied_copy.wait()
+    potential_copy.wait()
+
+
+def action_kernel(applied, own_terms, from_right, from_left, from_above, from_below, potential_source, action, potential, copied):
+    copy = pltpu.make_async_copy(potential_source, potential, copied.at[0])
+    copy.start()
 
     def apply(lead, column=None, shift=0):
         lanes = pl.ds(pl.multiple_of(lead * LANES, LANES), LANES)
-        above_rows = from_right[:, lanes].astype(jnp.float32)
-        below_rows = from_left[:, lanes].astype(jnp.float32)
+        high_rows = from_right[:, lanes].astype(jnp.float32)
+        low_rows = from_left[:, lanes].astype(jnp.float32)
         for k in range(2):
-            low = grid[pl.ds(starts[k] + 2 * lead * GRID_ROWS, SIDE), :]
-            high = grid[pl.ds(starts[k] + (2 * lead + 1) * GRID_ROWS, SIDE), :]
-            sampled = jnp.where(lane < SIDE, pltpu.roll(low, lows[k], 1), pltpu.roll(high, highs[k], 1))
-            terms = own_terms[pl.ds(pl.multiple_of((k * HALF + lead) * SIDE, SIDE), SIDE), :]
+            at = pl.ds(pl.multiple_of((k * HALF + lead) * SIDE, SIDE), SIDE)
+            terms = own_terms[at, :]
             if column is not None:
                 part = pl.ds(pl.multiple_of((lead - shift) * LANES, LANES), LANES)
                 terms = terms + column[k, :, part].astype(jnp.float32)
             rows = slice(k * RIM, (k + 1) * RIM)
             terms = jnp.concatenate(
-                [terms[:RIM] + below_rows[rows], terms[RIM:LOW], terms[LOW:] + above_rows[rows]], 0
+                [terms[:RIM] + low_rows[rows], terms[RIM:LOW], terms[LOW:] + high_rows[rows]], 0
             )
-            action[k, :, lanes] = sampled * own[k, :, lanes].astype(jnp.float32) - exx_share * terms
+            action[k, :, lanes] = applied[at, :] - exx_share * terms
 
     for start, stop, column in ((0, RIM_LEADS, from_below), (RIM_LEADS, LOW_LEADS, None), (LOW_LEADS, HALF, from_above)):
 
@@ -677,6 +720,7 @@
             apply(index + start, column=column, shift=start)
 
         for_leads(stop - start, part_step)
+    copy.wait()
 
 
 def shape_of(dims, dtype=jnp.bfloat16):
@@ -695,54 +739,90 @@
     corner_shape = shape_of((2 * RIM, RIM * SIDE))
     around = [side_shape] * 2 + [column_shape] * 2 + [corner_shape] * 4
 
-    pieces = pl.pallas_call(
+    core_shape = core_density.shape
+    narrow_shapes = [
+        (RIM, core_shape[1], LANES),
+        (core_shape[0] // 2, 2 * RIM, LANES),
+        (RIM // 2, 2 * RIM, LANES),
+    ]
+    grant = 64 * 1024 * 1024
+
+    gathered = pl.pallas_call(
         functools.partial(gather_kernel, mesh_x, mesh_y),
-        out_shape=around,
-        in_specs=[vmem],
-        out_specs=[hbm] * 8,
+        out_shape=around + [shape_of(dims) for dims in narrow_shapes],
+        in_specs=[vmem, hbm],
+        out_specs=[hbm] * 11,
         scratch_shapes=[
             pltpu.VMEM(side_shape.shape, jnp.bfloat16),
             pltpu.VMEM(side_shape.shape, jnp.bfloat16),
+            pltpu.VMEM(core_shape, jnp.float32),
+            pltpu.VMEM(narrow_shapes[0], jnp.bfloat16),
+            pltpu.VMEM(narrow_shapes[1], jnp.bfloat16),
             pltpu.SemaphoreType.DMA((8,)),
             pltpu.SemaphoreType.DMA((8,)),
+            pltpu.SemaphoreType.DMA((4,)),
         ],
         compiler_params=pltpu.CompilerParams(
-            collective_id=0, has_side_effects=True, vmem_limit_bytes=56 * 1024 * 1024
+            collective_id=0, has_side_effects=True, vmem_limit_bytes=grant
         ),
         name="gather_rims",
-    )(own)
+    )(own, core_density)
+    pieces = gathered[:8]
+
+    back_x = [((i + 1) % mesh_x, i) for i in range(mesh_x)]
+    back_y = [((i + 1) % mesh_y, i) for i in range(mesh_y)]
+    back_xy = [
+        ((i + 1) % mesh_x * mesh_y + (j + 1) % mesh_y, i * mesh_y + j)
+        for i in range(mesh_x)
+        for j in range(mesh_y)
+    ]
+    core_rims = [
+        lax.ppermute(gathered[8], "gx", back_x),
+        lax.ppermute(gathered[9], "gy", back_y),
+        lax.ppermute(gathered[10], ("gx", "gy"), back_xy),
+    ]
 
     terms = pairs_call(mesh_x, mesh_y, flat_anchors, flat_pairs, flat_count, [own] + list(pieces))
-    returned = pl.pallas_call(
+    grid_shape = terms[1].shape
+    *returned, applied, potential = pl.pallas_call(
         functools.partial(return_kernel, mesh_x, mesh_y),
-        out_shape=[side_shape] * 2 + [column_shape] * 2 + [shape_of((EDGE_ROWS, LANES), jnp.float32)],
-        in_specs=[vmem] * 2 + [hbm] * 6 + [vmem] * 2,
-        out_specs=[hbm] * 4 + [vmem],
+        out_shape=[side_shape] * 2
+        + [column_shape] * 2
+        + [shape_of((BASE_X, LANES), jnp.float32), shape_of(core_shape, jnp.float32)],
+        in_specs=[smem] + [hbm] * 14,
+        out_specs=[hbm] * 6,
         scratch_shapes=[
             pltpu.VMEM((4,) + corner_shape.shape, jnp.bfloat16),
             pltpu.VMEM(side_shape.shape, jnp.bfloat16),
             pltpu.VMEM(side_shape.shape, jnp.bfloat16),
-            pltpu.VMEM((RIM, SIDE - 16, LANES), jnp.bfloat16),
-            pltpu.VMEM((RIM, 2 * RIM, LANES), jnp.bfloat16),
-            pltpu.VMEM((RIM, SIDE - 16, LANES), jnp.bfloat16),
-            pltpu.VMEM((RIM, 2 * RIM, LANES), jnp.bfloat16),
-            pltpu.VMEM((RIM // 2, 2 * RIM, LANES), jnp.bfloat16),
-            pltpu.SemaphoreType.DMA((11,)),
-            pltpu.SemaphoreType.DMA((11,)),
+            pltpu.VMEM(side_shape.shape, jnp.bfloat16),
+            pltpu.VMEM(side_shape.shape, jnp.bfloat16),
+            pltpu.VMEM(grid_shape, jnp.float32),
+            pltpu.VMEM(core_shape, jnp.float32),
+            pltpu.VMEM(narrow_shapes[0], jnp.bfloat16),
+            pltpu.VMEM(narrow_shapes[1], jnp.bfloat16),
+            pltpu.VMEM(narrow_shapes[2], jnp.bfloat16),
+            pltpu.VMEM(own.shape, jnp.bfloat16),
+            pltpu.VMEM(core_shape, jnp.float32),
+            pltpu.VMEM((BASE_X, LANES), jnp.float32),
+            pltpu.SemaphoreType.DMA((8,)),
+            pltpu.SemaphoreType.DMA((8,)),
+            pltpu.SemaphoreType.DMA((10,)),
         ],
         compiler_params=pltpu.CompilerParams(
-            collective_id=1, has_side_effects=True, vmem_limit_bytes=56 * 1024 * 1024
+            collective_id=1, has_side_effects=True, vmem_limit_bytes=grant
         ),
         name="return_terms",
-    )(*terms[2:], terms[1], core_density)
+    )(flat_anchors, *terms[2:], terms[1], core_density, *core_rims, own)
     action, potential = pl.pallas_call(
-        functools.partial(action_kernel, mesh_x, mesh_y),
-        out_shape=[shape_of(own.shape, jnp.float32), shape_of(core_density.shape, jnp.float32)],
-        in_specs=[smem] + [vmem] * 7,
-        out_specs=[vmem] * 2,
-        compiler_params=pltpu.CompilerParams(vmem_limit_bytes=56 * 1024 * 1024),
+        action_kernel,
+        out_shape=[shape_of(own.shape, jnp.float32), shape_of(core_shape, jnp.float32)],
+        in_specs=[vmem] * 6 + [hbm],
+        out_specs=[vmem, hbm],
+        scratch_shapes=[pltpu.SemaphoreType.DMA((1,))],
+        compiler_params=pltpu.CompilerParams(vmem_limit_bytes=grant),
         name="action_terms",
-    )(flat_anchors, own, terms[0], *returned)
+    )(applied, terms[0], *returned, potential)
     return (action.reshape(orbitals.shape), potential)
 
 

time: 113 us -> 130 us (1.15)
  the two profiles are of different devices: /device:TPU:5 before, /device:TPU:25 now
where the time goes in v5:
time: 130 us; the launch traced here: 129 us
  Pallas kernels  126 us (97%)
  starting transfers between devices  2.07 us (2%)
  between operations  1.33 us (1%)
    pallas_call x1, Pallas kernels, local(): pl.pallas_call(action_kernel, out_shape=[shape_of(own.shape, jnp.float32)...  40.8 us
    pallas_call x1, Pallas kernels, local(): pl.pallas_call(functools.partial(return_kernel, mesh_x, mesh_y), out_shap...  39.1 us
    pallas_call x1, Pallas kernels, local(): pl.pallas_call(functools.partial(gather_kernel, mesh_x, mesh_y), out_shap...  32.7 us
    pallas_call x1, Pallas kernels, pairs_call(): pl.pallas_call(functools.partial(pair_kernel, mesh_x, mesh_y), out_shape=...  13.4 us
  transfers between devices with their start and end apart: 3, of which 0 were waited for; matrix products, arithmetic and copies ran while one was open for 0% of the time, Pallas kernels for 10%

profile of v5, /device:TPU:25, one launch (start us, length us, event | category | flops | bytes accessed | tf_op | source)
XLA Modules:
  0.0 129.4 jit_solution(9959471298766402435)
XLA Ops:
  0.6 32.7 %gather_rims.1 = (bf16[48,4096]{1,0:T(8,128)(2,1)}, bf16[48,4096]{1,0:T(8,128)(2,1)}, bf16[2,64,1536]{2,1,0:T(8,128)(2,1)}, bf16[2,64,1536]{2,1,0:T(8,128)(2,1)}...) custom-call(bf16[2,64,4096]{2,1,0:T(8,128)(2,1)} %bitcast.8, ...), custom_call_target="tpu_custom_call" | custom-call | tf_op jit(solution)/shard_map/gather_rims/pallas_call | solution.py:750
  33.4 2.1 %collective-permute-start = (bf16[24,48,128]{2,1,0:T(8,128)(2,1)}, bf16[24,48,128]{2,1,0:T(8,128)(2,1)}, u32[]{:S(2)}, u32[]{:S(2)}) collective-permute-start(bf16[24,48,128]{2,1,0:T(8,128)(2,1)} %get-tuple-element.48), channel_id=1, source_target_pairs={{16,0},{32,16},{48,32},{64,48},{80,64},{96,80},{112,96},{0,112},{1... | collective-permute-start | bytes 884744 | tf_op jit(solution)/shard_map/ppermute | solution.py:780
  35.4 0.0 collective-permute-start.1
  35.4 0.0 collective-permute-start.2
  36.1 13.4 %pair_terms.1 = (f32[4096,128]{1,0:T(8,128)}, f32[6424,128]{1,0:T(8,128)}, bf16[48,4096]{1,0:T(8,128)(2,1)}, bf16[48,4096]{1,0:T(8,128)(2,1)}, bf16[2,64,1536]{2...) custom-call(s32[3,256]{1,0:T(4,128)} %bitcast.11, ...), custom_call_target="tpu_custom_call" | custom-call | flops 40000000 | bytes 8000000 | tf_op jit(solution)/shard_map/pair_terms/pallas_call | solution.py:448
  49.5 0.0 collective-permute-done.2.refs_12_
  49.5 0.0 collective-permute-done.refs_10_
  49.5 0.0 collective-permute-done.1.refs_11_
  49.5 39.1 %return_terms.1 = (bf16[48,4096]{1,0:T(8,128)(2,1)}, bf16[48,4096]{1,0:T(8,128)(2,1)}, bf16[2,64,1536]{2,1,0:T(8,128)(2,1)}, bf16[2,64,1536]{2,1,0:T(8,128)(2,1)...) custom-call(s32[3,256]{1,0:T(4,128)} %bitcast.12, bf16[48,4096]{1,0:T(8,128)(2,1)} %get-tuple-element.39.refs_0_, ...), custom_call_target="tpu_custom_call" | custom-call | tf_op jit(solution)/shard_map/return_terms/pallas_call | solution.py:787
  88.7 40.8 %action_terms.1 = (f32[2,64,4096]{2,1,0:T(8,128)}, f32[48,48,128]{2,1,0:T(8,128)}) custom-call(f32[4096,128]{1,0:T(8,128)} %get-tuple-element.51.applied, f32[4096,128]{1,0:T(8,128)} %get-tuple-element.52.own_terms, bf16[48,4096]{1,0:T(8,128)(2,1)} %get-tuple-element.53.from_right, bf16[48,4096]{1,0:T(8,128)(2,1)} %get-tuple-element.54.from_left, ...), custom_call_target="tpu_custom_call" | custom-call | tf_op jit(solution)/shard_map/action_terms/pallas_call | solution.py:817
Async XLA Ops:
  33.4 16.1 %collective-permute-start = (bf16[24,48,128]{2,1,0:T(8,128)(2,1)}, bf16[24,48,128]{2,1,0:T(8,128)(2,1)}, u32[]{:S(2)}, u32[]{:S(2)}) collective-permute-start(bf16[24,48,128]{2,1,0:T(8,128)(2,1)} %get-tuple-element.48), channel_id=1, source_target_pairs={{16,0},{32,16},{48,32},{64,48},{80,64},{96,80},{112,96},{0,112},{1... | collective-permute-start | bytes 884744 | tf_op jit(solution)/shard_map/ppermute | solution.py:780
  35.4 14.1 %collective-permute-start.1 = (bf16[24,48,128]{2,1,0:T(8,128)(2,1)}, bf16[24,48,128]{2,1,0:T(8,128)(2,1)}, u32[]{:S(2)}, u32[]{:S(2)}) collective-permute-start(bf16[24,48,128]{2,1,0:T(8,128)(2,1)} %get-tuple-element.49), channel_id=1, source_target_pairs={{1,0},{2,1},{3,2},{4,3},{5,4},{6,5},{7,6},{8,7},{9,8},{10,9},{11,1... | collective-permute-start | bytes 884744 | tf_op jit(solution)/shard_map/ppermute | solution.py:781
  35.4 14.0 %collective-permute-start.2 = (bf16[12,48,128]{2,1,0:T(8,128)(2,1)}, bf16[12,48,128]{2,1,0:T(8,128)(2,1)}, u32[]{:S(2)}, u32[]{:S(2)}) collective-permute-start(bf16[12,48,128]{2,1,0:T(8,128)(2,1)} %get-tuple-element.50), channel_id=1, source_target_pairs={{17,0},{18,1},{19,2},{20,3},{21,4},{22,5},{23,6},{24,7},{25,8},{26... | collective-permute-start | bytes 442376 | tf_op jit(solution)/shard_map/ppermute | solution.py:782

commit v6 on v5

--- a/solution.py
+++ b/solution.py
@@ -694,8 +694,8 @@
     potential_copy.wait()
 
 
-def action_kernel(applied, own_terms, from_right, from_left, from_above, from_below, potential_source, action, potential, copied):
-    copy = pltpu.make_async_copy(potential_source, potential, copied.at[0])
+def action_kernel(applied, own_terms, from_right, from_left, from_above, from_below, potential_source, action, potential, staged, copied):
+    copy = pltpu.make_async_copy(potential_source, staged, copied.at[0])
     copy.start()
 
     def apply(lead, column=None, shift=0):
@@ -714,6 +714,9 @@
             )
             action[k, :, lanes] = applied[at, :] - exx_share * terms
 
+    copy.wait()
+    copy = pltpu.make_async_copy(staged, potential, copied.at[1])
+    copy.start()
     for start, stop, column in ((0, RIM_LEADS, from_below), (RIM_LEADS, LOW_LEADS, None), (LOW_LEADS, HALF, from_above)):
 
         def part_step(index, start=start, column=column):
@@ -819,7 +822,7 @@
         out_shape=[shape_of(own.shape, jnp.float32), shape_of(core_shape, jnp.float32)],
         in_specs=[vmem] * 6 + [hbm],
         out_specs=[vmem, hbm],
-        scratch_shapes=[pltpu.SemaphoreType.DMA((1,))],
+        scratch_shapes=[pltpu.VMEM(core_shape, jnp.float32), pltpu.SemaphoreType.DMA((2,))],
         compiler_params=pltpu.CompilerParams(vmem_limit_bytes=grant),
         name="action_terms",
     )(applied, terms[0], *returned, potential)

time: 130 us -> 95.7 us (0.74)
  Pallas kernels: 126 us -> 92.1 us
    pallas_call x1, Pallas kernels: 40.8 us -> 6.23 us  [local(): pl.pallas_call(action_kernel, out_shape=[shape_of(own.shape, jnp.float32)...]
    pallas_call x1, Pallas kernels: 13.4 us -> 17.8 us  [pairs_call(): pl.pallas_call(functools.partial(pair_kernel, mesh_x, mesh_y), out_shape=...]
    pallas_call x1, Pallas kernels: 39.1 us -> 35.3 us  [local(): pl.pallas_call(functools.partial(return_kernel, mesh_x, mesh_y), out_shap...]
  transfers between devices with their start and end apart: 3 -> 3, of which waited for: 0 -> 0; matrix products, arithmetic and copies ran while one was open for 0% -> 0% of each run, Pallas kernels for 10% -> 19%
where the time goes in v6:
time: 95.7 us; the launch traced here: 95.5 us
  Pallas kernels  92.1 us (96%)
  starting transfers between devices  2.07 us (2%)
  between operations  1.33 us (1%)
    pallas_call x1, Pallas kernels, local(): pl.pallas_call(functools.partial(return_kernel, mesh_x, mesh_y), out_shap...  35.3 us
    pallas_call x1, Pallas kernels, local(): pl.pallas_call(functools.partial(gather_kernel, mesh_x, mesh_y), out_shap...  32.7 us
    pallas_call x1, Pallas kernels, pairs_call(): pl.pallas_call(functools.partial(pair_kernel, mesh_x, mesh_y), out_shape=...  17.8 us
    pallas_call x1, Pallas kernels, local(): pl.pallas_call(action_kernel, out_shape=[shape_of(own.shape, jnp.float32)...  6.23 us
    ppermute x1, starting transfers between devices, local(): lax.ppermute(gathered[8], 'gx', back_x)  2.07 us
  transfers between devices with their start and end apart: 3, of which 0 were waited for; matrix products, arithmetic and copies ran while one was open for 0% of the time, Pallas kernels for 19%

profile of v6, /device:TPU:25, one launch (start us, length us, event | category | flops | bytes accessed | tf_op | source)
XLA Modules:
  0.0 95.5 jit_solution(12104233288452009540)
XLA Ops:
  0.6 32.7 %gather_rims.1 = (bf16[48,4096]{1,0:T(8,128)(2,1)}, bf16[48,4096]{1,0:T(8,128)(2,1)}, bf16[2,64,1536]{2,1,0:T(8,128)(2,1)}, bf16[2,64,1536]{2,1,0:T(8,128)(2,1)}...) custom-call(bf16[2,64,4096]{2,1,0:T(8,128)(2,1)} %bitcast.8, ...), custom_call_target="tpu_custom_call" | custom-call | tf_op jit(solution)/shard_map/gather_rims/pallas_call | solution.py:753
  33.4 2.1 %collective-permute-start = (bf16[24,48,128]{2,1,0:T(8,128)(2,1)}, bf16[24,48,128]{2,1,0:T(8,128)(2,1)}, u32[]{:S(2)}, u32[]{:S(2)}) collective-permute-start(bf16[24,48,128]{2,1,0:T(8,128)(2,1)} %get-tuple-element.48), channel_id=1, source_target_pairs={{16,0},{32,16},{48,32},{64,48},{80,64},{96,80},{112,96},{0,112},{1... | collective-permute-start | bytes 884744 | tf_op jit(solution)/shard_map/ppermute | solution.py:783
  35.4 0.0 collective-permute-start.1
  35.4 0.0 collective-permute-start.2
  36.1 17.8 %pair_terms.1 = (f32[4096,128]{1,0:T(8,128)}, f32[6424,128]{1,0:T(8,128)}, bf16[48,4096]{1,0:T(8,128)(2,1)}, bf16[48,4096]{1,0:T(8,128)(2,1)}, bf16[2,64,1536]{2...) custom-call(s32[3,256]{1,0:T(4,128)} %bitcast.11, ...), custom_call_target="tpu_custom_call" | custom-call | flops 40000000 | bytes 8000000 | tf_op jit(solution)/shard_map/pair_terms/pallas_call | solution.py:448
  53.9 0.0 collective-permute-done.2.refs_12_
  53.9 0.0 collective-permute-done.refs_10_
  53.9 0.0 collective-permute-done.1.refs_11_
  53.9 35.3 %return_terms.1 = (bf16[48,4096]{1,0:T(8,128)(2,1)}, bf16[48,4096]{1,0:T(8,128)(2,1)}, bf16[2,64,1536]{2,1,0:T(8,128)(2,1)}, bf16[2,64,1536]{2,1,0:T(8,128)(2,1)...) custom-call(s32[3,256]{1,0:T(4,128)} %bitcast.12, bf16[48,4096]{1,0:T(8,128)(2,1)} %get-tuple-element.39.refs_0_, ...), custom_call_target="tpu_custom_call" | custom-call | tf_op jit(solution)/shard_map/return_terms/pallas_call | solution.py:790
  89.2 6.2 %action_terms.1 = (f32[2,64,4096]{2,1,0:T(8,128)}, f32[48,48,128]{2,1,0:T(8,128)}) custom-call(f32[4096,128]{1,0:T(8,128)} %get-tuple-element.51.applied, f32[4096,128]{1,0:T(8,128)} %get-tuple-element.52.own_terms, bf16[48,4096]{1,0:T(8,128)(2,1)} %get-tuple-element.53.from_right, bf16[48,4096]{1,0:T(8,128)(2,1)} %get-tuple-element.54.from_left, ...), custom_call_target="tpu_custom_call" | custom-call | tf_op jit(solution)/shard_map/action_terms/pallas_call | solution.py:820
Async XLA Ops:
  33.4 20.5 %collective-permute-start = (bf16[24,48,128]{2,1,0:T(8,128)(2,1)}, bf16[24,48,128]{2,1,0:T(8,128)(2,1)}, u32[]{:S(2)}, u32[]{:S(2)}) collective-permute-start(bf16[24,48,128]{2,1,0:T(8,128)(2,1)} %get-tuple-element.48), channel_id=1, source_target_pairs={{16,0},{32,16},{48,32},{64,48},{80,64},{96,80},{112,96},{0,112},{1... | collective-permute-start | bytes 884744 | tf_op jit(solution)/shard_map/ppermute | solution.py:783
  35.4 18.5 %collective-permute-start.1 = (bf16[24,48,128]{2,1,0:T(8,128)(2,1)}, bf16[24,48,128]{2,1,0:T(8,128)(2,1)}, u32[]{:S(2)}, u32[]{:S(2)}) collective-permute-start(bf16[24,48,128]{2,1,0:T(8,128)(2,1)} %get-tuple-element.49), channel_id=1, source_target_pairs={{1,0},{2,1},{3,2},{4,3},{5,4},{6,5},{7,6},{8,7},{9,8},{10,9},{11,1... | collective-permute-start | bytes 884744 | tf_op jit(solution)/shard_map/ppermute | solution.py:784
  35.4 18.4 %collective-permute-start.2 = (bf16[12,48,128]{2,1,0:T(8,128)(2,1)}, bf16[12,48,128]{2,1,0:T(8,128)(2,1)}, u32[]{:S(2)}, u32[]{:S(2)}) collective-permute-start(bf16[12,48,128]{2,1,0:T(8,128)(2,1)} %get-tuple-element.50), channel_id=1, source_target_pairs={{17,0},{18,1},{19,2},{20,3},{21,4},{22,5},{23,6},{24,7},{25,8},{26... | collective-permute-start | bytes 442376 | tf_op jit(solution)/shard_map/ppermute | solution.py:785
